TPU v7x, 32 devices: a whole 2x2x4 slice. The times are simulated.
32 devices in a mesh: groups: 2 (over y), expert: 8 (over z, core), hidden: 2 (over x), tok: 1.
Axes of the slice: x: 2, y: 2, z: 4, core: 2. Of those that a mesh axis runs over, the one named last changes fastest.
Arguments:
- out_grad: bfloat16 [2560, 1152], P(('groups', 'expert', 'tok')), parts along dimension 0, may hold values from -2.5 to 2.5
- expert_index: int32 [2560, 2], P(('groups', 'expert', 'tok')), parts along dimension 0, may hold values from 0 to 3, all different within a row; in each aligned block of 160 rows (0 to 159, 160 to 319, ...) at most 100 rows name the same one
- gate_values: float32 [2560, 2], P(('groups', 'expert', 'tok')), parts along dimension 0, may hold values from 0.2 to 1
- dispatched_inputs: bfloat16 [8, 800, 1152], P('expert', ('groups', 'tok')), parts along dimension 1, may hold values from -6 to 6
- w_gate: bfloat16 [8, 1152, 2304], P('expert', None, 'hidden'), may hold values from -0.1875 to 0.1875
- w_up: bfloat16 [8, 1152, 2304], P('expert', None, 'hidden'), may hold values from -0.1875 to 0.1875
- w_down: bfloat16 [8, 2304, 1152], P('expert', 'hidden'), may hold values from -0.09375 to 0.09375
Outputs:
- input_grad: bfloat16 [2560, 1152], P(('groups', 'expert', 'tok'), 'hidden'), parts along dimension 0
- gate_grad: bfloat16 [2560, 2], P(('groups', 'expert', 'tok')), parts along dimension 0
There are 2 independent parts, one for each index of `groups`. A program takes and returns all parts, laid end to end along the dimension named above; an argument that names none is the same for every part. Nothing has to cross between parts.
Inputs may be any that keep to these rules, and one draw needn't show every extreme that they name: `expert_index`: each row names two different experts. In each aligned block of 160 rows (the rows of one device) no expert is named by more than 100 rows, and in some block some expert is named by exactly 100 rows.
All inputs are finite; a program needn't handle non-finite values.
Results may differ from a plain program's by a relative error of at most 0.014.
Values may be sent and summed in bfloat16 or wider, within the bound.
No kernel may reach another device: no remote copies, remote signals or barrier semaphores. Data moves between devices by JAX's collectives and lax.ppermute only.
A program may use at most 64 MiB of HBM per device.

v0:
```python
import jax
import jax.numpy as jnp
from jax import lax
from jax.sharding import PartitionSpec as P


def swapped(block, axis, bit):
    count = lax.axis_size(axis)
    route = []
    for low in range(count):
        high = low | 1 << bit
        if high != low and high < count:
            route += [(low, high), (high, low)]
    return lax.ppermute(block, axis, route)


def expert_rows(inputs, cotangent, gate_mat, up_mat, down_mat):
    gate_pre = jnp.dot(inputs, gate_mat, preferred_element_type=jnp.float32)
    up_pre = jnp.dot(inputs, up_mat, preferred_element_type=jnp.float32)
    sigmoid_gate = jax.nn.sigmoid(gate_pre)
    hidden_act = gate_pre * sigmoid_gate * up_pre
    d_hidden = lax.dot_general(
        cotangent, down_mat, (((1,), (1,)), ((), ())), preferred_element_type=jnp.float32
    )
    gate_part = jnp.sum(hidden_act * d_hidden, axis=1)
    d_up = (d_hidden * gate_pre * sigmoid_gate).astype(jnp.bfloat16)
    d_gate = (d_hidden * up_pre * sigmoid_gate * (1.0 + gate_pre * (1.0 - sigmoid_gate))).astype(
        jnp.bfloat16
    )
    back_part = lax.dot_general(
        d_gate, gate_mat, (((1,), (1,)), ((), ())), preferred_element_type=jnp.float32
    )
    back_part = back_part + lax.dot_general(
        d_up, up_mat, (((1,), (1,)), ((), ())), preferred_element_type=jnp.float32
    )
    return (back_part, gate_part)


def local(out_grad, expert_index, gate_values, dispatched_inputs, w_gate, w_up, w_down):
    expert_count = lax.axis_size("expert")
    hidden_count = lax.axis_size("hidden")
    pair_pos = lax.axis_index("expert") % 2
    tok_rows = out_grad.shape[0]
    model_width = out_grad.shape[1]
    half_rows = dispatched_inputs.shape[1]
    slot_rows = 2 * half_rows
    capacity = slot_rows // expert_count
    expert_total = expert_count // 2
    feat_share = model_width // hidden_count
    feat_half = feat_share // 2
    own_rows = dispatched_inputs[0]
    other_rows = swapped(own_rows, "expert", 0)
    saved_rows = jnp.where(
        pair_pos == 0,
        jnp.concatenate([own_rows, other_rows], axis=0),
        jnp.concatenate([other_rows, own_rows], axis=0),
    )
    flat_expert = expert_index.reshape(-1)
    onehot = (flat_expert[:, None] == jnp.arange(expert_total, dtype=jnp.int32)[None, :]).astype(
        jnp.int32
    )
    before = jnp.cumsum(onehot, axis=0) - onehot
    slot_pos = jnp.sum(onehot * before, axis=1)
    target = flat_expert * capacity + slot_pos
    token_ids = jnp.arange(2 * tok_rows, dtype=jnp.int32) // 2
    source_row = jnp.full((expert_total * capacity,), tok_rows, jnp.int32).at[target].set(token_ids)
    padded = jnp.concatenate([out_grad, jnp.zeros((1, model_width), jnp.bfloat16)], axis=0)
    outgoing = jnp.repeat(
        padded[source_row].reshape(expert_total, capacity, model_width), 2, axis=0
    )
    routed = lax.all_to_all(outgoing, "expert", split_axis=0, concat_axis=0, tiled=True).reshape(
        slot_rows, model_width
    )
    gate_mat = w_gate[0]
    up_mat = w_up[0]
    down_mat = w_down[0]
    back_part, gate_part = expert_rows(saved_rows, routed, gate_mat, up_mat, down_mat)
    spread = jnp.broadcast_to(gate_part[:, None], (slot_rows, hidden_count))
    shares = (
        lax.psum_scatter(
            back_part.astype(jnp.bfloat16), "hidden", scatter_dimension=1, tiled=True
        ).astype(jnp.float32),
        lax.psum_scatter(
            spread.astype(jnp.bfloat16), "hidden", scatter_dimension=1, tiled=True
        ).astype(jnp.float32),
    )
    grad_share = shares[0]
    gate_sum = shares[1][:, 0]
    kept_half = lax.dynamic_slice_in_dim(grad_share, pair_pos * feat_half, feat_half, 1)
    given_half = lax.dynamic_slice_in_dim(grad_share, (1 - pair_pos) * feat_half, feat_half, 1)
    partner = (
        swapped(given_half.astype(jnp.bfloat16), "expert", 0).astype(given_half.dtype),
        swapped(gate_sum.astype(jnp.bfloat16), "expert", 0).astype(gate_sum.dtype),
    )
    grad_half = kept_half + partner[0]
    gate_total = gate_sum + partner[1]
    returned = (
        lax.all_to_all(
            grad_half.astype(jnp.bfloat16).reshape(expert_count, capacity, feat_half),
            "expert",
            split_axis=0,
            concat_axis=0,
            tiled=True,
        ),
        lax.all_to_all(
            gate_total.astype(jnp.bfloat16).reshape(expert_count, capacity),
            "expert",
            split_axis=0,
            concat_axis=0,
            tiled=True,
        ),
    )
    back_rows = returned[0].reshape(expert_total, 2, capacity, feat_half).transpose(0, 2, 1, 3)
    back_rows = back_rows.reshape(expert_total * capacity, feat_share)
    gate_rows = returned[1].reshape(expert_total, 2, capacity)[:, 0, :].reshape(-1)
    ret_rows = back_rows[target].astype(jnp.float32).reshape(tok_rows, 2, feat_share)
    input_grad = jnp.sum(gate_values[:, :, None] * ret_rows, axis=1).astype(jnp.bfloat16)
    gate_grad = gate_rows[target].reshape(tok_rows, 2)
    return (input_grad, gate_grad)


def solution(mesh):
    in_specs = (
        P(("groups", "expert", "tok"), None),
        P(("groups", "expert", "tok"), None),
        P(("groups", "expert", "tok"), None),
        P("expert", ("groups", "tok"), None),
        P("expert", None, "hidden"),
        P("expert", None, "hidden"),
        P("expert", "hidden", None),
    )
    out_specs = (P(("groups", "expert", "tok"), "hidden"), P(("groups", "expert", "tok"), None))
    return jax.shard_map(local, mesh=mesh, in_specs=in_specs, out_specs=out_specs, check_vma=False)
```

profile of v0, /device:TPU:0, one launch (start us, length us, event | category | flops | bytes accessed | tf_op | source)
XLA Modules:
  0.0 185.9 jit_solution(10313998124430692470)
XLA Ops:
  7.2 0.8 broadcast_multiply_fusion
  8.0 0.8 copy.31
  8.8 0.1 copy.30
  8.9 0.1 mul.63
  9.1 0.1 eq.27
  9.3 1.2 reduce-window.6
  10.5 0.2 slice_reduce_fusion
  10.7 0.2 reduce-window.9
  11.0 2.9 %scatter_custom_fusion = s32[400]{0:T(512)S(1)} fusion(s32[320]{0:T(512)S(1)} %fusion.16, s32[320]{0:T(512)S(1)} %add_select_fusion, s32[]{:T(128)} %constant.45.clone.1), kind=kCustom, calls=%fused_computation.50 | custom fusion | bytes 1604 | tf_op jit(solution)/shard_map/scatter | solution.py:66
  14.0 1.0 concatenate.9
  15.0 2.7 %gather_fusion = bf16[400,1152]{1,0:T(8,128)(2,1)} fusion(bf16[161,1152]{1,0:T(8,128)(2,1)S(1)} %concatenate.9, s32[1024]{0:T(1024)S(1)} %pad_clamp_fusion.1), kind=kCustom, calls=%fused_computation | custom fusion | bytes 1844800 | tf_op jit(solution)/shard_map/gather | solution.py:69
  17.7 2.3 %reshape.82 = bf16[4,100,1152]{2,1,0:T(8,128)(2,1)} reshape(bf16[400,1152]{1,0:T(8,128)(2,1)} %gather_fusion) | data formatting | bytes 1843200 | tf_op jit(solution)/shard_map/reshape | solution.py:69
  20.0 2.6 %broadcast_in_dim.10 = bf16[4,2,100,1152]{3,2,1,0:T(8,128)(2,1)} broadcast(bf16[4,100,1152]{2,1,0:T(8,128)(2,1)} %reshape.82), dimensions={0,2,3} | broadcast | bytes 2764800 | tf_op jit(solution)/shard_map/broadcast_in_dim | solution.py:68
  22.6 6.3 %all-to-all-start = ((bf16[8,100,1152]{2,1,0:T(8,128)(2,1)}), bf16[8,100,1152]{2,1,0:T(8,128)(2,1)}, u32[]{:S(2)}, u32[]{:S(2)}) async-start(bf16[8,100,1152]{2,1,0:T(8,128)(2,1)} %bitcast.39), calls=%async_computation | async-start | bytes 3833856 | tf_op jit(solution)/shard_map/all_to_all | solution.py:71
  29.0 0.5 collective-permute-start
  29.4 2.6 %collective-permute-done = bf16[400,1152]{1,0:T(8,128)(2,1)} collective-permute-done((bf16[400,1152]{1,0:T(8,128)(2,1)}, bf16[400,1152]{1,0:T(8,128)(2,1)}, u32[]{:S(2)}, u32[]{:S(2)}) %collective-permute-start) | collective-permute-done | bytes 921632 | tf_op jit(solution)/shard_map/ppermute | solution.py:14
  32.1 6.6 %fusion.3 = f32[800,1152]{1,0:T(8,128)} fusion(bf16[1,1152,1152]{2,1,0:T(8,128)(2,1)S(1)} %copy-done, bf16[400,1152]{1,0:T(8,128)(2,1)} %collective-permute-done, bf16[400,1152]{1,0:T(8,128)(2,1)} %bitcast.46, pred[]{:T(512)S(6)} %eq.34), kind=kOutput, calls=%fused_computation.12 | convolution fusion | flops 2131660800 | bytes 8183809 | tf_op jit(solution)/shard_map/dot_general | solution.py:18
  38.7 6.1 %fusion.6 = f32[800,1152]{1,0:T(8,128)} fusion(bf16[1,1152,1152]{2,1,0:T(8,128)(2,1)S(1)} %copy-done.3, bf16[400,1152]{1,0:T(8,128)(2,1)} %collective-permute-done, bf16[400,1152]{1,0:T(8,128)(2,1)S(1)} %bitcast.47, pred[]{:T(512)S(6)} %eq.34), kind=kOutput, calls=%fused_computation.15 | convolution fusion | flops 2131660800 | bytes 8183809 | tf_op jit(solution)/shard_map/dot_general | solution.py:19
  44.8 29.4 %all-to-all-done = bf16[8,100,1152]{2,1,0:T(8,128)(2,1)} async-done(((bf16[8,100,1152]{2,1,0:T(8,128)(2,1)}), bf16[8,100,1152]{2,1,0:T(8,128)(2,1)}, u32[]{:S(2)}, u32[]{:S(2)}) %all-to-all-start) | async-done | bytes 1843232 | tf_op jit(solution)/shard_map/all_to_all | solution.py:71
  74.2 2.6 %reshape.84 = bf16[800,1152]{1,0:T(8,128)(2,1)} reshape(bf16[8,100,1152]{2,1,0:T(8,128)(2,1)} %all-to-all-done) | data formatting | bytes 3686400 | tf_op jit(solution)/shard_map/reshape | solution.py:71
  76.9 7.6 %multiply_reduce_fusion = (bf16[800]{0:T(1024)(128)(2,1)S(1)}, f32[800,1152]{1,0:T(8,128)S(1)}) fusion(f32[800,1152]{1,0:T(8,128)} %fusion.6, f32[800,1152]{1,0:T(8,128)} %fusion.3, bf16[800,1152]{1,0:T(8,128)(2,1)} %reshape.84, bf16[1,1152,1152]{2,1,0:T(8,128)(2,1)} %param.13), kind=kOutput, calls=%fused_computation.5 | convolution fusion | flops 2129816832 | bytes 15558208 | tf_op jit(solution)/shard_map/dot_general | solution.py:22
  84.5 3.7 %fusion.1 = f32[800,1152]{1,0:T(8,128)S(1)} fusion(bf16[1,1152,1152]{2,1,0:T(8,128)(2,1)S(1)} %copy-done, f32[800,1152]{1,0:T(8,128)S(1)} %copy-done.7, f32[800,1152]{1,0:T(8,128)S(1)} %get-tuple-element.9, f32[800,1152]{1,0:T(8,128)S(1)} %copy-done.8), kind=kOutput, calls=%fused_computation.10 | convolution fusion | flops 2132582400 | bytes 17399808 | tf_op jit(solution)/shard_map/dot_general | solution.py:30
  88.3 4.1 %fusion = bf16[800,1152]{1,0:T(8,128)(2,1)} fusion(f32[800,1152]{1,0:T(8,128)S(1)} %fusion.1, bf16[1,1152,1152]{2,1,0:T(8,128)(2,1)S(1)} %copy-done.4, f32[800,1152]{1,0:T(8,128)S(1)} %get-tuple-element.9, f32[800,1152]{1,0:T(8,128)S(1)} %copy-done.7), kind=kOutput, calls=%fused_computation.9 | convolution fusion | flops 2130739200 | bytes 15556608 | tf_op jit(solution)/shard_map/dot_general | solution.py:33
  92.4 4.0 %copy.38 = bf16[800,1152]{0,1:T(8,128)(2,1)} copy(bf16[800,1152]{1,0:T(8,128)(2,1)} %fusion) | data formatting | bytes 3686400
  96.5 30.5 %reduce-scatter.4.cloned.1.call-done = bf16[576,800]{1,0:T(8,128)(2,1)} async-done(((bf16[1152,800]{1,0:T(8,128)(2,1)}), bf16[576,800]{1,0:T(8,128)(2,1)}) %reduce-scatter.4.cloned.1.call-update) | async-done | bytes 921616
  127.0 1.4 bitcast_convert_fusion
  128.4 1.3 copy-done.1
  129.7 0.9 dynamic-slice_convert_fusion
  130.5 0.6 dynamic-slice
  131.1 4.9 %all-reduce.2 = bf16[800,2]{0,1:T(2,128)(2,1)S(1)} all-reduce(bf16[800,2]{0,1:T(2,128)(2,1)S(1)} %broadcast_in_dim.11), channel_id=3, replica_groups=mesh['groups'=2,'expert'=8,'hidden'=2,'tok'=1] {'hidden'}, use_global_device_ids=true, to_apply=%region_7.8.clone | all-reduce | flops 1600 | bytes 6400
  136.0 0.7 dynamic-slice_reduce_fusion
  136.8 1.1 collective-permute-done.2
  137.9 0.7 all_to_all.16
  138.6 4.6 %all-to-all-start.2 = ((bf16[8,1,100]{2,1,0:T(2,128)(2,1)}), bf16[8,1,100]{2,1,0:T(2,128)(2,1)S(1)}, u32[]{:S(2)}, u32[]{:S(2)}) async-start(bf16[8,1,100]{2,1,0:T(2,128)(2,1)} %all_to_all.16), calls=%async_computation.2 | async-start | bytes 8192 | tf_op jit(solution)/shard_map/all_to_all | solution.py:105
  143.2 2.1 %add_convert_fusion = bf16[800,288]{0,1:T(8,128)(2,1)} fusion(bf16[800,288]{0,1:T(8,128)(2,1)S(1)} %collective-permute-done.1, f32[800,576]{0,1:T(8,128)} %copy-done.1, s32[]{:T(128)S(6)} %select_n.47), kind=kLoop, calls=%fused_computation.22 | loop fusion | flops 691200 | bytes 1843204 | tf_op jit(solution)/shard_map/convert_element_type | solution.py:99
  145.4 1.9 %reshape.85 = bf16[8,100,288]{1,0,2:T(8,128)(2,1)S(1)} reshape(bf16[800,288]{0,1:T(8,128)(2,1)} %add_convert_fusion) | data formatting | bytes 921600 | tf_op jit(solution)/shard_map/reshape | solution.py:99
  147.3 0.9 copy.34
  148.1 0.6 all-to-all-done.2
  148.7 4.5 %all-to-all-start.1 = ((bf16[8,100,288]{1,2,0:T(8,128)(2,1)}), bf16[8,100,288]{1,2,0:T(8,128)(2,1)S(1)}, u32[]{:S(2)}, u32[]{:S(2)}) async-start(bf16[8,100,288]{1,2,0:T(8,128)(2,1)} %copy.34), calls=%async_computation.1 | async-start | bytes 1179648 | tf_op jit(solution)/shard_map/all_to_all | solution.py:98
  153.5 2.5 %gather_fusion.2 = bf16[320]{0:T(512)(128)(2,1)S(1)} fusion(bf16[400]{0:T(512)(128)(2,1)S(1)} %reshape_squeeze.3, s32[1024]{0:T(1024)S(1)} %pad_clamp_fusion), kind=kCustom, calls=%fused_computation.2 | custom fusion | bytes 2560 | tf_op jit(solution)/shard_map/gather | solution.py:118
  156.0 0.2 reshape.89
  156.1 0.7 copy.37
  156.8 13.2 %all-to-all-done.1 = bf16[8,100,288]{1,2,0:T(8,128)(2,1)S(1)} async-done(((bf16[8,100,288]{1,2,0:T(8,128)(2,1)}), bf16[8,100,288]{1,2,0:T(8,128)(2,1)S(1)}, u32[]{:S(2)}, u32[]{:S(2)}) %all-to-all-start.1) | async-done | bytes 460832 | tf_op jit(solution)/shard_map/all_to_all | solution.py:98
  170.0 1.2 copy.35
  171.2 2.1 %reshape.87 = bf16[400,576]{1,0:T(8,128)(2,1)S(1)} reshape(bf16[4,100,2,288]{3,2,1,0:T(2,128)(2,1)} %bitcast.40) | data formatting | bytes 921600 | tf_op jit(solution)/shard_map/reshape | solution.py:114
  173.3 2.6 %gather_fusion.1 = bf16[320,576]{1,0:T(8,128)(2,1)} fusion(bf16[400,576]{1,0:T(8,128)(2,1)S(1)} %reshape.87, s32[1024]{0:T(1024)S(1)} %pad_clamp_fusion), kind=kCustom, calls=%fused_computation.1 | custom fusion | bytes 738560 | tf_op jit(solution)/shard_map/gather | solution.py:116
  175.9 1.4 reshape.91
  177.3 1.7 multiply_reduce_fusion.1
  (39 shorter events, 0.6 us)
Async XLA Ops:
  7.2 24.9 %copy-start = (bf16[1,1152,1152]{2,1,0:T(8,128)(2,1)S(1)}, bf16[1,1152,1152]{2,1,0:T(8,128)(2,1)}, u32[]{:S(2)}) copy-start(bf16[1,1152,1152]{2,1,0:T(8,128)(2,1)} %param.11) | copy-start | bytes 7962628
  22.6 51.6 %all-to-all-start = ((bf16[8,100,1152]{2,1,0:T(8,128)(2,1)}), bf16[8,100,1152]{2,1,0:T(8,128)(2,1)}, u32[]{:S(2)}, u32[]{:S(2)}) async-start(bf16[8,100,1152]{2,1,0:T(8,128)(2,1)} %bitcast.39), calls=%async_computation | async-start | bytes 3833856 | tf_op jit(solution)/shard_map/all_to_all | solution.py:71
  28.9 98.0 %reduce-scatter.4.cloned.1.call-start = ((), (), s32[]{:S(2)}) async-start(), calls=%async_computation.4 | async-start | bytes 3096576
  29.0 3.1 %collective-permute-start = (bf16[400,1152]{1,0:T(8,128)(2,1)}, bf16[400,1152]{1,0:T(8,128)(2,1)}, u32[]{:S(2)}, u32[]{:S(2)}) collective-permute-start(bf16[400,1152]{1,0:T(8,128)(2,1)} %bitcast.45), channel_id=1, source_target_pairs={{0,2},{2,0},{4,6},{6,4},{8,10},{10,8},{12,14},{14,12},{1,3},{3,1},... | collective-permute-start | bytes 2764808 | tf_op jit(solution)/shard_map/ppermute | solution.py:14
  29.4 9.2 %copy-start.3 = (bf16[1,1152,1152]{2,1,0:T(8,128)(2,1)S(1)}, bf16[1,1152,1152]{2,1,0:T(8,128)(2,1)}, u32[]{:S(2)}) copy-start(bf16[1,1152,1152]{2,1,0:T(8,128)(2,1)} %param.12) | copy-start | bytes 7962628
  29.4 9.2 %copy-start.5 = (bf16[1,400,1152]{2,1,0:T(8,128)(2,1)S(1)}, bf16[1,400,1152]{2,1,0:T(8,128)(2,1)}, u32[]{:S(2)}) copy-start(bf16[1,400,1152]{2,1,0:T(8,128)(2,1)} %param.10) | copy-start | bytes 2764804
  76.9 7.6 %copy-start.7 = (f32[800,1152]{1,0:T(8,128)S(1)}, f32[800,1152]{1,0:T(8,128)}, u32[]{:S(2)}) copy-start(f32[800,1152]{1,0:T(8,128)} %fusion.3) | copy-start | bytes 11059204
  76.9 7.6 %copy-start.8 = (f32[800,1152]{1,0:T(8,128)S(1)}, f32[800,1152]{1,0:T(8,128)}, u32[]{:S(2)}) copy-start(f32[800,1152]{1,0:T(8,128)} %fusion.6) | copy-start | bytes 11059204
  84.5 3.7 %copy-start.4 = (bf16[1,1152,1152]{2,1,0:T(8,128)(2,1)S(1)}, bf16[1,1152,1152]{2,1,0:T(8,128)(2,1)}, u32[]{:S(2)}) copy-start(bf16[1,1152,1152]{2,1,0:T(8,128)(2,1)} %param.12) | copy-start | bytes 7962628
  96.4 34.1 %copy-start.6 = (u32[32]{0:T(128)S(1)}, u32[32]{0:T(128)}, u32[]{:S(2)}) copy-start(u32[32]{0:T(128)} %constant.70) | copy-start | bytes 388
  128.3 1.3 copy-start.1
  129.7 23.6 %copy-start.2 = (f32[160,2]{0,1:T(2,128)S(1)}, f32[160,2]{0,1:T(2,128)}, u32[]{:S(2)}) copy-start(f32[160,2]{0,1:T(2,128)} %param.9) | copy-start | bytes 3844
  130.5 12.7 %collective-permute-start.1 = (bf16[800,288]{0,1:T(8,128)(2,1)}, bf16[800,288]{0,1:T(8,128)(2,1)S(1)}, u32[]{:S(2)}, u32[]{:S(2)}) collective-permute-start(bf16[800,288]{0,1:T(8,128)(2,1)} %dynamic-slice_convert_fusion), channel_id=1, source_target_pairs={{0,2},{2,0},{4,6},{6,4},{8,10},{10,8},{12,14},{14,12},{1,3},{3,1},... | collective-permute-start | bytes 1382408 | tf_op jit(solution)/shard_map/ppermute | solution.py:14
  136.7 1.2 collective-permute-start.2
  138.6 10.1 %all-to-all-start.2 = ((bf16[8,1,100]{2,1,0:T(2,128)(2,1)}), bf16[8,1,100]{2,1,0:T(2,128)(2,1)S(1)}, u32[]{:S(2)}, u32[]{:S(2)}) async-start(bf16[8,1,100]{2,1,0:T(2,128)(2,1)} %all_to_all.16), calls=%async_computation.2 | async-start | bytes 8192 | tf_op jit(solution)/shard_map/all_to_all | solution.py:105
  148.7 21.3 %all-to-all-start.1 = ((bf16[8,100,288]{1,2,0:T(8,128)(2,1)}), bf16[8,100,288]{1,2,0:T(8,128)(2,1)S(1)}, u32[]{:S(2)}, u32[]{:S(2)}) async-start(bf16[8,100,288]{1,2,0:T(8,128)(2,1)} %copy.34), calls=%async_computation.1 | async-start | bytes 1179648 | tf_op jit(solution)/shard_map/all_to_all | solution.py:98
Sparse Core Ops, SparseCore 0:
  96.6 30.3 reduce-scatter.3
where the time goes:
time: 187 us; the launch traced here: 186 us
  waiting for transfers between devices  77.5 us (41%)
  local copies, waits for them, and re-layouts  37.3 us (20%)
  matrix products  28.2 us (15%)
  starting transfers between devices  16 us (9%)
  between operations  14.3 us (8%)
  other arithmetic  7.62 us (4%)
  blocking collectives  4.92 us (3%)
    unnamed x2, waiting for transfers between devices  30.5 us
    all_to_all x1, waiting for transfers between devices, local(): lax.all_to_all(outgoing, 'expert', split_axis=0, concat_axis=0, tiled=True)  29.4 us
    all_to_all x1, waiting for transfers between devices, local(): lax.all_to_all(grad_half.astype(jnp.bfloat16).reshape(expert_count, capac...  13.2 us
    dot_general x1, matrix products, expert_rows(): lax.dot_general(cotangent, down_mat, (((1,), (1,)), ((), ())), preferred_...  7.63 us
    unnamed x25, local copies, waits for them, and re-layouts  7.55 us
    dot_general x1, matrix products, expert_rows(): gate_pre = jnp.dot(inputs, gate_mat, preferred_element_type=jnp.float32)  6.58 us
    all_to_all x1, starting transfers between devices, local(): lax.all_to_all(outgoing, 'expert', split_axis=0, concat_axis=0, tiled=True)  6.33 us
    dot_general x1, matrix products, expert_rows(): up_pre = jnp.dot(inputs, up_mat, preferred_element_type=jnp.float32)  6.14 us
  transfers between devices with their start and end apart: 7, of which 6 were waited for; matrix products, arithmetic and copies ran while one was open for 12% of the time, Pallas kernels for 0%

commit v1 on v0

v1 whole, which is shorter than its diff:
```python
import functools

import jax
import jax.numpy as jnp
from jax import lax
from jax.experimental import pallas as pl
from jax.experimental.pallas import tpu as pltpu
from jax.sharding import PartitionSpec as P

LANES = 128
NT = (((1,), (1,)), ((), ()))
TN = (((0,), (0,)), ((), ()))
VMEM_LIMIT = 40 << 20


def params():
    return pltpu.CompilerParams(vmem_limit_bytes=VMEM_LIMIT)


def whole():
    return pl.BlockSpec(memory_space=pltpu.VMEM)


def smem():
    return pl.BlockSpec(memory_space=pltpu.SMEM)


def dot(a, b, dims=(((1,), (0,)), ((), ()))):
    return lax.dot_general(a, b, dims, preferred_element_type=jnp.float32)


def relative(expert_index, peer, peers):
    shifted = expert_index - peer
    return jnp.where(shifted < 0, shifted + peers, shifted)


def named_by(rel, rows):
    lane = lax.broadcasted_iota(jnp.int32, (rows, LANES), 1)
    return (rel[:, 0:1] == lane) | (rel[:, 1:2] == lane)


def route_kernel(peers, padded, meta, index_ref, grad_ref, *outs):
    rows = grad_ref.shape[0]
    rel = relative(index_ref[...], meta[0], peers)
    named = named_by(rel, rows).astype(jnp.bfloat16)
    first = lax.broadcasted_iota(jnp.int32, (rows, rows), 0)
    second = lax.broadcasted_iota(jnp.int32, (rows, rows), 1)
    slots = dot(named, (first < second).astype(jnp.bfloat16), TN)
    present = dot(named, (first == second).astype(jnp.bfloat16), TN)
    place = lax.broadcasted_iota(jnp.int32, (padded, rows), 0)
    grad = grad_ref[...]
    for d, out in enumerate(outs):
        pick = (place == slots[d : d + 1, :].astype(jnp.int32)) & (present[d : d + 1, :] > 0.5)
        out[...] = dot(pick.astype(jnp.bfloat16), grad).astype(jnp.bfloat16)


def route(meta, expert_index, out_grad, peers, padded):
    rows, width = out_grad.shape
    return pl.pallas_call(
        functools.partial(route_kernel, peers, padded),
        out_shape=[jax.ShapeDtypeStruct((padded, width), jnp.bfloat16)] * peers,
        in_specs=[smem(), whole(), whole()],
        out_specs=[whole()] * peers,
        compiler_params=params(),
        cost_estimate=pl.CostEstimate(
            flops=2 * peers * padded * rows * width,
            bytes_accessed=2 * width * (rows + peers * padded),
            transcendentals=0,
        ),
        name="route",
    )(meta, expert_index, out_grad)


def forward_kernel(peers, cap, padded, order, meta, own_ref, other_ref, gate_ref, up_ref, act_ref, slope_ref, hid_ref, own32, other32, rows_ref):
    half_rows = own_ref.shape[0]

    @pl.when(pl.program_id(0) == 0)
    def _():
        for source, wide in ((own_ref, own32), (other_ref, other32)):
            wide[pl.ds(0, half_rows), :] = source[...].astype(jnp.float32)
            wide[pl.ds(half_rows, wide.shape[0] - half_rows), :] = jnp.zeros(
                (wide.shape[0] - half_rows, wide.shape[1]), jnp.float32
            )
        peer, pair = meta[0], meta[1]
        for wide, half in ((own32, pair), (other32, 1 - pair)):
            for k in range(peers):
                source = half * peers + k
                away = peer - lax.div(source, 2)
                away = jnp.where(away < 0, away + peers, away)
                swap = jnp.where(lax.rem(source, 2) == pair, 0, 1)
                position = 0
                for n, (d, core) in enumerate(order):
                    position += jnp.where((away == d) & (swap == core), n, 0)
                target = pl.ds(pl.multiple_of(position * padded, 16), padded)
                rows_ref[target, :] = wide[pl.ds(k * cap, padded), :].astype(jnp.bfloat16)

    rows = rows_ref[...]
    gate = dot(rows, gate_ref[0])
    up = dot(rows, up_ref[0])
    sig = jax.nn.sigmoid(gate)
    act = gate * sig
    act_ref[...] = act.astype(jnp.bfloat16)
    slope_ref[...] = (up * sig * (1.0 + gate * (1.0 - sig))).astype(jnp.bfloat16)
    hid_ref[...] = (act * up).astype(jnp.bfloat16)


def unit_block(units):
    for size in (384, 256, 128):
        if units % size == 0:
            return size
    return units


def forward(meta, own, other, w_gate, w_up, peers, cap, padded, order):
    half_rows, width = own.shape
    units = w_gate.shape[2]
    block = unit_block(units)
    rows = len(order) * padded
    deep = -(-(half_rows + padded) // 16) * 16
    column = pl.BlockSpec((rows, block), lambda j: (0, j))
    weight = pl.BlockSpec((1, width, block), lambda j: (0, 0, j))
    return pl.pallas_call(
        functools.partial(forward_kernel, peers, cap, padded, order),
        grid=(units // block,),
        out_shape=[jax.ShapeDtypeStruct((rows, units), jnp.bfloat16)] * 3,
        in_specs=[smem(), whole(), whole(), weight, weight],
        out_specs=[column] * 3,
        scratch_shapes=[
            pltpu.VMEM((deep, width), jnp.float32),
            pltpu.VMEM((deep, width), jnp.float32),
            pltpu.VMEM((rows, width), jnp.bfloat16),
        ],
        compiler_params=params(),
        cost_estimate=pl.CostEstimate(
            flops=4 * rows * width * units,
            bytes_accessed=2 * (2 * width * units + 3 * rows * units + rows * width),
            transcendentals=rows * units,
        ),
        name="forward",
    )(meta, own, other, w_gate, w_up)


def backward_kernel(count, cap, padded, meta, *refs):
    cots = refs[:count]
    act_ref, slope_ref, hid_ref, gate_ref, up_ref, down_ref = refs[count : count + 6]
    keep, give, cot_ref, sum_ref, part_ref = refs[count + 6 :]
    step = pl.program_id(0)

    @pl.when(step == 0)
    def _():
        for n, cot in enumerate(cots):
            cot_ref[pl.ds(n * padded, padded), :] = cot[...]

    d_hidden = dot(cot_ref[...], down_ref[0], NT)
    part = jnp.sum(d_hidden * hid_ref[...].astype(jnp.float32), axis=1, keepdims=True)
    d_gate = (d_hidden * slope_ref[...].astype(jnp.float32)).astype(jnp.bfloat16)
    d_up = (d_hidden * act_ref[...].astype(jnp.float32)).astype(jnp.bfloat16)
    back = dot(d_gate, gate_ref[0], NT) + dot(d_up, up_ref[0], NT)

    @pl.when(step == 0)
    def _():
        sum_ref[...] = back
        part_ref[...] = jnp.broadcast_to(part, part_ref.shape)

    @pl.when(step > 0)
    def _():
        sum_ref[...] += back
        part_ref[...] += jnp.broadcast_to(part, part_ref.shape)

    @pl.when(step == pl.num_programs(0) - 1)
    def _():
        shares, kept, share = give.shape
        row = lax.broadcasted_iota(jnp.int32, (padded, share), 0)
        lane = lax.broadcasted_iota(jnp.int32, (padded, LANES), 1)
        diagonal = lax.broadcasted_iota(jnp.int32, (padded, LANES), 0) == lane
        for n in range(count):
            rows = pl.ds(n * padded, padded)
            total = sum_ref[rows, :]
            line = jnp.sum(jnp.where(diagonal, part_ref[rows, :], 0.0), axis=0, keepdims=True)
            line = jnp.concatenate([line, jnp.zeros((1, share - LANES), jnp.float32)], axis=1)
            pieces = [total[:, i * share : (i + 1) * share] for i in range(shares)]
            for r in range(shares):
                piece = pieces[r]
                for i in range(shares):
                    piece = jnp.where(meta[2] == (i - r) % shares, pieces[i], piece)
                piece = jnp.where(row < cap, piece, jnp.where(row == cap, line, 0.0))
                if n < count // 2:
                    keep[r, rows, :] = piece
                else:
                    give[r, pl.ds(n * padded - kept, padded), :] = piece.astype(jnp.bfloat16)


def backward(meta, cots, first, tables, w_gate, w_up, w_down, cap, padded, shares):
    count = len(cots)
    width = cots[0].shape[1]
    units = w_gate.shape[2]
    block = unit_block(units)
    rows = count * padded
    kept = rows // 2
    share = width // shares
    table = pl.BlockSpec((rows, block), lambda j: (first, j))
    weight = pl.BlockSpec((1, width, block), lambda j: (0, 0, j))
    return pl.pallas_call(
        functools.partial(backward_kernel, count, cap, padded),
        grid=(units // block,),
        out_shape=[
            jax.ShapeDtypeStruct((shares, kept, share), jnp.float32),
            jax.ShapeDtypeStruct((shares, kept, share), jnp.bfloat16),
        ],
        in_specs=[smem()]
        + [whole()] * count
        + [table] * 3
        + [weight, weight, pl.BlockSpec((1, block, width), lambda j: (0, j, 0))],
        out_specs=[whole()] * 2,
        scratch_shapes=[
            pltpu.VMEM((rows, width), jnp.bfloat16),
            pltpu.VMEM((rows, width), jnp.float32),
            pltpu.VMEM((rows, LANES), jnp.float32),
        ],
        compiler_params=params(),
        cost_estimate=pl.CostEstimate(
            flops=6 * rows * width * units,
            bytes_accessed=2 * (3 * width * units + 3 * rows * units + 4 * rows * width),
            transcendentals=0,
        ),
        name="backward",
    )(meta, *cots, *tables, w_gate, w_up, w_down)


def combine_kernel(peers, cap, meta, index_ref, gates_ref, *refs):
    blocks = refs[:peers]
    grad_ref, gate_out = refs[peers:]
    rows = index_ref.shape[0]
    padded = blocks[0].shape[0]
    rel = relative(index_ref[...], meta[0], peers)
    gates = gates_ref[...]
    named = named_by(rel, rows)
    first = lax.broadcasted_iota(jnp.int32, (rows, rows), 0)
    second = lax.broadcasted_iota(jnp.int32, (rows, rows), 1)
    slots = dot((second < first).astype(jnp.bfloat16), named.astype(jnp.bfloat16)).astype(jnp.int32)
    place = lax.broadcasted_iota(jnp.int32, (rows, padded), 1)
    total = jnp.zeros(grad_ref.shape, jnp.float32)
    products = jnp.zeros((rows, 2), jnp.float32)
    for d, block in enumerate(blocks):
        chosen = rel == d
        weight = jnp.sum(jnp.where(chosen, gates, 0.0), axis=1, keepdims=True)
        hit = jnp.max(chosen.astype(jnp.int32), axis=1, keepdims=True) > 0
        pick = (place == slots[:, d : d + 1]) & hit
        values = block[...]
        total += weight * dot(pick.astype(jnp.bfloat16), values)
        line = values[cap : cap + 1, :padded].astype(jnp.float32)
        found = jnp.sum(jnp.where(pick, line, 0.0), axis=1, keepdims=True)
        products += jnp.where(chosen, found, 0.0)
    grad_ref[...] = total.astype(jnp.bfloat16)
    gate_out[...] = products.astype(jnp.bfloat16)


def combine(meta, expert_index, gate_values, blocks, cap):
    rows = expert_index.shape[0]
    peers = len(blocks)
    padded, share = blocks[0].shape
    return pl.pallas_call(
        functools.partial(combine_kernel, peers, cap),
        out_shape=[
            jax.ShapeDtypeStruct((rows, share), jnp.bfloat16),
            jax.ShapeDtypeStruct((rows, 2), jnp.bfloat16),
        ],
        in_specs=[smem()] + [whole()] * (2 + peers),
        out_specs=[whole()] * 2,
        compiler_params=params(),
        cost_estimate=pl.CostEstimate(
            flops=2 * peers * padded * rows * share,
            bytes_accessed=2 * share * (rows + peers * padded),
            transcendentals=0,
        ),
        name="combine",
    )(meta, expert_index, gate_values, *blocks)


def swap_pair(block):
    count = lax.axis_size("expert")
    return lax.ppermute(block, "expert", [(i, i ^ 1) for i in range(count)])


def sum_hidden(pieces):
    count = lax.axis_size("hidden")
    total = pieces[0]
    for r in range(1, count):
        ring = [(i, (i + r) % count) for i in range(count)]
        total = total + lax.ppermute(pieces[r].astype(jnp.bfloat16), "hidden", ring).astype(jnp.float32)
    return total.astype(jnp.bfloat16)


def shifted(block, d):
    count = lax.axis_size("expert")
    return lax.ppermute(block, "expert", [(i, (i + 2 * d) % count) for i in range(count)])


def local(out_grad, expert_index, gate_values, dispatched_inputs, w_gate, w_up, w_down):
    peers = lax.axis_size("expert") // 2
    shares = lax.axis_size("hidden")
    index = lax.axis_index("expert")
    meta = jnp.stack([index // 2, index % 2, lax.axis_index("hidden")]).astype(jnp.int32)
    own_rows = dispatched_inputs[0]
    cap = own_rows.shape[0] // peers
    padded = (cap // 16 + 1) * 16
    other_rows = swap_pair(own_rows)
    sent = route(meta, expert_index, out_grad, peers, padded)

    far = sorted(range(1, peers), key=lambda d: -min(d, peers - d))
    arrived = {0: sent[0]}
    for d in far:
        arrived[d] = shifted(sent[d], d)
    ranked = [0] + far
    groups = [ranked[: peers // 2], ranked[peers // 2 :]]
    order = []
    for group in groups:
        order += [(d, 0) for d in group] + [(d, 1) for d in group]
    tables = forward(meta, own_rows, other_rows, w_gate, w_up, peers, cap, padded, tuple(order))

    returned = {}
    for n, group in enumerate(groups):
        cots = [arrived[d] for d in group] + [swap_pair(arrived[d]) for d in group]
        keep, give = backward(
            meta, cots, n, tables, w_gate, w_up, w_down, cap, padded, shares
        )
        got = swap_pair(give)
        total = sum_hidden([keep[r] + got[r].astype(jnp.float32) for r in range(shares)])
        for m, d in enumerate(group):
            block = total[m * padded : (m + 1) * padded]
            returned[d] = shifted(block, -d) if d else block
    blocks = [returned[d] for d in range(peers)]
    return tuple(combine(meta, expert_index, gate_values, blocks, cap))


def solution(mesh):
    in_specs = (
        P(("groups", "expert", "tok"), None),
        P(("groups", "expert", "tok"), None),
        P(("groups", "expert", "tok"), None),
        P("expert", ("groups", "tok"), None),
        P("expert", None, "hidden"),
        P("expert", None, "hidden"),
        P("expert", "hidden", None),
    )
    out_specs = (P(("groups", "expert", "tok"), "hidden"), P(("groups", "expert", "tok"), None))
    return jax.shard_map(local, mesh=mesh, in_specs=in_specs, out_specs=out_specs, check_vma=False)
```

time: 187 us -> 95.7 us (0.51)
  waiting for transfers between devices: 77.5 us -> 41.2 us
  Pallas kernels: 0 us -> 33.5 us
  local copies, waits for them, and re-layouts: 37.3 us -> 7.28 us
  matrix products: 28.2 us -> 0 us
  between operations: 14.3 us -> 0.8 us
  other arithmetic: 7.62 us -> 0.43 us
  blocking collectives: 4.92 us -> 0 us
  starting transfers between devices: 16 us -> 12.2 us
    all_to_all x3 -> x0, waiting for transfers between devices: 43.2 us -> none  [the longest x1 29.4 us: local(): lax.all_to_all(outgoing, 'expert', split_axis=0, concat_axis=0, tiled=True)]
    ppermute x3 -> x15, waiting for transfers between devices: 3.78 us -> 41.2 us  [the longest x6 31.2 us: shifted(): lax.ppermute(block, 'expert', [(i, (i + 2 * d) % count) for i in range(co...]
    pallas_call x0 -> x5, Pallas kernels: none -> 33.5 us  [the longest x2 20 us: backward(): pl.pallas_call(functools.partial(backward_kernel, count, cap, padded), gr...]
    unnamed x2 -> x0, waiting for transfers between devices: 30.5 us -> none
    dot_general x5 -> x0, matrix products: 28.2 us -> none  [the longest x1 7.63 us: expert_rows(): lax.dot_general(cotangent, down_mat, (((1,), (1,)), ((), ())), preferred_...]
    all_to_all x3 -> x0, starting transfers between devices: 15.4 us -> none  [the longest x1 6.33 us: local(): lax.all_to_all(outgoing, 'expert', split_axis=0, concat_axis=0, tiled=True)]
    ppermute x3 -> x15, starting transfers between devices: 0.54 us -> 12.2 us  [the longest x6 7.85 us: shifted(): lax.ppermute(block, 'expert', [(i, (i + 2 * d) % count) for i in range(co...]
    reshape x7 -> x0, local copies, waits for them, and re-layouts: 11.1 us -> none  [the longest x2 2.77 us: local(): grad_half.astype(jnp.bfloat16).reshape(expert_count, capacity, feat_half)]
  transfers between devices with their start and end apart: 7 -> 15, of which waited for: 6 -> 9; matrix products, arithmetic and copies ran while one was open for 12% -> 1% of each run, Pallas kernels for 0% -> 33%
where the time goes in v1:
time: 95.7 us; the launch traced here: 95.4 us
  waiting for transfers between devices  41.2 us (43%)
  Pallas kernels  33.5 us (35%)
  starting transfers between devices  12.2 us (13%)
  local copies, waits for them, and re-layouts  7.28 us (8%)
    ppermute x6, waiting for transfers between devices, shifted(): lax.ppermute(block, 'expert', [(i, (i + 2 * d) % count) for i in range(co...  31.2 us
    pallas_call x2, Pallas kernels, backward(): pl.pallas_call(functools.partial(backward_kernel, count, cap, padded), gr...  20 us
    pallas_call x1, Pallas kernels, forward(): pl.pallas_call(functools.partial(forward_kernel, peers, cap, padded, orde...  10 us
    ppermute x2, waiting for transfers between devices, sum_hidden(): lax.ppermute(pieces[r].astype(jnp.bfloat16), 'hidden', ring)  9.68 us
    ppermute x6, starting transfers between devices, shifted(): lax.ppermute(block, 'expert', [(i, (i + 2 * d) % count) for i in range(co...  7.85 us
    unnamed x16, local copies, waits for them, and re-layouts  6.57 us
    ppermute x2, starting transfers between devices, sum_hidden(): lax.ppermute(pieces[r].astype(jnp.bfloat16), 'hidden', ring)  3.11 us
    pallas_call x1, Pallas kernels, combine(): pl.pallas_call(functools.partial(combine_kernel, peers, cap), out_shape=[...  2.19 us
  transfers between devices with their start and end apart: 15, of which 9 were waited for; matrix products, arithmetic and copies ran while one was open for 1% of the time, Pallas kernels for 33%

profile of v1, /device:TPU:0, one launch (start us, length us, event | category | flops | bytes accessed | tf_op | source)
XLA Modules:
  0.0 95.4 jit_solution(6476330957090846813)
XLA Ops:
  0.6 0.5 collective-permute-start.3
  1.1 0.8 copy.10.index_ref
  2.0 0.1 pad_add_fusion.meta
  2.0 1.0 %copy-done.5 = bf16[160,1152]{1,0:T(8,128)(2,1)S(1)} copy-done((bf16[160,1152]{1,0:T(8,128)(2,1)S(1)}, bf16[160,1152]{1,0:T(8,128)(2,1)}, u32[]{:S(2)}) %copy-start.5) | copy-done | bytes 368664
  3.0 1.3 %route.1 = (bf16[112,1152]{1,0:T(8,128)(2,1)S(1)}, bf16[112,1152]{1,0:T(8,128)(2,1)S(1)}, bf16[112,1152]{1,0:T(8,128)(2,1)S(1)}, bf16[112,1152]{1,0:T(8,128)(2,1)S(1)}) custom-call(s32[3]{0:T(128)S(1)} %pad_add_fusion.meta, s32[160,2]{1,0:T(8,128)S(1)} %copy.10.index_ref, bf16[160,1152]{1,0:T(8,128)(2,1)S(1)} %copy-done.5), custom_call_target="tpu_custom_call" | custom-call | flops 165150720 | bytes 1400832 | tf_op jit(solution)/shard_map/route/pallas_call | solution.py:59
  4.3 2.7 %collective-permute-start.6 = (bf16[112,1152]{1,0:T(8,128)(2,1)S(1)}, bf16[112,1152]{1,0:T(8,128)(2,1)S(1)}, u32[]{:S(2)}, u32[]{:S(2)}) collective-permute-start(bf16[112,1152]{1,0:T(8,128)(2,1)S(1)} %get-tuple-element.20), channel_id=1, source_target_pairs={{0,4},{2,6},{4,8},{6,10},{8,12},{10,14},{12,0},{14,2},{1,5},{3,7},... | collective-permute-start | bytes 774152 | tf_op jit(solution)/shard_map/ppermute | solution.py:296
  7.0 2.1 %collective-permute-start.7 = (bf16[112,1152]{1,0:T(8,128)(2,1)S(1)}, bf16[112,1152]{1,0:T(8,128)(2,1)S(1)}, u32[]{:S(2)}, u32[]{:S(2)}) collective-permute-start(bf16[112,1152]{1,0:T(8,128)(2,1)S(1)} %get-tuple-element.21), channel_id=1, source_target_pairs={{0,12},{2,14},{4,0},{6,2},{8,4},{10,6},{12,8},{14,10},{1,13},{3,15... | collective-permute-start | bytes 774152 | tf_op jit(solution)/shard_map/ppermute | solution.py:296
  9.1 0.9 collective-permute-start
  10.0 0.0 collective-permute-start.1
  10.0 6.1 %collective-permute-done.6.refs_0_ = bf16[112,1152]{1,0:T(8,128)(2,1)S(1)} collective-permute-done((bf16[112,1152]{1,0:T(8,128)(2,1)S(1)}, bf16[112,1152]{1,0:T(8,128)(2,1)S(1)}, u32[]{:S(2)}, u32[]{:S(2)}) %collective-permute-start.6) | collective-permute-done | bytes 258080 | tf_op jit(solution)/shard_map/ppermute | solution.py:296
  16.1 0.0 collective-permute-start.8
  16.1 4.7 %collective-permute-done.7.refs_1_ = bf16[112,1152]{1,0:T(8,128)(2,1)S(1)} collective-permute-done((bf16[112,1152]{1,0:T(8,128)(2,1)S(1)}, bf16[112,1152]{1,0:T(8,128)(2,1)S(1)}, u32[]{:S(2)}, u32[]{:S(2)}) %collective-permute-start.7) | collective-permute-done | bytes 258080 | tf_op jit(solution)/shard_map/ppermute | solution.py:296
  20.8 0.0 collective-permute-start.9
  20.8 11.6 %collective-permute-done.refs_1_ = bf16[112,1152]{1,0:T(8,128)(2,1)S(1)} collective-permute-done((bf16[112,1152]{1,0:T(8,128)(2,1)S(1)}, bf16[112,1152]{1,0:T(8,128)(2,1)S(1)}, u32[]{:S(2)}, u32[]{:S(2)}) %collective-permute-start) | collective-permute-done | bytes 258080 | tf_op jit(solution)/shard_map/ppermute | solution.py:296
  32.5 0.0 collective-permute-start.2
  32.5 0.0 collective-permute-done.3.other_ref
  32.5 1.7 %copy-done = bf16[1,1152,1152]{2,1,0:T(8,128)(2,1)S(1)} copy-done((bf16[1,1152,1152]{2,1,0:T(8,128)(2,1)S(1)}, bf16[1,1152,1152]{2,1,0:T(8,128)(2,1)}, u32[]{:S(2)}) %copy-start) | copy-done | bytes 2654232
  34.3 1.7 %copy-done.2 = bf16[1,1152,1152]{2,1,0:T(8,128)(2,1)S(1)} copy-done((bf16[1,1152,1152]{2,1,0:T(8,128)(2,1)S(1)}, bf16[1,1152,1152]{2,1,0:T(8,128)(2,1)}, u32[]{:S(2)}) %copy-start.2) | copy-done | bytes 2654232
  36.0 1.2 %copy-done.4 = bf16[1,400,1152]{2,1,0:T(8,128)(2,1)S(1)} copy-done((bf16[1,400,1152]{2,1,0:T(8,128)(2,1)S(1)}, bf16[1,400,1152]{2,1,0:T(8,128)(2,1)}, u32[]{:S(2)}) %copy-start.4) | copy-done | bytes 921624
  37.2 10.0 %forward.1 = (bf16[896,1152]{1,0:T(8,128)(2,1)S(1)}, bf16[896,1152]{1,0:T(8,128)(2,1)S(1)}, bf16[896,1152]{1,0:T(8,128)(2,1)S(1)}) custom-call(s32[3]{0:T(128)S(1)} %pad_add_fusion.meta, bf16[400,1152]{1,0:T(8,128)(2,1)S(1)} %bitcast.17, bf16[400,1152]{1,0:T(8,128)(2,1)S(1)} %collective-permute-done.3.other_ref, bf16[1,1152,1152]{2,1,0:T(8,128)(2,1)S(1)} %copy-done, ...), custom_call_target="tpu_custom_call" | custom-call | flops 4756340736 | bytes 13565952 | tf_op jit(solution)/shard_map/forward/pallas_call | solution.py:122
  47.2 0.0 collective-permute-done.8.refs_2_
  47.2 0.0 collective-permute-done.9.refs_3_
  47.3 10.0 %backward.3 = (f32[2,224,576]{2,1,0:T(8,128)S(1)}, bf16[2,224,576]{2,1,0:T(8,128)(2,1)S(1)}) custom-call(s32[3]{0:T(128)S(1)} %pad_add_fusion.meta, bf16[112,1152]{1,0:T(8,128)(2,1)S(1)} %collective-permute-done.6.refs_0_, bf16[112,1152]{1,0:T(8,128)(2,1)S(1)} %collective-permute-done.7.refs_1_, bf16[112,1152]{1,0:T(8,128)(2,1)S(1)} %collective-permute-done.8.refs_2_, ...), custom_call_target="tpu_custom_call" | custom-call | flops 3567255552 | bytes 15187968 | tf_op jit(solution)/shard_map/backward/pallas_call | solution.py:203
  57.3 0.5 collective-permute-start.10
  57.8 0.0 collective-permute-done.1.refs_2_
  57.8 0.0 collective-permute-done.2.refs_3_
  57.8 10.0 %backward.2 = (f32[2,224,576]{2,1,0:T(8,128)S(1)}, bf16[2,224,576]{2,1,0:T(8,128)(2,1)S(1)}) custom-call(s32[3]{0:T(128)S(1)} %pad_add_fusion.meta, bf16[112,1152]{1,0:T(8,128)(2,1)S(1)} %get-tuple-element.13.refs_0_, bf16[112,1152]{1,0:T(8,128)(2,1)S(1)} %collective-permute-done.refs_1_, bf16[112,1152]{1,0:T(8,128)(2,1)S(1)} %collective-permute-done.1.refs_2_, ...), custom_call_target="tpu_custom_call" | custom-call | flops 3567255552 | bytes 15187968 | tf_op jit(solution)/shard_map/backward/pallas_call | solution.py:203
  67.8 0.1 collective-permute-start.4
  67.9 0.0 collective-permute-done.10
  67.9 0.1 fusion.3
  68.0 1.6 %collective-permute-start.11 = (bf16[224,576]{1,0:T(8,128)(2,1)S(1)}, bf16[224,576]{1,0:T(8,128)(2,1)S(1)}, u32[]{:S(2)}, u32[]{:S(2)}) collective-permute-start(bf16[224,576]{1,0:T(8,128)(2,1)S(1)} %fusion.3), channel_id=1, source_target_pairs={{0,1},{1,0},{2,3},{3,2},{4,5},{5,4},{6,7},{7,6},{8,9},{9,8},{10,11... | collective-permute-start | bytes 774152 | tf_op jit(solution)/shard_map/ppermute | solution.py:290
  69.5 0.3 collective-permute-done.4
  69.9 0.1 fusion.2
  69.9 0.0 copy-start.6
  69.9 1.6 %collective-permute-start.5 = (bf16[224,576]{1,0:T(8,128)(2,1)S(1)}, bf16[224,576]{1,0:T(8,128)(2,1)S(1)}, u32[]{:S(2)}, u32[]{:S(2)}) collective-permute-start(bf16[224,576]{1,0:T(8,128)(2,1)S(1)} %fusion.2), channel_id=1, source_target_pairs={{0,1},{1,0},{2,3},{3,2},{4,5},{5,4},{6,7},{7,6},{8,9},{9,8},{10,11... | collective-permute-start | bytes 774152 | tf_op jit(solution)/shard_map/ppermute | solution.py:290
  71.5 6.2 %collective-permute-done.11 = bf16[224,576]{1,0:T(8,128)(2,1)S(1)} collective-permute-done((bf16[224,576]{1,0:T(8,128)(2,1)S(1)}, bf16[224,576]{1,0:T(8,128)(2,1)S(1)}, u32[]{:S(2)}, u32[]{:S(2)}) %collective-permute-start.11) | collective-permute-done | bytes 258080 | tf_op jit(solution)/shard_map/ppermute | solution.py:290
  77.7 0.1 fusion
  77.8 1.7 %collective-permute-start.12 = (bf16[112,576]{1,0:T(8,128)(2,1)S(1)}, bf16[112,576]{1,0:T(8,128)(2,1)S(1)}, u32[]{:S(2)}, u32[]{:S(2)}) collective-permute-start(bf16[112,576]{1,0:T(8,128)(2,1)S(1)} %get-tuple-element.27), channel_id=1, source_target_pairs={{0,12},{2,14},{4,0},{6,2},{8,4},{10,6},{12,8},{14,10},{1,13},{3,15... | collective-permute-start | bytes 387080 | tf_op jit(solution)/shard_map/ppermute | solution.py:296
  79.5 0.4 collective-permute-start.14
  79.9 3.5 %collective-permute-done.5 = bf16[224,576]{1,0:T(8,128)(2,1)S(1)} collective-permute-done((bf16[224,576]{1,0:T(8,128)(2,1)S(1)}, bf16[224,576]{1,0:T(8,128)(2,1)S(1)}, u32[]{:S(2)}, u32[]{:S(2)}) %collective-permute-start.5) | collective-permute-done | bytes 258080 | tf_op jit(solution)/shard_map/ppermute | solution.py:290
  83.4 0.1 fusion.1
  83.6 0.1 collective-permute-start.13
  83.6 0.1 copy.11.gates_ref
  83.8 0.8 collective-permute-done.12.refs_1_
  84.5 2.5 %collective-permute-done.14.refs_3_ = bf16[112,576]{1,0:T(8,128)(2,1)S(1)} collective-permute-done((bf16[112,576]{1,0:T(8,128)(2,1)S(1)}, bf16[112,576]{1,0:T(8,128)(2,1)S(1)}, u32[]{:S(2)}, u32[]{:S(2)}) %collective-permute-start.14) | collective-permute-done | bytes 129056 | tf_op jit(solution)/shard_map/ppermute | solution.py:296
  87.1 5.5 %collective-permute-done.13.refs_2_ = bf16[112,576]{1,0:T(8,128)(2,1)S(1)} collective-permute-done((bf16[112,576]{1,0:T(8,128)(2,1)S(1)}, bf16[112,576]{1,0:T(8,128)(2,1)S(1)}, u32[]{:S(2)}, u32[]{:S(2)}) %collective-permute-start.13) | collective-permute-done | bytes 129056 | tf_op jit(solution)/shard_map/ppermute | solution.py:296
  92.5 2.2 %combine.1 = (bf16[160,576]{1,0:T(8,128)(2,1)}, bf16[160,2]{1,0:T(8,128)(2,1)S(1)}) custom-call(s32[3]{0:T(128)S(1)} %pad_add_fusion.meta, s32[160,2]{1,0:T(8,128)S(1)} %copy.10.index_ref, f32[160,2]{1,0:T(8,128)S(1)} %copy.11.gates_ref, bf16[112,576]{1,0:T(8,128)(2,1)S(1)} %get-tuple-element.29.refs_0_, ...), custom_call_target="tpu_custom_call" | custom-call | flops 82575360 | bytes 700416 | tf_op jit(solution)/shard_map/combine/pallas_call | solution.py:262
  94.7 0.7 copy.12
  (11 shorter events, 0.1 us)
Async XLA Ops:
  0.6 31.9 %collective-permute-start.3 = (bf16[400,1152]{1,0:T(8,128)(2,1)}, bf16[400,1152]{1,0:T(8,128)(2,1)S(1)}, u32[]{:S(2)}, u32[]{:S(2)}) collective-permute-start(bf16[400,1152]{1,0:T(8,128)(2,1)} %bitcast.16), channel_id=1, source_target_pairs={{0,2},{2,0},{4,6},{6,4},{8,10},{10,8},{12,14},{14,12},{1,3},{3,1},... | collective-permute-start | bytes 2764808 | tf_op jit(solution)/shard_map/ppermute | solution.py:282
  2.0 1.0 %copy-start.5 = (bf16[160,1152]{1,0:T(8,128)(2,1)S(1)}, bf16[160,1152]{1,0:T(8,128)(2,1)}, u32[]{:S(2)}) copy-start(bf16[160,1152]{1,0:T(8,128)(2,1)} %grad_ref.1) | copy-start | bytes 1105924
  4.3 11.8 %collective-permute-start.6 = (bf16[112,1152]{1,0:T(8,128)(2,1)S(1)}, bf16[112,1152]{1,0:T(8,128)(2,1)S(1)}, u32[]{:S(2)}, u32[]{:S(2)}) collective-permute-start(bf16[112,1152]{1,0:T(8,128)(2,1)S(1)} %get-tuple-element.20), channel_id=1, source_target_pairs={{0,4},{2,6},{4,8},{6,10},{8,12},{10,14},{12,0},{14,2},{1,5},{3,7},... | collective-permute-start | bytes 774152 | tf_op jit(solution)/shard_map/ppermute | solution.py:296
  7.0 13.8 %collective-permute-start.7 = (bf16[112,1152]{1,0:T(8,128)(2,1)S(1)}, bf16[112,1152]{1,0:T(8,128)(2,1)S(1)}, u32[]{:S(2)}, u32[]{:S(2)}) collective-permute-start(bf16[112,1152]{1,0:T(8,128)(2,1)S(1)} %get-tuple-element.21), channel_id=1, source_target_pairs={{0,12},{2,14},{4,0},{6,2},{8,4},{10,6},{12,8},{14,10},{1,13},{3,15... | collective-permute-start | bytes 774152 | tf_op jit(solution)/shard_map/ppermute | solution.py:296
  9.1 23.4 %collective-permute-start = (bf16[112,1152]{1,0:T(8,128)(2,1)S(1)}, bf16[112,1152]{1,0:T(8,128)(2,1)S(1)}, u32[]{:S(2)}, u32[]{:S(2)}) collective-permute-start(bf16[112,1152]{1,0:T(8,128)(2,1)S(1)} %get-tuple-element.14), channel_id=1, source_target_pairs={{0,8},{2,10},{4,12},{6,14},{8,0},{10,2},{12,4},{14,6},{1,9},{3,11}... | collective-permute-start | bytes 774152 | tf_op jit(solution)/shard_map/ppermute | solution.py:296
  10.0 47.8 %collective-permute-start.1 = (bf16[112,1152]{1,0:T(8,128)(2,1)S(1)}, bf16[112,1152]{1,0:T(8,128)(2,1)S(1)}, u32[]{:S(2)}, u32[]{:S(2)}) collective-permute-start(bf16[112,1152]{1,0:T(8,128)(2,1)S(1)} %get-tuple-element.13.refs_0_), channel_id=1, source_target_pairs={{0,2},{2,0},{4,6},{6,4},{8,10},{10,8},{12,14},{14,12},{1,3},{3,1},... | collective-permute-start | bytes 774152 | tf_op jit(solution)/shard_map/ppermute | solution.py:282
  16.1 31.1 %collective-permute-start.8 = (bf16[112,1152]{1,0:T(8,128)(2,1)S(1)}, bf16[112,1152]{1,0:T(8,128)(2,1)S(1)}, u32[]{:S(2)}, u32[]{:S(2)}) collective-permute-start(bf16[112,1152]{1,0:T(8,128)(2,1)S(1)} %collective-permute-done.6.refs_0_), channel_id=1, source_target_pairs={{0,2},{2,0},{4,6},{6,4},{8,10},{10,8},{12,14},{14,12},{1,3},{3,1},... | collective-permute-start | bytes 774152 | tf_op jit(solution)/shard_map/ppermute | solution.py:282
  20.8 26.4 %collective-permute-start.9 = (bf16[112,1152]{1,0:T(8,128)(2,1)S(1)}, bf16[112,1152]{1,0:T(8,128)(2,1)S(1)}, u32[]{:S(2)}, u32[]{:S(2)}) collective-permute-start(bf16[112,1152]{1,0:T(8,128)(2,1)S(1)} %collective-permute-done.7.refs_1_), channel_id=1, source_target_pairs={{0,2},{2,0},{4,6},{6,4},{8,10},{10,8},{12,14},{14,12},{1,3},{3,1},... | collective-permute-start | bytes 774152 | tf_op jit(solution)/shard_map/ppermute | solution.py:282
  32.5 25.4 %collective-permute-start.2 = (bf16[112,1152]{1,0:T(8,128)(2,1)S(1)}, bf16[112,1152]{1,0:T(8,128)(2,1)S(1)}, u32[]{:S(2)}, u32[]{:S(2)}) collective-permute-start(bf16[112,1152]{1,0:T(8,128)(2,1)S(1)} %collective-permute-done.refs_1_), channel_id=1, source_target_pairs={{0,2},{2,0},{4,6},{6,4},{8,10},{10,8},{12,14},{14,12},{1,3},{3,1},... | collective-permute-start | bytes 774152 | tf_op jit(solution)/shard_map/ppermute | solution.py:282
  32.5 1.8 %copy-start = (bf16[1,1152,1152]{2,1,0:T(8,128)(2,1)S(1)}, bf16[1,1152,1152]{2,1,0:T(8,128)(2,1)}, u32[]{:S(2)}) copy-start(bf16[1,1152,1152]{2,1,0:T(8,128)(2,1)} %refs_7_.3) | copy-start | bytes 7962628
  34.3 1.7 %copy-start.2 = (bf16[1,1152,1152]{2,1,0:T(8,128)(2,1)S(1)}, bf16[1,1152,1152]{2,1,0:T(8,128)(2,1)}, u32[]{:S(2)}) copy-start(bf16[1,1152,1152]{2,1,0:T(8,128)(2,1)} %refs_8_.3) | copy-start | bytes 7962628
  36.0 1.2 %copy-start.4 = (bf16[1,400,1152]{2,1,0:T(8,128)(2,1)S(1)}, bf16[1,400,1152]{2,1,0:T(8,128)(2,1)}, u32[]{:S(2)}) copy-start(bf16[1,400,1152]{2,1,0:T(8,128)(2,1)} %param.10) | copy-start | bytes 2764804
  37.2 10.1 %copy-start.1 = (bf16[1,1152,1152]{2,1,0:T(8,128)(2,1)S(1)}, bf16[1,1152,1152]{2,1,0:T(8,128)(2,1)}, u32[]{:S(2)}) copy-start(bf16[1,1152,1152]{2,1,0:T(8,128)(2,1)} %refs_7_.3) | copy-start | bytes 7962628
  37.2 10.1 %copy-start.3 = (bf16[1,1152,1152]{2,1,0:T(8,128)(2,1)S(1)}, bf16[1,1152,1152]{2,1,0:T(8,128)(2,1)}, u32[]{:S(2)}) copy-start(bf16[1,1152,1152]{2,1,0:T(8,128)(2,1)} %refs_8_.3) | copy-start | bytes 7962628
  57.3 10.6 %collective-permute-start.10 = (bf16[2,224,576]{2,1,0:T(8,128)(2,1)S(1)}, bf16[2,224,576]{2,1,0:T(8,128)(2,1)S(1)}, u32[]{:S(2)}, u32[]{:S(2)}) collective-permute-start(bf16[2,224,576]{2,1,0:T(8,128)(2,1)S(1)} %get-tuple-element.23), channel_id=1, source_target_pairs={{0,2},{2,0},{4,6},{6,4},{8,10},{10,8},{12,14},{14,12},{1,3},{3,1},... | collective-permute-start | bytes 1548296 | tf_op jit(solution)/shard_map/ppermute | solution.py:282
  67.8 2.0 %collective-permute-start.4 = (bf16[2,224,576]{2,1,0:T(8,128)(2,1)S(1)}, bf16[2,224,576]{2,1,0:T(8,128)(2,1)S(1)}, u32[]{:S(2)}, u32[]{:S(2)}) collective-permute-start(bf16[2,224,576]{2,1,0:T(8,128)(2,1)S(1)} %get-tuple-element.19), channel_id=1, source_target_pairs={{0,2},{2,0},{4,6},{6,4},{8,10},{10,8},{12,14},{14,12},{1,3},{3,1},... | collective-permute-start | bytes 1548296 | tf_op jit(solution)/shard_map/ppermute | solution.py:282
  68.0 9.7 %collective-permute-start.11 = (bf16[224,576]{1,0:T(8,128)(2,1)S(1)}, bf16[224,576]{1,0:T(8,128)(2,1)S(1)}, u32[]{:S(2)}, u32[]{:S(2)}) collective-permute-start(bf16[224,576]{1,0:T(8,128)(2,1)S(1)} %fusion.3), channel_id=1, source_target_pairs={{0,1},{1,0},{2,3},{3,2},{4,5},{5,4},{6,7},{7,6},{8,9},{9,8},{10,11... | collective-permute-start | bytes 774152 | tf_op jit(solution)/shard_map/ppermute | solution.py:290
  69.9 13.7 %copy-start.6 = (f32[160,2]{0,1:T(2,128)S(1)}, f32[160,2]{0,1:T(2,128)}, u32[]{:S(2)}) copy-start(f32[160,2]{0,1:T(2,128)} %param.9) | copy-start | bytes 3844
  69.9 13.5 %collective-permute-start.5 = (bf16[224,576]{1,0:T(8,128)(2,1)S(1)}, bf16[224,576]{1,0:T(8,128)(2,1)S(1)}, u32[]{:S(2)}, u32[]{:S(2)}) collective-permute-start(bf16[224,576]{1,0:T(8,128)(2,1)S(1)} %fusion.2), channel_id=1, source_target_pairs={{0,1},{1,0},{2,3},{3,2},{4,5},{5,4},{6,7},{7,6},{8,9},{9,8},{10,11... | collective-permute-start | bytes 774152 | tf_op jit(solution)/shard_map/ppermute | solution.py:290
  77.8 6.7 %collective-permute-start.12 = (bf16[112,576]{1,0:T(8,128)(2,1)S(1)}, bf16[112,576]{1,0:T(8,128)(2,1)S(1)}, u32[]{:S(2)}, u32[]{:S(2)}) collective-permute-start(bf16[112,576]{1,0:T(8,128)(2,1)S(1)} %get-tuple-element.27), channel_id=1, source_target_pairs={{0,12},{2,14},{4,0},{6,2},{8,4},{10,6},{12,8},{14,10},{1,13},{3,15... | collective-permute-start | bytes 387080 | tf_op jit(solution)/shard_map/ppermute | solution.py:296
  79.5 7.5 %collective-permute-start.14 = (bf16[112,576]{1,0:T(8,128)(2,1)S(1)}, bf16[112,576]{1,0:T(8,128)(2,1)S(1)}, u32[]{:S(2)}, u32[]{:S(2)}) collective-permute-start(bf16[112,576]{1,0:T(8,128)(2,1)S(1)} %get-tuple-element.26), channel_id=1, source_target_pairs={{0,4},{2,6},{4,8},{6,10},{8,12},{10,14},{12,0},{14,2},{1,5},{3,7},... | collective-permute-start | bytes 387080 | tf_op jit(solution)/shard_map/ppermute | solution.py:296
  83.6 9.0 %collective-permute-start.13 = (bf16[112,576]{1,0:T(8,128)(2,1)S(1)}, bf16[112,576]{1,0:T(8,128)(2,1)S(1)}, u32[]{:S(2)}, u32[]{:S(2)}) collective-permute-start(bf16[112,576]{1,0:T(8,128)(2,1)S(1)} %get-tuple-element.28), channel_id=1, source_target_pairs={{0,8},{2,10},{4,12},{6,14},{8,0},{10,2},{12,4},{14,6},{1,9},{3,11}... | collective-permute-start | bytes 387080 | tf_op jit(solution)/shard_map/ppermute | solution.py:296

commit v2 on v0

v2 whole, which is shorter than its diff:
```python
import functools

import jax
import jax.numpy as jnp
from jax import lax
from jax.experimental import pallas as pl
from jax.experimental.pallas import tpu as pltpu
from jax.sharding import PartitionSpec as P

LANES = 128
NT = (((1,), (1,)), ((), ()))


def params(limit=10 << 20):
    return pltpu.CompilerParams(vmem_limit_bytes=limit)


def whole():
    return pl.BlockSpec(memory_space=pltpu.VMEM)


def smem():
    return pl.BlockSpec(memory_space=pltpu.SMEM)


def cost():
    return pl.CostEstimate(flops=1000, bytes_accessed=1000, transcendentals=0)


def in_hbm(value):
    return pltpu.with_memory_space_constraint(value, pltpu.HBM)


def dot(a, b, dims=(((1,), (0,)), ((), ()))):
    return lax.dot_general(a, b, dims, preferred_element_type=jnp.float32)


def ring(value, peers):
    return jnp.where(value < 0, value + peers, value)


def named_rows(index_ref, peer, peers):
    rel = ring(index_ref[...] - peer, peers)
    count, rows = rel.shape
    expert = lax.broadcasted_iota(jnp.int32, (-(-peers // 8) * 8, rows), 0)
    named = rel[0:1, :] == expert
    for k in range(1, count):
        named = named | (rel[k : k + 1, :] == expert)
    return rel, named


def slot_rows(named):
    rows = named.shape[1]
    first = lax.broadcasted_iota(jnp.int32, (rows, rows), 0)
    second = lax.broadcasted_iota(jnp.int32, (rows, rows), 1)
    before = dot(named.astype(jnp.bfloat16), (first < second).astype(jnp.bfloat16))
    return jnp.where(named, before.astype(jnp.int32), -1)


def route_kernel(peers, padded, spread, meta, index_hbm, grad_hbm, *refs):
    outs, (index_ref, grad_ref, sems) = refs[:peers], refs[peers:]
    copies = [
        pltpu.make_async_copy(index_hbm, index_ref, sems.at[0]),
        pltpu.make_async_copy(grad_hbm, grad_ref, sems.at[1]),
    ]
    for copy in copies:
        copy.start()
    copies[0].wait()
    rows = grad_ref.shape[0]
    _, named = named_rows(index_ref, meta[0], peers)
    slots = slot_rows(named)
    place = lax.broadcasted_iota(jnp.int32, (padded, rows), 0)
    copies[1].wait()
    grad = grad_ref[...]
    for d, out in enumerate(outs):
        pick = (place == slots[d : d + 1, :]).astype(jnp.bfloat16)
        block = dot(pick, grad)
        share = out.shape[1]
        if d in spread:
            chosen = block[:, :share]
            for i in range(1, block.shape[1] // share):
                chosen = jnp.where(meta[2] == i, block[:, i * share : (i + 1) * share], chosen)
            block = chosen
        out[...] = block.astype(jnp.bfloat16)


def route(meta, index_rows, out_grad, peers, padded, spread, shares):
    width = out_grad.shape[1]
    hbm = pl.BlockSpec(memory_space=pltpu.HBM)
    return pl.pallas_call(
        functools.partial(route_kernel, peers, padded, spread),
        out_shape=[
            jax.ShapeDtypeStruct((padded, width // shares if d in spread else width), jnp.bfloat16)
            for d in range(peers)
        ],
        in_specs=[smem(), hbm, hbm],
        out_specs=[whole()] * peers,
        scratch_shapes=[
            pltpu.VMEM(index_rows.shape, index_rows.dtype),
            pltpu.VMEM(out_grad.shape, out_grad.dtype),
            pltpu.SemaphoreType.DMA((2,)),
        ],
        compiler_params=params(),
        cost_estimate=cost(),
        name="route",
    )(meta, in_hbm(index_rows), in_hbm(out_grad))


def unit_blocks(units):
    return [pl.ds(start, min(256, units - start)) for start in range(0, units, 256)]


def forward_kernel(peers, cap, padded, order, meta, own_hbm, other_ref, gate_hbm, up_hbm, down_hbm, act_ref, slope_ref, hid_ref, gate_ref, up_ref, down_ref, own_ref, rows_ref, sems):
    first = pltpu.make_async_copy(own_hbm.at[0], own_ref, sems.at[0])
    last = pltpu.make_async_copy(down_hbm.at[0], down_ref, sems.at[1])
    first.start()
    units = unit_blocks(gate_ref.shape[1])
    loads = []
    for n, unit in enumerate(units):
        loads.append(
            [
                pltpu.make_async_copy(source.at[0, :, unit], target.at[:, unit], sems.at[2 + 2 * n + m])
                for m, (source, target) in enumerate(((gate_hbm, gate_ref), (up_hbm, up_ref)))
            ]
        )
        for load in loads[-1]:
            load.start()
    last.start()
    peer, pair = meta[0], meta[1]
    first.wait()
    for values, half in ((own_ref[...], pair), (other_ref[...], 1 - pair)):
        for k in range(peers):
            source = half * peers + k
            away = ring(peer - lax.div(source, 2), peers)
            swap = jnp.where(lax.rem(source, 2) == pair, 0, 1)
            position = 0
            for n, (d, core) in enumerate(order):
                position += jnp.where((away == d) & (swap == core), n, 0)
            target = pl.ds(pl.multiple_of(position * padded, 16), padded)
            block = values[k * cap : (k + 1) * cap]
            empty = jnp.zeros((padded - cap, values.shape[1]), values.dtype)
            rows_ref[target, :] = jnp.concatenate([block, empty], axis=0)
    rows = rows_ref[...]
    for unit, load in zip(units, loads):
        for copy in load:
            copy.wait()
        gate = dot(rows, gate_ref[:, unit])
        up = dot(rows, up_ref[:, unit])
        sig = jax.nn.sigmoid(gate)
        act = gate * sig
        act_ref[:, unit] = act.astype(jnp.bfloat16)
        slope_ref[:, unit] = (up * (sig + act * (1.0 - sig))).astype(jnp.bfloat16)
        hid_ref[:, unit] = (act * up).astype(jnp.bfloat16)
    last.wait()


def forward(meta, dispatched, other, w_gate, w_up, w_down, peers, cap, padded, order):
    half_rows, width = other.shape
    units = w_gate.shape[2]
    rows = len(order) * padded
    hbm = pl.BlockSpec(memory_space=pltpu.HBM)
    weights = [w_gate, w_up, w_down]
    return pl.pallas_call(
        functools.partial(forward_kernel, peers, cap, padded, order),
        out_shape=[jax.ShapeDtypeStruct((rows, units), jnp.bfloat16)] * 3
        + [pltpu.VMEM(w.shape[1:], w.dtype) for w in weights],
        in_specs=[smem(), hbm, whole(), hbm, hbm, hbm],
        out_specs=[whole()] * 6,
        scratch_shapes=[
            pltpu.VMEM((half_rows, width), jnp.bfloat16),
            pltpu.VMEM((rows, width), jnp.bfloat16),
            pltpu.SemaphoreType.DMA((2 + 2 * len(unit_blocks(units)),)),
        ],
        compiler_params=params(14 << 20),
        cost_estimate=cost(),
        name="forward",
    )(meta, in_hbm(dispatched), other, *[in_hbm(w) for w in weights])


def backward_kernel(counts, cap, first, meta, *refs):
    cots, refs = refs[: sum(counts)], refs[sum(counts) :]
    act_ref, slope_ref, hid_ref, gate_ref, up_ref, down_ref, keep, give, cot_ref, gate_grad, up_grad = refs
    padded = cots[0].shape[0]
    at = 0
    for n, parts in enumerate(counts):
        pieces = [ref[...] for ref in cots[at : at + parts]]
        at += parts
        full = jnp.concatenate([pieces[-i % parts] for i in range(parts)], axis=1)
        for h in range(1, parts):
            turned = jnp.concatenate([pieces[(h - i) % parts] for i in range(parts)], axis=1)
            full = jnp.where(meta[2] == h, turned, full)
        cot_ref[pl.ds(n * padded, padded), :] = full
    rows = pl.ds(first, len(counts) * padded)
    cot = cot_ref[...]
    part = jnp.zeros((len(counts) * padded, 1), jnp.float32)
    for unit in unit_blocks(gate_ref.shape[1]):
        d_hidden = dot(cot, down_ref[unit, :], NT)
        part += jnp.sum(d_hidden * hid_ref[rows, unit].astype(jnp.float32), axis=1, keepdims=True)
        gate_grad[:, unit] = (d_hidden * slope_ref[rows, unit].astype(jnp.float32)).astype(jnp.bfloat16)
        up_grad[:, unit] = (d_hidden * act_ref[rows, unit].astype(jnp.float32)).astype(jnp.bfloat16)
    back = dot(gate_grad[...], gate_ref[...], NT) + dot(up_grad[...], up_ref[...], NT)
    shares, kept, share = give.shape
    row = lax.broadcasted_iota(jnp.int32, (padded, share), 0)
    lane = lax.broadcasted_iota(jnp.int32, (padded, LANES), 1)
    diagonal = lax.broadcasted_iota(jnp.int32, (padded, LANES), 0) == lane
    for n in range(len(counts)):
        block = slice(n * padded, (n + 1) * padded)
        out, start = (keep, n * padded) if n < len(counts) // 2 else (give, n * padded - kept)
        line = jnp.sum(jnp.where(diagonal, part[block], 0.0), axis=0, keepdims=True)
        line = jnp.concatenate([line, jnp.zeros((1, share - LANES), jnp.float32)], axis=1)
        pieces = [back[block, i * share : (i + 1) * share] for i in range(shares)]
        for r in range(shares):
            piece = pieces[r]
            for i in range(shares):
                if i != r:
                    piece = jnp.where(meta[2] == (i - r) % shares, pieces[i], piece)
            piece = jnp.where(row < cap, piece, jnp.where(row == cap, line, 0.0))
            out[r, pl.ds(start, padded), :] = piece.astype(out.dtype)


def backward(meta, cots, tables, first, gate_mat, up_mat, down_mat, cap, shares):
    padded = cots[0][0].shape[0]
    width, units = gate_mat.shape
    rows = len(cots) * padded
    share = width // shares
    parts = [part for cot in cots for part in cot]
    return pl.pallas_call(
        functools.partial(backward_kernel, [len(cot) for cot in cots], cap, first),
        out_shape=[
            jax.ShapeDtypeStruct((shares, rows // 2, share), jnp.float32),
            jax.ShapeDtypeStruct((shares, rows // 2, share), jnp.bfloat16),
        ],
        in_specs=[smem()] + [whole()] * (len(parts) + 6),
        out_specs=[whole()] * 2,
        scratch_shapes=[
            pltpu.VMEM((rows, width), jnp.bfloat16),
            pltpu.VMEM((rows, units), jnp.bfloat16),
            pltpu.VMEM((rows, units), jnp.bfloat16),
        ],
        compiler_params=params(14 << 20),
        cost_estimate=cost(),
        name="backward",
    )(meta, *parts, *tables, gate_mat, up_mat, down_mat)


def combine_kernel(peers, cap, meta, index_ref, gates_ref, *refs):
    blocks = refs[:peers]
    grad_ref, gate_out = refs[peers:]
    rows = grad_ref.shape[0]
    padded = blocks[0].shape[0]
    rel, named = named_rows(index_ref, meta[0], peers)
    slots = slot_rows(named)
    gates = gates_ref[...]
    diagonal = lax.broadcasted_iota(jnp.int32, (rows, rows), 0) == lax.broadcasted_iota(
        jnp.int32, (rows, rows), 1
    )

    def column(row):
        return jnp.sum(jnp.where(diagonal, row, 0), axis=1, keepdims=True)

    place = lax.broadcasted_iota(jnp.int32, (rows, padded), 1)
    total = jnp.zeros(grad_ref.shape, jnp.float32)
    products = jnp.zeros(rel.shape, jnp.float32)
    for d, block in enumerate(blocks):
        chosen = rel == d
        weight = column(jnp.sum(jnp.where(chosen, gates, 0.0), axis=0, keepdims=True))
        pick = (place == column(slots[d : d + 1, :])).astype(jnp.bfloat16)
        values = block[...]
        total += weight * dot(pick, values)
        found = dot(values[cap:padded, :padded], pick, NT)
        products += jnp.where(chosen, found[0:1, :], 0.0)
    grad_ref[...] = total.astype(jnp.bfloat16)
    gate_out[...] = products.astype(jnp.bfloat16)


def combine(meta, index_rows, gate_rows, blocks, cap):
    count, rows = index_rows.shape
    peers = len(blocks)
    padded, share = blocks[0].shape
    return pl.pallas_call(
        functools.partial(combine_kernel, peers, cap),
        out_shape=[
            jax.ShapeDtypeStruct((rows, share), jnp.bfloat16),
            jax.ShapeDtypeStruct((count, rows), jnp.bfloat16),
        ],
        in_specs=[smem()] + [whole()] * (2 + peers),
        out_specs=[whole()] * 2,
        compiler_params=params(),
        cost_estimate=cost(),
        name="combine",
    )(meta, index_rows, gate_rows, *blocks)


def after(value, others):
    return lax.optimization_barrier((value, others))[0]


def swap_pair(block):
    count = lax.axis_size("expert")
    return lax.ppermute(block, "expert", [(i, i ^ 1) for i in range(count)])


def hidden_ring(block, r):
    count = lax.axis_size("hidden")
    return lax.ppermute(block, "hidden", [(i, (i + r) % count) for i in range(count)])


def shifted(block, d):
    count = lax.axis_size("expert")
    return lax.ppermute(block, "expert", [(i, (i + 2 * d) % count) for i in range(count)])


def chunk_groups(peers):
    rest = sorted(range(1, peers), key=lambda d: (-min(d, peers - d), d))
    rest = rest[:1] + sorted(rest[1:], key=lambda d: (min(d, peers - d), d))
    return [[0]] + [rest[n : n + 2] for n in range(0, len(rest), 2)]


def local(out_grad, expert_index, gate_values, dispatched_inputs, w_gate, w_up, w_down):
    peers = lax.axis_size("expert") // 2
    shares = lax.axis_size("hidden")
    index = lax.axis_index("expert")
    meta = jnp.stack([index // 2, index % 2, lax.axis_index("hidden")]).astype(jnp.int32)
    half_rows = dispatched_inputs.shape[1]
    cap = half_rows // peers
    padded = (cap // 16 + 1) * 16
    index_rows = expert_index.T
    other_rows = swap_pair(dispatched_inputs[0])
    sent = route(meta, index_rows, out_grad, peers, padded, (), shares)
    arrived = [shifted(block, d) if d else block for d, block in enumerate(sent)]

    groups = chunk_groups(peers)
    order = tuple((d, swap) for group in groups for swap in (0, 1) for d in group)
    *tables, gate_mat, up_mat, down_mat = forward(
        meta, dispatched_inputs, other_rows, w_gate, w_up, w_down, peers, cap, padded, order
    )

    gives, crossings, totals, returned = [], [], [], {}
    first = 0
    ready = {d: arrived[d] for d in groups[0]}

    def finish(n, later):
        total, parts, _ = crossings[n]
        for part in after(parts, later):
            total = total + part.astype(jnp.float32)
        totals.append(total.astype(jnp.bfloat16))
        for m, d in enumerate(groups[n]):
            block = totals[n][m * padded : (m + 1) * padded]
            returned[d] = shifted(block, -d) if d else block

    for n, group in enumerate(groups):
        swapped = {d: swap_pair(ready[d]) for d in group}
        cots = [[ready[d]] for d in group] + [[swapped[d]] for d in group]
        cots = after(cots, ([c[2] for c in crossings], totals, gives))
        keep, give = backward(meta, cots, tables, first, gate_mat, up_mat, down_mat, cap, shares)
        first += 2 * len(group) * padded
        gives.append(give)
        ready = {}
        for d in groups[n + 1] if n + 1 < len(groups) else []:
            ready[d] = after(arrived[d], give)
        done = list(ready.values())
        if n:
            finish(n - 1, give)
            done.append(totals[-1])
        got = swap_pair(after(give, done))
        pieces = [keep[r] + got[r].astype(jnp.float32) for r in range(shares)]
        crossing = [piece.astype(jnp.bfloat16) for piece in pieces[1:]]
        crossings.append((pieces[0], [hidden_ring(c, r + 1) for r, c in enumerate(crossing)], crossing))
    finish(len(groups) - 1, [])
    blocks = [returned[d] for d in range(peers)]
    input_grad, gate_grad = combine(meta, index_rows, gate_values.T, blocks, cap)
    return input_grad, gate_grad.T


def solution(mesh):
    in_specs = (
        P(("groups", "expert", "tok"), None),
        P(("groups", "expert", "tok"), None),
        P(("groups", "expert", "tok"), None),
        P("expert", ("groups", "tok"), None),
        P("expert", None, "hidden"),
        P("expert", None, "hidden"),
        P("expert", "hidden", None),
    )
    out_specs = (P(("groups", "expert", "tok"), "hidden"), P(("groups", "expert", "tok"), None))
    return jax.shard_map(local, mesh=mesh, in_specs=in_specs, out_specs=out_specs, check_vma=False)
```

time: 187 us -> 67.2 us (0.36)
  waiting for transfers between devices: 77.5 us -> 22.4 us
  local copies, waits for them, and re-layouts: 37.3 us -> 0.04 us
  matrix products: 28.2 us -> 0 us
  Pallas kernels: 0 us -> 27.4 us
  between operations: 14.3 us -> 0.76 us
  other arithmetic: 7.62 us -> 0.45 us
  blocking collectives: 4.92 us -> 0 us
    all_to_all x3 -> x0, waiting for transfers between devices: 43.2 us -> none  [the longest x1 29.4 us: local(): lax.all_to_all(outgoing, 'expert', split_axis=0, concat_axis=0, tiled=True)]
    unnamed x2 -> x0, waiting for transfers between devices: 30.5 us -> none
    dot_general x5 -> x0, matrix products: 28.2 us -> none  [the longest x1 7.63 us: expert_rows(): lax.dot_general(cotangent, down_mat, (((1,), (1,)), ((), ())), preferred_...]
    pallas_call x0 -> x6, Pallas kernels: none -> 27.4 us  [the longest x3 14.1 us: backward(): pl.pallas_call(functools.partial(backward_kernel, [len(cot) for cot in co...]
    ppermute x3 -> x17, waiting for transfers between devices: 3.78 us -> 22.4 us  [the longest x6 13.4 us: shifted(): lax.ppermute(block, 'expert', [(i, (i + 2 * d) % count) for i in range(co...]
    all_to_all x3 -> x0, starting transfers between devices: 15.4 us -> none  [the longest x1 6.33 us: local(): lax.all_to_all(outgoing, 'expert', split_axis=0, concat_axis=0, tiled=True)]
    ppermute x3 -> x17, starting transfers between devices: 0.54 us -> 15.9 us  [the longest x6 9.8 us: shifted(): lax.ppermute(block, 'expert', [(i, (i + 2 * d) % count) for i in range(co...]
    reshape x7 -> x0, local copies, waits for them, and re-layouts: 11.1 us -> none  [the longest x2 2.77 us: local(): grad_half.astype(jnp.bfloat16).reshape(expert_count, capacity, feat_half)]
  transfers between devices with their start and end apart: 7 -> 17, of which waited for: 6 -> 7; matrix products, arithmetic and copies ran while one was open for 12% -> 0% of each run, Pallas kernels for 0% -> 38%
where the time goes in v2:
time: 67.2 us; the launch traced here: 67 us
  Pallas kernels  27.4 us (41%)
  waiting for transfers between devices  22.4 us (33%)
  starting transfers between devices  15.9 us (24%)
  between operations  0.76 us (1%)
    pallas_call x3, Pallas kernels, backward(): pl.pallas_call(functools.partial(backward_kernel, [len(cot) for cot in co...  14.1 us
    ppermute x6, waiting for transfers between devices, shifted(): lax.ppermute(block, 'expert', [(i, (i + 2 * d) % count) for i in range(co...  13.4 us
    ppermute x6, starting transfers between devices, shifted(): lax.ppermute(block, 'expert', [(i, (i + 2 * d) % count) for i in range(co...  9.8 us
    pallas_call x1, Pallas kernels, forward(): pl.pallas_call(functools.partial(forward_kernel, peers, cap, padded, orde...  9.34 us
    ppermute x3, waiting for transfers between devices, hidden_ring(): lax.ppermute(block, 'hidden', [(i, (i + r) % count) for i in range(count)])  5.98 us
    ppermute x3, starting transfers between devices, hidden_ring(): lax.ppermute(block, 'hidden', [(i, (i + r) % count) for i in range(count)])  4.33 us
    ppermute x8, waiting for transfers between devices, swap_pair(): return lax.ppermute(block, 'expert', [(i, i ^ 1) for i in range(count)])  3.04 us
    pallas_call x1, Pallas kernels, route(): pl.pallas_call(functools.partial(route_kernel, peers, padded, spread), ou...  2.03 us
  transfers between devices with their start and end apart: 17, of which 7 were waited for; matrix products, arithmetic and copies ran while one was open for 0% of the time, Pallas kernels for 38%

profile of v2, /device:TPU:0, one launch (start us, length us, event | category | flops | bytes accessed | tf_op | source)
XLA Modules:
  0.0 67.0 jit_solution(1227821612561640603)
XLA Ops:
  0.6 0.5 collective-permute-start.1
  1.1 0.1 pad_add_fusion.meta
  1.2 2.0 %route.1 = (bf16[112,1152]{1,0:T(8,128)(2,1)S(1)}, bf16[112,1152]{1,0:T(8,128)(2,1)S(1)}, bf16[112,1152]{1,0:T(8,128)(2,1)S(1)}, bf16[112,1152]{1,0:T(8,128)(2,1)S(1)}) custom-call(s32[3]{0:T(128)S(1)} %pad_add_fusion.meta, s32[2,160]{1,0:T(2,128)} %bitcast.25, bf16[160,1152]{1,0:T(8,128)(2,1)} %grad_hbm.1), custom_call_target="tpu_custom_call" | custom-call | flops 1000 | bytes 1000 | tf_op jit(solution)/shard_map/route/pallas_call | solution.py:90
  3.3 0.1 collective-permute-start
  3.4 3.0 %collective-permute-start.3 = (bf16[112,1152]{1,0:T(8,128)(2,1)S(1)}, bf16[112,1152]{1,0:T(8,128)(2,1)S(1)}, u32[]{:S(2)}, u32[]{:S(2)}) collective-permute-start(bf16[112,1152]{1,0:T(8,128)(2,1)S(1)} %get-tuple-element.49), channel_id=1, source_target_pairs={{0,4},{2,6},{4,8},{6,10},{8,12},{10,14},{12,0},{14,2},{1,5},{3,7},... | collective-permute-start | bytes 774152 | tf_op jit(solution)/shard_map/ppermute | solution.py:310
  6.4 2.6 %collective-permute-start.2 = (bf16[112,1152]{1,0:T(8,128)(2,1)S(1)}, bf16[112,1152]{1,0:T(8,128)(2,1)S(1)}, u32[]{:S(2)}, u32[]{:S(2)}) collective-permute-start(bf16[112,1152]{1,0:T(8,128)(2,1)S(1)} %get-tuple-element.47), channel_id=1, source_target_pairs={{0,8},{2,10},{4,12},{6,14},{8,0},{10,2},{12,4},{14,6},{1,9},{3,11}... | collective-permute-start | bytes 774152 | tf_op jit(solution)/shard_map/ppermute | solution.py:310
  9.0 0.0 collective-permute-done.refs_1_
  9.0 0.0 collective-permute-done.1.other_ref
  9.0 9.3 %forward.1 = (bf16[896,1152]{1,0:T(8,128)(2,1)S(1)}, bf16[896,1152]{1,0:T(8,128)(2,1)S(1)}, bf16[896,1152]{1,0:T(8,128)(2,1)S(1)}, bf16[1152,1152]{1,0:T(8,128)(...) custom-call(s32[3]{0:T(128)S(1)} %pad_add_fusion.meta, bf16[1,400,1152]{2,1,0:T(8,128)(2,1)} %own_hbm.1, ...), custom_call_target="tpu_custom_call" | custom-call | flops 1000 | bytes 1000 | tf_op jit(solution)/shard_map/forward/pallas_call | solution.py:163
  18.3 3.9 %backward.3 = (f32[2,112,576]{2,1,0:T(8,128)S(1)}, bf16[2,112,576]{2,1,0:T(8,128)(2,1)S(1)}) custom-call(s32[3]{0:T(128)S(1)} %pad_add_fusion.meta, bf16[112,1152]{1,0:T(8,128)(2,1)S(1)} %get-tuple-element.37.refs_0_, bf16[112,1152]{1,0:T(8,128)(2,1)S(1)} %collective-permute-done.refs_1_, bf16[896,1152]{1,0:T(8,128)(2,1)S(1)} %get-tuple-element.39.refs_2_.refs_4_, ...), custom_call_target="tpu_custom_call" | custom-call | flops 1000 | bytes 1000 | tf_op jit(solution)/shard_map/backward/pallas_call | solution.py:227
  22.2 0.0 collective-permute-done.3.refs_1_
  22.2 3.7 %collective-permute-done.2.refs_0_ = bf16[112,1152]{1,0:T(8,128)(2,1)S(1)} collective-permute-done((bf16[112,1152]{1,0:T(8,128)(2,1)S(1)}, bf16[112,1152]{1,0:T(8,128)(2,1)S(1)}, u32[]{:S(2)}, u32[]{:S(2)}) %collective-permute-start.2) | collective-permute-done | bytes 258080 | tf_op jit(solution)/shard_map/ppermute | solution.py:310
  25.9 0.0 collective-permute-start.4
  26.0 1.6 %collective-permute-start.8 = (bf16[112,1152]{1,0:T(8,128)(2,1)S(1)}, bf16[112,1152]{1,0:T(8,128)(2,1)S(1)}, u32[]{:S(2)}, u32[]{:S(2)}) collective-permute-start(bf16[112,1152]{1,0:T(8,128)(2,1)S(1)} %get-tuple-element.59), channel_id=1, source_target_pairs={{0,12},{2,14},{4,0},{6,2},{8,4},{10,6},{12,8},{14,10},{1,13},{3,15... | collective-permute-start | bytes 774152 | tf_op jit(solution)/shard_map/ppermute | solution.py:310
  27.6 0.2 collective-permute-start.7
  27.8 0.3 collective-permute-start.6
  28.1 0.0 collective-permute-done.4
  28.1 1.6 %collective-permute-start.5 = (bf16[112,576]{1,0:T(8,128)(2,1)S(1)}, bf16[112,576]{1,0:T(8,128)(2,1)S(1)}, u32[]{:S(2)}, u32[]{:S(2)}) collective-permute-start(bf16[112,576]{1,0:T(8,128)(2,1)S(1)} %fusion.4), channel_id=1, source_target_pairs={{0,1},{1,0},{2,3},{3,2},{4,5},{5,4},{6,7},{7,6},{8,9},{9,8},{10,11... | collective-permute-start | bytes 387080 | tf_op jit(solution)/shard_map/ppermute | solution.py:305
  29.7 0.0 collective-permute-done.7.refs_3_
  29.7 0.0 collective-permute-done.6.refs_2_
  29.7 6.4 %backward.4 = (f32[2,224,576]{2,1,0:T(8,128)S(1)}, bf16[2,224,576]{2,1,0:T(8,128)(2,1)S(1)}) custom-call(s32[3]{0:T(128)S(1)} %pad_add_fusion.meta, bf16[112,1152]{1,0:T(8,128)(2,1)S(1)} %collective-permute-done.2.refs_0_, bf16[112,1152]{1,0:T(8,128)(2,1)S(1)} %collective-permute-done.3.refs_1_, bf16[112,1152]{1,0:T(8,128)(2,1)S(1)} %collective-permute-done.6.refs_2_, ...), custom_call_target="tpu_custom_call" | custom-call | flops 1000 | bytes 1000 | tf_op jit(solution)/shard_map/backward/pallas_call | solution.py:227
  36.1 0.0 collective-permute-done.8.refs_0_
  36.1 0.0 collective-permute-done.5
  36.1 0.1 fusion.3.refs_0_
  36.1 0.1 collective-permute-start.9
  36.2 0.5 collective-permute-start.11
  36.7 1.5 %collective-permute-done.9 = bf16[2,224,576]{2,1,0:T(8,128)(2,1)S(1)} collective-permute-done((bf16[2,224,576]{2,1,0:T(8,128)(2,1)S(1)}, bf16[2,224,576]{2,1,0:T(8,128)(2,1)S(1)}, u32[]{:S(2)}, u32[]{:S(2)}) %collective-permute-start.9) | collective-permute-done | bytes 516128 | tf_op jit(solution)/shard_map/ppermute | solution.py:300
  38.2 0.1 fusion.1
  38.3 1.3 %collective-permute-start.10 = (bf16[224,576]{1,0:T(8,128)(2,1)S(1)}, bf16[224,576]{1,0:T(8,128)(2,1)S(1)}, u32[]{:S(2)}, u32[]{:S(2)}) collective-permute-start(bf16[224,576]{1,0:T(8,128)(2,1)S(1)} %fusion.1), channel_id=1, source_target_pairs={{0,1},{1,0},{2,3},{3,2},{4,5},{5,4},{6,7},{7,6},{8,9},{9,8},{10,11... | collective-permute-start | bytes 774152 | tf_op jit(solution)/shard_map/ppermute | solution.py:305
  39.6 0.0 collective-permute-done.11.refs_1_
  39.6 3.9 %backward.5 = (f32[2,112,576]{2,1,0:T(8,128)S(1)}, bf16[2,112,576]{2,1,0:T(8,128)(2,1)S(1)}) custom-call(s32[3]{0:T(128)S(1)} %pad_add_fusion.meta, bf16[112,1152]{1,0:T(8,128)(2,1)S(1)} %collective-permute-done.8.refs_0_, bf16[112,1152]{1,0:T(8,128)(2,1)S(1)} %collective-permute-done.11.refs_1_, bf16[896,1152]{1,0:T(8,128)(2,1)S(1)} %get-tuple-element.39.refs_2_.refs_4_, ...), custom_call_target="tpu_custom_call" | custom-call | flops 1000 | bytes 1000 | tf_op jit(solution)/shard_map/backward/pallas_call | solution.py:227
  43.5 0.0 copy-start
  43.5 0.0 copy-start.1
  43.5 3.7 %collective-permute-done.10 = bf16[224,576]{1,0:T(8,128)(2,1)S(1)} collective-permute-done((bf16[224,576]{1,0:T(8,128)(2,1)S(1)}, bf16[224,576]{1,0:T(8,128)(2,1)S(1)}, u32[]{:S(2)}, u32[]{:S(2)}) %collective-permute-start.10) | collective-permute-done | bytes 258080 | tf_op jit(solution)/shard_map/ppermute | solution.py:305
  47.2 0.1 fusion
  47.3 0.1 collective-permute-start.14
  47.4 1.6 %collective-permute-done.14 = bf16[2,112,576]{2,1,0:T(8,128)(2,1)S(1)} collective-permute-done((bf16[2,112,576]{2,1,0:T(8,128)(2,1)S(1)}, bf16[2,112,576]{2,1,0:T(8,128)(2,1)S(1)}, u32[]{:S(2)}, u32[]{:S(2)}) %collective-permute-start.14) | collective-permute-done | bytes 258080 | tf_op jit(solution)/shard_map/ppermute | solution.py:300
  49.0 1.4 %collective-permute-start.15 = (bf16[112,576]{1,0:T(8,128)(2,1)S(1)}, bf16[112,576]{1,0:T(8,128)(2,1)S(1)}, u32[]{:S(2)}, u32[]{:S(2)}) collective-permute-start(bf16[112,576]{1,0:T(8,128)(2,1)S(1)} %fusion.5), channel_id=1, source_target_pairs={{0,1},{1,0},{2,3},{3,2},{4,5},{5,4},{6,7},{7,6},{8,9},{9,8},{10,11... | collective-permute-start | bytes 387080 | tf_op jit(solution)/shard_map/ppermute | solution.py:305
  50.5 2.1 %collective-permute-start.12 = (bf16[112,576]{1,0:T(8,128)(2,1)S(1)}, bf16[112,576]{1,0:T(8,128)(2,1)S(1)}, u32[]{:S(2)}, u32[]{:S(2)}) collective-permute-start(bf16[112,576]{1,0:T(8,128)(2,1)S(1)} %get-tuple-element.71), channel_id=1, source_target_pairs={{0,12},{2,14},{4,0},{6,2},{8,4},{10,6},{12,8},{14,10},{1,13},{3,15... | collective-permute-start | bytes 387080 | tf_op jit(solution)/shard_map/ppermute | solution.py:310
  52.6 0.0 collective-permute-start.13
  52.6 2.3 %collective-permute-done.15 = bf16[112,576]{1,0:T(8,128)(2,1)S(1)} collective-permute-done((bf16[112,576]{1,0:T(8,128)(2,1)S(1)}, bf16[112,576]{1,0:T(8,128)(2,1)S(1)}, u32[]{:S(2)}, u32[]{:S(2)}) %collective-permute-start.15) | collective-permute-done | bytes 129056 | tf_op jit(solution)/shard_map/ppermute | solution.py:305
  54.9 0.1 fusion.2
  54.9 0.5 collective-permute-start.16
  55.4 1.3 %collective-permute-done.12.refs_1_ = bf16[112,576]{1,0:T(8,128)(2,1)S(1)} collective-permute-done((bf16[112,576]{1,0:T(8,128)(2,1)S(1)}, bf16[112,576]{1,0:T(8,128)(2,1)S(1)}, u32[]{:S(2)}, u32[]{:S(2)}) %collective-permute-start.12) | collective-permute-done | bytes 129056 | tf_op jit(solution)/shard_map/ppermute | solution.py:310
  56.7 8.4 %collective-permute-done.13.refs_2_ = bf16[112,576]{1,0:T(8,128)(2,1)S(1)} collective-permute-done((bf16[112,576]{1,0:T(8,128)(2,1)S(1)}, bf16[112,576]{1,0:T(8,128)(2,1)S(1)}, u32[]{:S(2)}, u32[]{:S(2)}) %collective-permute-start.13) | collective-permute-done | bytes 129056 | tf_op jit(solution)/shard_map/ppermute | solution.py:310
  65.1 0.0 collective-permute-done.16.refs_3_
  65.1 0.0 copy-done.1
  65.1 1.9 %combine.1 = (bf16[160,576]{1,0:T(8,128)(2,1)}, bf16[2,160]{1,0:T(2,128)(2,1)}) custom-call(s32[3]{0:T(128)S(1)} %pad_add_fusion.meta, s32[2,160]{1,0:T(2,128)S(1)} %bitcast.26, f32[2,160]{1,0:T(2,128)S(1)} %bitcast.27, bf16[112,576]{1,0:T(8,128)(2,1)S(1)} %fusion.3.refs_0_, bf16[112,576]{1,0:T(8,128)(2,1)S(1)} %collective-permute-done.12.refs_1_, ...), custom_call_target="tpu_custom_call" | custom-call | flops 1000 | bytes 1000 | tf_op jit(solution)/shard_map/combine/pallas_call | solution.py:280
  (4 shorter events, 0.1 us)
Async XLA Ops:
  0.6 8.4 %collective-permute-start.1 = (bf16[400,1152]{1,0:T(8,128)(2,1)}, bf16[400,1152]{1,0:T(8,128)(2,1)S(1)}, u32[]{:S(2)}, u32[]{:S(2)}) collective-permute-start(bf16[400,1152]{1,0:T(8,128)(2,1)} %bitcast.28), channel_id=1, source_target_pairs={{0,2},{2,0},{4,6},{6,4},{8,10},{10,8},{12,14},{14,12},{1,3},{3,1},... | collective-permute-start | bytes 2764808 | tf_op jit(solution)/shard_map/ppermute | solution.py:300
  3.3 5.7 %collective-permute-start = (bf16[112,1152]{1,0:T(8,128)(2,1)S(1)}, bf16[112,1152]{1,0:T(8,128)(2,1)S(1)}, u32[]{:S(2)}, u32[]{:S(2)}) collective-permute-start(bf16[112,1152]{1,0:T(8,128)(2,1)S(1)} %get-tuple-element.37.refs_0_), channel_id=1, source_target_pairs={{0,2},{2,0},{4,6},{6,4},{8,10},{10,8},{12,14},{14,12},{1,3},{3,1},... | collective-permute-start | bytes 774152 | tf_op jit(solution)/shard_map/ppermute | solution.py:300
  3.4 18.9 %collective-permute-start.3 = (bf16[112,1152]{1,0:T(8,128)(2,1)S(1)}, bf16[112,1152]{1,0:T(8,128)(2,1)S(1)}, u32[]{:S(2)}, u32[]{:S(2)}) collective-permute-start(bf16[112,1152]{1,0:T(8,128)(2,1)S(1)} %get-tuple-element.49), channel_id=1, source_target_pairs={{0,4},{2,6},{4,8},{6,10},{8,12},{10,14},{12,0},{14,2},{1,5},{3,7},... | collective-permute-start | bytes 774152 | tf_op jit(solution)/shard_map/ppermute | solution.py:310
  6.4 19.5 %collective-permute-start.2 = (bf16[112,1152]{1,0:T(8,128)(2,1)S(1)}, bf16[112,1152]{1,0:T(8,128)(2,1)S(1)}, u32[]{:S(2)}, u32[]{:S(2)}) collective-permute-start(bf16[112,1152]{1,0:T(8,128)(2,1)S(1)} %get-tuple-element.47), channel_id=1, source_target_pairs={{0,8},{2,10},{4,12},{6,14},{8,0},{10,2},{12,4},{14,6},{1,9},{3,11}... | collective-permute-start | bytes 774152 | tf_op jit(solution)/shard_map/ppermute | solution.py:310
  25.9 2.1 %collective-permute-start.4 = (bf16[2,112,576]{2,1,0:T(8,128)(2,1)S(1)}, bf16[2,112,576]{2,1,0:T(8,128)(2,1)S(1)}, u32[]{:S(2)}, u32[]{:S(2)}) collective-permute-start(bf16[2,112,576]{2,1,0:T(8,128)(2,1)S(1)} %get-tuple-element.51), channel_id=1, source_target_pairs={{0,2},{2,0},{4,6},{6,4},{8,10},{10,8},{12,14},{14,12},{1,3},{3,1},... | collective-permute-start | bytes 774152 | tf_op jit(solution)/shard_map/ppermute | solution.py:300
  26.0 10.1 %collective-permute-start.8 = (bf16[112,1152]{1,0:T(8,128)(2,1)S(1)}, bf16[112,1152]{1,0:T(8,128)(2,1)S(1)}, u32[]{:S(2)}, u32[]{:S(2)}) collective-permute-start(bf16[112,1152]{1,0:T(8,128)(2,1)S(1)} %get-tuple-element.59), channel_id=1, source_target_pairs={{0,12},{2,14},{4,0},{6,2},{8,4},{10,6},{12,8},{14,10},{1,13},{3,15... | collective-permute-start | bytes 774152 | tf_op jit(solution)/shard_map/ppermute | solution.py:310
  27.6 2.1 %collective-permute-start.7 = (bf16[112,1152]{1,0:T(8,128)(2,1)S(1)}, bf16[112,1152]{1,0:T(8,128)(2,1)S(1)}, u32[]{:S(2)}, u32[]{:S(2)}) collective-permute-start(bf16[112,1152]{1,0:T(8,128)(2,1)S(1)} %collective-permute-done.3.refs_1_), channel_id=1, source_target_pairs={{0,2},{2,0},{4,6},{6,4},{8,10},{10,8},{12,14},{14,12},{1,3},{3,1},... | collective-permute-start | bytes 774152 | tf_op jit(solution)/shard_map/ppermute | solution.py:300
  27.8 1.9 %collective-permute-start.6 = (bf16[112,1152]{1,0:T(8,128)(2,1)S(1)}, bf16[112,1152]{1,0:T(8,128)(2,1)S(1)}, u32[]{:S(2)}, u32[]{:S(2)}) collective-permute-start(bf16[112,1152]{1,0:T(8,128)(2,1)S(1)} %collective-permute-done.2.refs_0_), channel_id=1, source_target_pairs={{0,2},{2,0},{4,6},{6,4},{8,10},{10,8},{12,14},{14,12},{1,3},{3,1},... | collective-permute-start | bytes 774152 | tf_op jit(solution)/shard_map/ppermute | solution.py:300
  28.1 8.0 %collective-permute-start.5 = (bf16[112,576]{1,0:T(8,128)(2,1)S(1)}, bf16[112,576]{1,0:T(8,128)(2,1)S(1)}, u32[]{:S(2)}, u32[]{:S(2)}) collective-permute-start(bf16[112,576]{1,0:T(8,128)(2,1)S(1)} %fusion.4), channel_id=1, source_target_pairs={{0,1},{1,0},{2,3},{3,2},{4,5},{5,4},{6,7},{7,6},{8,9},{9,8},{10,11... | collective-permute-start | bytes 387080 | tf_op jit(solution)/shard_map/ppermute | solution.py:305
  36.1 2.0 %collective-permute-start.9 = (bf16[2,224,576]{2,1,0:T(8,128)(2,1)S(1)}, bf16[2,224,576]{2,1,0:T(8,128)(2,1)S(1)}, u32[]{:S(2)}, u32[]{:S(2)}) collective-permute-start(bf16[2,224,576]{2,1,0:T(8,128)(2,1)S(1)} %get-tuple-element.61), channel_id=1, source_target_pairs={{0,2},{2,0},{4,6},{6,4},{8,10},{10,8},{12,14},{14,12},{1,3},{3,1},... | collective-permute-start | bytes 1548296 | tf_op jit(solution)/shard_map/ppermute | solution.py:300
  36.2 3.4 %collective-permute-start.11 = (bf16[112,1152]{1,0:T(8,128)(2,1)S(1)}, bf16[112,1152]{1,0:T(8,128)(2,1)S(1)}, u32[]{:S(2)}, u32[]{:S(2)}) collective-permute-start(bf16[112,1152]{1,0:T(8,128)(2,1)S(1)} %collective-permute-done.8.refs_0_), channel_id=1, source_target_pairs={{0,2},{2,0},{4,6},{6,4},{8,10},{10,8},{12,14},{14,12},{1,3},{3,1},... | collective-permute-start | bytes 774152 | tf_op jit(solution)/shard_map/ppermute | solution.py:300
  38.3 8.9 %collective-permute-start.10 = (bf16[224,576]{1,0:T(8,128)(2,1)S(1)}, bf16[224,576]{1,0:T(8,128)(2,1)S(1)}, u32[]{:S(2)}, u32[]{:S(2)}) collective-permute-start(bf16[224,576]{1,0:T(8,128)(2,1)S(1)} %fusion.1), channel_id=1, source_target_pairs={{0,1},{1,0},{2,3},{3,2},{4,5},{5,4},{6,7},{7,6},{8,9},{9,8},{10,11... | collective-permute-start | bytes 774152 | tf_op jit(solution)/shard_map/ppermute | solution.py:305
  43.5 21.6 %copy-start = (s32[160,2]{0,1:T(2,128)S(1)}, s32[160,2]{0,1:T(2,128)}, u32[]{:S(2)}) copy-start(s32[160,2]{0,1:T(2,128)} %param.8) | copy-start | bytes 3844
  43.5 21.6 %copy-start.1 = (f32[160,2]{0,1:T(2,128)S(1)}, f32[160,2]{0,1:T(2,128)}, u32[]{:S(2)}) copy-start(f32[160,2]{0,1:T(2,128)} %param.9) | copy-start | bytes 3844
  47.3 1.6 %collective-permute-start.14 = (bf16[2,112,576]{2,1,0:T(8,128)(2,1)S(1)}, bf16[2,112,576]{2,1,0:T(8,128)(2,1)S(1)}, u32[]{:S(2)}, u32[]{:S(2)}) collective-permute-start(bf16[2,112,576]{2,1,0:T(8,128)(2,1)S(1)} %get-tuple-element.67), channel_id=1, source_target_pairs={{0,2},{2,0},{4,6},{6,4},{8,10},{10,8},{12,14},{14,12},{1,3},{3,1},... | collective-permute-start | bytes 774152 | tf_op jit(solution)/shard_map/ppermute | solution.py:300
  49.0 5.9 %collective-permute-start.15 = (bf16[112,576]{1,0:T(8,128)(2,1)S(1)}, bf16[112,576]{1,0:T(8,128)(2,1)S(1)}, u32[]{:S(2)}, u32[]{:S(2)}) collective-permute-start(bf16[112,576]{1,0:T(8,128)(2,1)S(1)} %fusion.5), channel_id=1, source_target_pairs={{0,1},{1,0},{2,3},{3,2},{4,5},{5,4},{6,7},{7,6},{8,9},{9,8},{10,11... | collective-permute-start | bytes 387080 | tf_op jit(solution)/shard_map/ppermute | solution.py:305
  50.5 6.3 %collective-permute-start.12 = (bf16[112,576]{1,0:T(8,128)(2,1)S(1)}, bf16[112,576]{1,0:T(8,128)(2,1)S(1)}, u32[]{:S(2)}, u32[]{:S(2)}) collective-permute-start(bf16[112,576]{1,0:T(8,128)(2,1)S(1)} %get-tuple-element.71), channel_id=1, source_target_pairs={{0,12},{2,14},{4,0},{6,2},{8,4},{10,6},{12,8},{14,10},{1,13},{3,15... | collective-permute-start | bytes 387080 | tf_op jit(solution)/shard_map/ppermute | solution.py:310
  52.6 12.5 %collective-permute-start.13 = (bf16[112,576]{1,0:T(8,128)(2,1)S(1)}, bf16[112,576]{1,0:T(8,128)(2,1)S(1)}, u32[]{:S(2)}, u32[]{:S(2)}) collective-permute-start(bf16[112,576]{1,0:T(8,128)(2,1)S(1)} %get-tuple-element.70), channel_id=1, source_target_pairs={{0,8},{2,10},{4,12},{6,14},{8,0},{10,2},{12,4},{14,6},{1,9},{3,11}... | collective-permute-start | bytes 387080 | tf_op jit(solution)/shard_map/ppermute | solution.py:310
  54.9 10.2 %collective-permute-start.16 = (bf16[112,576]{1,0:T(8,128)(2,1)S(1)}, bf16[112,576]{1,0:T(8,128)(2,1)S(1)}, u32[]{:S(2)}, u32[]{:S(2)}) collective-permute-start(bf16[112,576]{1,0:T(8,128)(2,1)S(1)} %fusion.2), channel_id=1, source_target_pairs={{0,4},{2,6},{4,8},{6,10},{8,12},{10,14},{12,0},{14,2},{1,5},{3,7},... | collective-permute-start | bytes 387080 | tf_op jit(solution)/shard_map/ppermute | solution.py:310

commit v3 on v2

--- a/solution.py
+++ b/solution.py
@@ -177,10 +177,11 @@
     )(meta, in_hbm(dispatched), other, *[in_hbm(w) for w in weights])
 
 
-def backward_kernel(counts, cap, first, meta, *refs):
+def backward_kernel(counts, cap, padded, first, meta, *refs):
     cots, refs = refs[: sum(counts)], refs[sum(counts) :]
-    act_ref, slope_ref, hid_ref, gate_ref, up_ref, down_ref, keep, give, cot_ref, gate_grad, up_grad = refs
-    padded = cots[0].shape[0]
+    act_ref, slope_ref, hid_ref, gate_ref, up_ref, down_ref, keep = refs[:7]
+    gives, (cot_ref, gate_grad, up_grad) = refs[7:-3], refs[-3:]
+    sent_rows = cots[0].shape[0]
     at = 0
     for n, parts in enumerate(counts):
         pieces = [ref[...] for ref in cots[at : at + parts]]
@@ -189,6 +190,9 @@
         for h in range(1, parts):
             turned = jnp.concatenate([pieces[(h - i) % parts] for i in range(parts)], axis=1)
             full = jnp.where(meta[2] == h, turned, full)
+        if padded > sent_rows:
+            empty = jnp.zeros((padded - sent_rows, full.shape[1]), full.dtype)
+            full = jnp.concatenate([full, empty], axis=0)
         cot_ref[pl.ds(n * padded, padded), :] = full
     rows = pl.ds(first, len(counts) * padded)
     cot = cot_ref[...]
@@ -199,13 +203,13 @@
         gate_grad[:, unit] = (d_hidden * slope_ref[rows, unit].astype(jnp.float32)).astype(jnp.bfloat16)
         up_grad[:, unit] = (d_hidden * act_ref[rows, unit].astype(jnp.float32)).astype(jnp.bfloat16)
     back = dot(gate_grad[...], gate_ref[...], NT) + dot(up_grad[...], up_ref[...], NT)
-    shares, kept, share = give.shape
-    row = lax.broadcasted_iota(jnp.int32, (padded, share), 0)
-    lane = lax.broadcasted_iota(jnp.int32, (padded, LANES), 1)
-    diagonal = lax.broadcasted_iota(jnp.int32, (padded, LANES), 0) == lane
+    shares, _, share = keep.shape
+    row = lax.broadcasted_iota(jnp.int32, (sent_rows, share), 0)
+    lane = lax.broadcasted_iota(jnp.int32, (sent_rows, LANES), 1)
+    diagonal = lax.broadcasted_iota(jnp.int32, (sent_rows, LANES), 0) == lane
+    blocks = [[] for _ in range(shares)]
     for n in range(len(counts)):
-        block = slice(n * padded, (n + 1) * padded)
-        out, start = (keep, n * padded) if n < len(counts) // 2 else (give, n * padded - kept)
+        block = slice(n * padded, n * padded + sent_rows)
         line = jnp.sum(jnp.where(diagonal, part[block], 0.0), axis=0, keepdims=True)
         line = jnp.concatenate([line, jnp.zeros((1, share - LANES), jnp.float32)], axis=1)
         pieces = [back[block, i * share : (i + 1) * share] for i in range(shares)]
@@ -214,24 +218,27 @@
             for i in range(shares):
                 if i != r:
                     piece = jnp.where(meta[2] == (i - r) % shares, pieces[i], piece)
-            piece = jnp.where(row < cap, piece, jnp.where(row == cap, line, 0.0))
-            out[r, pl.ds(start, padded), :] = piece.astype(out.dtype)
-
-
-def backward(meta, cots, tables, first, gate_mat, up_mat, down_mat, cap, shares):
-    padded = cots[0][0].shape[0]
+            blocks[r].append(jnp.where(row < cap, piece, jnp.where(row == cap, line, 0.0)))
+    half = len(counts) // 2
+    for r in range(shares):
+        keep[r] = jnp.concatenate(blocks[r][:half], axis=0)
+        gives[r][...] = jnp.concatenate(blocks[r][half:], axis=0).astype(jnp.bfloat16)
+
+
+def backward(meta, cots, tables, first, gate_mat, up_mat, down_mat, cap, padded, shares):
+    kept = len(cots) // 2 * cots[0][0].shape[0]
     width, units = gate_mat.shape
     rows = len(cots) * padded
     share = width // shares
     parts = [part for cot in cots for part in cot]
     return pl.pallas_call(
-        functools.partial(backward_kernel, [len(cot) for cot in cots], cap, first),
+        functools.partial(backward_kernel, [len(cot) for cot in cots], cap, padded, first),
         out_shape=[
-            jax.ShapeDtypeStruct((shares, rows // 2, share), jnp.float32),
-            jax.ShapeDtypeStruct((shares, rows // 2, share), jnp.bfloat16),
+            jax.ShapeDtypeStruct((shares, kept, share), jnp.float32),
+            *[jax.ShapeDtypeStruct((kept, share), jnp.bfloat16)] * shares,
         ],
         in_specs=[smem()] + [whole()] * (len(parts) + 6),
-        out_specs=[whole()] * 2,
+        out_specs=[whole()] * (1 + shares),
         scratch_shapes=[
             pltpu.VMEM((rows, width), jnp.bfloat16),
             pltpu.VMEM((rows, units), jnp.bfloat16),
@@ -243,11 +250,10 @@
     )(meta, *parts, *tables, gate_mat, up_mat, down_mat)
 
 
-def combine_kernel(peers, cap, meta, index_ref, gates_ref, *refs):
-    blocks = refs[:peers]
-    grad_ref, gate_out = refs[peers:]
-    rows = grad_ref.shape[0]
-    padded = blocks[0].shape[0]
+def combine_kernel(peers, cap, early, late, meta, index_ref, gates_ref, *refs):
+    blocks = refs[: len(early)]
+    sum_ref, product_ref, pick_ref, weight_ref = refs[len(early) :]
+    rows, padded = sum_ref.shape[0], pick_ref.shape[2]
     rel, named = named_rows(index_ref, meta[0], peers)
     slots = slot_rows(named)
     gates = gates_ref[...]
@@ -259,36 +265,69 @@
         return jnp.sum(jnp.where(diagonal, row, 0), axis=1, keepdims=True)
 
     place = lax.broadcasted_iota(jnp.int32, (rows, padded), 1)
-    total = jnp.zeros(grad_ref.shape, jnp.float32)
+    total = jnp.zeros(sum_ref.shape, jnp.float32)
     products = jnp.zeros(rel.shape, jnp.float32)
-    for d, block in enumerate(blocks):
+    for n, d in enumerate(early + late):
         chosen = rel == d
         weight = column(jnp.sum(jnp.where(chosen, gates, 0.0), axis=0, keepdims=True))
         pick = (place == column(slots[d : d + 1, :])).astype(jnp.bfloat16)
-        values = block[...]
-        total += weight * dot(pick, values)
+        if n < len(early):
+            values = blocks[n][...]
+            total += weight * dot(pick, values)
+            found = dot(values[cap:padded, :padded], pick, NT)
+            products += jnp.where(chosen, found[0:1, :], 0.0)
+        else:
+            pick_ref[n - len(early)] = pick
+            weight_ref[n - len(early)] = jnp.broadcast_to(weight, weight_ref.shape[1:])
+    sum_ref[...] = total
+    product_ref[...] = products
+
+
+def combine_late_kernel(peers, cap, late, meta, index_ref, sum_in, product_in, pick_ref, weight_ref, *refs):
+    blocks, (grad_ref, gate_out) = refs[: len(late)], refs[len(late) :]
+    rel = ring(index_ref[...] - meta[0], peers)
+    total = sum_in[...]
+    products = product_in[...]
+    for n, (d, block) in enumerate(zip(late, blocks)):
+        values, pick = block[...], pick_ref[n]
+        padded = values.shape[0]
+        total += weight_ref[n][:, 0:1] * dot(pick, values)
         found = dot(values[cap:padded, :padded], pick, NT)
-        products += jnp.where(chosen, found[0:1, :], 0.0)
+        products += jnp.where(rel == d, found[0:1, :], 0.0)
     grad_ref[...] = total.astype(jnp.bfloat16)
     gate_out[...] = products.astype(jnp.bfloat16)
 
 
-def combine(meta, index_rows, gate_rows, blocks, cap):
+def combine(meta, index_rows, gate_rows, returned, early, late, cap):
     count, rows = index_rows.shape
-    peers = len(blocks)
-    padded, share = blocks[0].shape
+    peers = len(early) + len(late)
+    padded, share = returned[0].shape
+    partial = pl.pallas_call(
+        functools.partial(combine_kernel, peers, cap, early, late),
+        out_shape=[
+            jax.ShapeDtypeStruct((rows, share), jnp.float32),
+            jax.ShapeDtypeStruct((count, rows), jnp.float32),
+            jax.ShapeDtypeStruct((len(late), rows, padded), jnp.bfloat16),
+            jax.ShapeDtypeStruct((len(late), rows, LANES), jnp.float32),
+        ],
+        in_specs=[smem()] + [whole()] * (2 + len(early)),
+        out_specs=[whole()] * 4,
+        compiler_params=params(),
+        cost_estimate=cost(),
+        name="combine",
+    )(meta, index_rows, gate_rows, *[returned[d] for d in early])
     return pl.pallas_call(
-        functools.partial(combine_kernel, peers, cap),
+        functools.partial(combine_late_kernel, peers, cap, late),
         out_shape=[
             jax.ShapeDtypeStruct((rows, share), jnp.bfloat16),
             jax.ShapeDtypeStruct((count, rows), jnp.bfloat16),
         ],
-        in_specs=[smem()] + [whole()] * (2 + peers),
+        in_specs=[smem()] + [whole()] * (5 + len(late)),
         out_specs=[whole()] * 2,
         compiler_params=params(),
         cost_estimate=cost(),
-        name="combine",
-    )(meta, index_rows, gate_rows, *blocks)
+        name="combine_late",
+    )(meta, index_rows, *partial, *[returned[d] for d in late])
 
 
 def after(value, others):
@@ -323,10 +362,11 @@
     meta = jnp.stack([index // 2, index % 2, lax.axis_index("hidden")]).astype(jnp.int32)
     half_rows = dispatched_inputs.shape[1]
     cap = half_rows // peers
-    padded = (cap // 16 + 1) * 16
+    sent_rows = (cap // 8 + 1) * 8
+    padded = -(-sent_rows // 16) * 16
     index_rows = expert_index.T
     other_rows = swap_pair(dispatched_inputs[0])
-    sent = route(meta, index_rows, out_grad, peers, padded, (), shares)
+    sent = route(meta, index_rows, out_grad, peers, sent_rows, (), shares)
     arrived = [shifted(block, d) if d else block for d, block in enumerate(sent)]
 
     groups = chunk_groups(peers)
@@ -345,14 +385,16 @@
             total = total + part.astype(jnp.float32)
         totals.append(total.astype(jnp.bfloat16))
         for m, d in enumerate(groups[n]):
-            block = totals[n][m * padded : (m + 1) * padded]
+            block = totals[n][m * sent_rows : (m + 1) * sent_rows]
             returned[d] = shifted(block, -d) if d else block
 
     for n, group in enumerate(groups):
         swapped = {d: swap_pair(ready[d]) for d in group}
         cots = [[ready[d]] for d in group] + [[swapped[d]] for d in group]
         cots = after(cots, ([c[2] for c in crossings], totals, gives))
-        keep, give = backward(meta, cots, tables, first, gate_mat, up_mat, down_mat, cap, shares)
+        keep, *give = backward(
+            meta, cots, tables, first, gate_mat, up_mat, down_mat, cap, padded, shares
+        )
         first += 2 * len(group) * padded
         gives.append(give)
         ready = {}
@@ -362,13 +404,16 @@
         if n:
             finish(n - 1, give)
             done.append(totals[-1])
-        got = swap_pair(after(give, done))
+        got = after([swap_pair(part) for part in give], done)
         pieces = [keep[r] + got[r].astype(jnp.float32) for r in range(shares)]
         crossing = [piece.astype(jnp.bfloat16) for piece in pieces[1:]]
         crossings.append((pieces[0], [hidden_ring(c, r + 1) for r, c in enumerate(crossing)], crossing))
     finish(len(groups) - 1, [])
-    blocks = [returned[d] for d in range(peers)]
-    input_grad, gate_grad = combine(meta, index_rows, gate_values.T, blocks, cap)
+    late = sorted({d for d in groups[1][:1] + groups[-1] if d})
+    early = [d for d in range(peers) if d not in late]
+    input_grad, gate_grad = combine(
+        meta, index_rows, gate_values.T, returned, early, late, cap
+    )
     return input_grad, gate_grad.T
 
 

time: 67.2 us -> 60.1 us (0.89)
  waiting for transfers between devices: 22.4 us -> 14.2 us
  Pallas kernels: 27.4 us -> 28.1 us
    ppermute x6, waiting for transfers between devices: 13.4 us -> 8.71 us  [shifted(): lax.ppermute(block, 'expert', [(i, (i + 2 * d) % count) for i in range(co...]
    ppermute x8 -> x11, waiting for transfers between devices: 3.04 us -> 1.15 us  [swap_pair(): return lax.ppermute(block, 'expert', [(i, i ^ 1) for i in range(count)])]
    ppermute x3, waiting for transfers between devices: 5.98 us -> 4.29 us  [hidden_ring(): lax.ppermute(block, 'hidden', [(i, (i + r) % count) for i in range(count)])]
    ppermute x8 -> x11, starting transfers between devices: 1.81 us -> 2.59 us  [swap_pair(): return lax.ppermute(block, 'expert', [(i, i ^ 1) for i in range(count)])]
    pallas_call x1 -> x2, Pallas kernels: 1.88 us -> 2.55 us  [the longest x1 1.5 us: combine(): pl.pallas_call(functools.partial(combine_late_kernel, peers, cap, late),...]
  transfers between devices with their start and end apart: 17 -> 20, of which waited for: 7 -> 7; matrix products, arithmetic and copies ran while one was open for 0% -> 1% of each run, Pallas kernels for 38% -> 44%
where the time goes in v3:
time: 60.1 us; the launch traced here: 60 us
  Pallas kernels  28.1 us (47%)
  starting transfers between devices  16.5 us (27%)
  waiting for transfers between devices  14.2 us (24%)
  between operations  0.77 us (1%)
    pallas_call x3, Pallas kernels, backward(): pl.pallas_call(functools.partial(backward_kernel, [len(cot) for cot in co...  14.2 us
    ppermute x6, starting transfers between devices, shifted(): lax.ppermute(block, 'expert', [(i, (i + 2 * d) % count) for i in range(co...  9.57 us
    pallas_call x1, Pallas kernels, forward(): pl.pallas_call(functools.partial(forward_kernel, peers, cap, padded, orde...  9.32 us
    ppermute x6, waiting for transfers between devices, shifted(): lax.ppermute(block, 'expert', [(i, (i + 2 * d) % count) for i in range(co...  8.71 us
    ppermute x3, starting transfers between devices, hidden_ring(): lax.ppermute(block, 'hidden', [(i, (i + r) % count) for i in range(count)])  4.35 us
    ppermute x3, waiting for transfers between devices, hidden_ring(): lax.ppermute(block, 'hidden', [(i, (i + r) % count) for i in range(count)])  4.29 us
    ppermute x11, starting transfers between devices, swap_pair(): return lax.ppermute(block, 'expert', [(i, i ^ 1) for i in range(count)])  2.59 us
    pallas_call x1, Pallas kernels, route(): pl.pallas_call(functools.partial(route_kernel, peers, padded, spread), ou...  2.02 us
  transfers between devices with their start and end apart: 20, of which 7 were waited for; matrix products, arithmetic and copies ran while one was open for 1% of the time, Pallas kernels for 44%

profile of v3, /device:TPU:0, one launch (start us, length us, event | category | flops | bytes accessed | tf_op | source)
XLA Modules:
  0.0 60.0 jit_solution(14373677139098169563)
XLA Ops:
  0.6 0.5 collective-permute-start.1
  1.1 0.1 pad_add_fusion.meta
  1.2 2.0 %route.1 = (bf16[104,1152]{1,0:T(8,128)(2,1)S(1)}, bf16[104,1152]{1,0:T(8,128)(2,1)S(1)}, bf16[104,1152]{1,0:T(8,128)(2,1)S(1)}, bf16[104,1152]{1,0:T(8,128)(2,1)S(1)}) custom-call(s32[3]{0:T(128)S(1)} %pad_add_fusion.meta, s32[2,160]{1,0:T(2,128)} %bitcast.37, bf16[160,1152]{1,0:T(8,128)(2,1)} %grad_hbm.1), custom_call_target="tpu_custom_call" | custom-call | flops 1000 | bytes 1000 | tf_op jit(solution)/shard_map/route/pallas_call | solution.py:90
  3.3 0.1 collective-permute-start
  3.4 3.0 %collective-permute-start.5 = (bf16[104,1152]{1,0:T(8,128)(2,1)S(1)}, bf16[104,1152]{1,0:T(8,128)(2,1)S(1)}, u32[]{:S(2)}, u32[]{:S(2)}) collective-permute-start(bf16[104,1152]{1,0:T(8,128)(2,1)S(1)} %get-tuple-element.60), channel_id=1, source_target_pairs={{0,4},{2,6},{4,8},{6,10},{8,12},{10,14},{12,0},{14,2},{1,5},{3,7},... | collective-permute-start | bytes 718856 | tf_op jit(solution)/shard_map/ppermute | solution.py:349
  6.4 2.6 %collective-permute-start.4 = (bf16[104,1152]{1,0:T(8,128)(2,1)S(1)}, bf16[104,1152]{1,0:T(8,128)(2,1)S(1)}, u32[]{:S(2)}, u32[]{:S(2)}) collective-permute-start(bf16[104,1152]{1,0:T(8,128)(2,1)S(1)} %get-tuple-element.58), channel_id=1, source_target_pairs={{0,8},{2,10},{4,12},{6,14},{8,0},{10,2},{12,4},{14,6},{1,9},{3,11}... | collective-permute-start | bytes 718856 | tf_op jit(solution)/shard_map/ppermute | solution.py:349
  9.0 9.3 %forward.1 = (bf16[896,1152]{1,0:T(8,128)(2,1)S(1)}, bf16[896,1152]{1,0:T(8,128)(2,1)S(1)}, bf16[896,1152]{1,0:T(8,128)(2,1)S(1)}, bf16[1152,1152]{1,0:T(8,128)(...) custom-call(s32[3]{0:T(128)S(1)} %pad_add_fusion.meta, bf16[1,400,1152]{2,1,0:T(8,128)(2,1)} %own_hbm.1, ...), custom_call_target="tpu_custom_call" | custom-call | flops 1000 | bytes 1000 | tf_op jit(solution)/shard_map/forward/pallas_call | solution.py:163
  18.3 3.9 %backward.3 = (f32[2,104,576]{2,1,0:T(8,128)S(1)}, bf16[104,576]{1,0:T(8,128)(2,1)S(1)}, bf16[104,576]{1,0:T(8,128)(2,1)S(1)}) custom-call(s32[3]{0:T(128)S(1)} %pad_add_fusion.meta, bf16[104,1152]{1,0:T(8,128)(2,1)S(1)} %get-tuple-element.47.refs_0_, bf16[104,1152]{1,0:T(8,128)(2,1)S(1)} %collective-permute-done.refs_1_, ...), custom_call_target="tpu_custom_call" | custom-call | flops 1000 | bytes 1000 | tf_op jit(solution)/shard_map/backward/pallas_call | solution.py:234
  22.2 0.1 collective-permute-start.2
  22.3 0.5 collective-permute-start.3
  22.8 1.4 %collective-permute-start.11 = (bf16[104,1152]{1,0:T(8,128)(2,1)S(1)}, bf16[104,1152]{1,0:T(8,128)(2,1)S(1)}, u32[]{:S(2)}, u32[]{:S(2)}) collective-permute-start(bf16[104,1152]{1,0:T(8,128)(2,1)S(1)} %get-tuple-element.72), channel_id=1, source_target_pairs={{0,12},{2,14},{4,0},{6,2},{8,4},{10,6},{12,8},{14,10},{1,13},{3,15... | collective-permute-start | bytes 718856 | tf_op jit(solution)/shard_map/ppermute | solution.py:349
  24.2 0.0 collective-permute-done.5.refs_1_
  24.2 0.0 collective-permute-start.8
  24.2 0.6 collective-permute-done.4.refs_0_
  24.8 0.0 collective-permute-start.7
  24.8 0.0 collective-permute-done.2
  24.8 1.6 %collective-permute-start.6 = (bf16[104,576]{1,0:T(8,128)(2,1)S(1)}, bf16[104,576]{1,0:T(8,128)(2,1)S(1)}, u32[]{:S(2)}, u32[]{:S(2)}) collective-permute-start(bf16[104,576]{1,0:T(8,128)(2,1)S(1)} %fusion.6), channel_id=1, source_target_pairs={{0,1},{1,0},{2,3},{3,2},{4,5},{5,4},{6,7},{7,6},{8,9},{9,8},{10,11... | collective-permute-start | bytes 359432 | tf_op jit(solution)/shard_map/ppermute | solution.py:344
  26.4 0.0 collective-permute-done.8.refs_3_
  26.4 0.0 collective-permute-done.7.refs_2_
  26.4 6.4 %backward.4 = (f32[2,208,576]{2,1,0:T(8,128)S(1)}, bf16[208,576]{1,0:T(8,128)(2,1)S(1)}, bf16[208,576]{1,0:T(8,128)(2,1)S(1)}) custom-call(s32[3]{0:T(128)S(1)} %pad_add_fusion.meta, bf16[104,1152]{1,0:T(8,128)(2,1)S(1)} %collective-permute-done.4.refs_0_, bf16[104,1152]{1,0:T(8,128)(2,1)S(1)} %collective-permute-done.5.refs_1_, ...), custom_call_target="tpu_custom_call" | custom-call | flops 1000 | bytes 1000 | tf_op jit(solution)/shard_map/backward/pallas_call | solution.py:234
  32.7 0.3 collective-permute-start.10
  33.0 0.3 collective-permute-start.9
  33.3 0.0 collective-permute-done.11.refs_0_
  33.3 0.0 collective-permute-done.6
  33.3 0.2 collective-permute-start.13
  33.5 0.1 fusion.8.refs_0_
  33.6 0.8 %collective-permute-done.10 = bf16[208,576]{1,0:T(8,128)(2,1)S(1)} collective-permute-done((bf16[208,576]{1,0:T(8,128)(2,1)S(1)}, bf16[208,576]{1,0:T(8,128)(2,1)S(1)}, u32[]{:S(2)}, u32[]{:S(2)}) %collective-permute-start.10) | collective-permute-done | bytes 239648 | tf_op jit(solution)/shard_map/ppermute | solution.py:339
  34.3 0.4 collective-permute-done.9
  34.7 0.1 fusion
  34.8 1.4 %collective-permute-start.12 = (bf16[208,576]{1,0:T(8,128)(2,1)S(1)}, bf16[208,576]{1,0:T(8,128)(2,1)S(1)}, u32[]{:S(2)}, u32[]{:S(2)}) collective-permute-start(bf16[208,576]{1,0:T(8,128)(2,1)S(1)} %fusion), channel_id=1, source_target_pairs={{0,1},{1,0},{2,3},{3,2},{4,5},{5,4},{6,7},{7,6},{8,9},{9,8},{10,11... | collective-permute-start | bytes 718856 | tf_op jit(solution)/shard_map/ppermute | solution.py:344
  36.2 0.0 collective-permute-done.13.refs_1_
  36.2 3.9 %backward.5 = (f32[2,104,576]{2,1,0:T(8,128)S(1)}, bf16[104,576]{1,0:T(8,128)(2,1)S(1)}, bf16[104,576]{1,0:T(8,128)(2,1)S(1)}) custom-call(s32[3]{0:T(128)S(1)} %pad_add_fusion.meta, bf16[104,1152]{1,0:T(8,128)(2,1)S(1)} %collective-permute-done.11.refs_0_, bf16[104,1152]{1,0:T(8,128)(2,1)S(1)} %collective-permute-done.13.refs_1_, ...), custom_call_target="tpu_custom_call" | custom-call | flops 1000 | bytes 1000 | tf_op jit(solution)/shard_map/backward/pallas_call | solution.py:234
  40.1 0.0 copy-start
  40.2 0.0 copy-start.1
  40.2 0.1 collective-permute-start.16
  40.2 0.5 collective-permute-start.17
  40.7 2.6 %collective-permute-done.12 = bf16[208,576]{1,0:T(8,128)(2,1)S(1)} collective-permute-done((bf16[208,576]{1,0:T(8,128)(2,1)S(1)}, bf16[208,576]{1,0:T(8,128)(2,1)S(1)}, u32[]{:S(2)}, u32[]{:S(2)}) %collective-permute-start.12) | collective-permute-done | bytes 239648 | tf_op jit(solution)/shard_map/ppermute | solution.py:344
  43.4 0.1 fusion.2
  43.5 1.4 %collective-permute-start.18 = (bf16[104,576]{1,0:T(8,128)(2,1)S(1)}, bf16[104,576]{1,0:T(8,128)(2,1)S(1)}, u32[]{:S(2)}, u32[]{:S(2)}) collective-permute-start(bf16[104,576]{1,0:T(8,128)(2,1)S(1)} %fusion.3), channel_id=1, source_target_pairs={{0,1},{1,0},{2,3},{3,2},{4,5},{5,4},{6,7},{7,6},{8,9},{9,8},{10,11... | collective-permute-start | bytes 359432 | tf_op jit(solution)/shard_map/ppermute | solution.py:344
  44.9 1.7 %collective-permute-start.14 = (bf16[104,576]{1,0:T(8,128)(2,1)S(1)}, bf16[104,576]{1,0:T(8,128)(2,1)S(1)}, u32[]{:S(2)}, u32[]{:S(2)}) collective-permute-start(bf16[104,576]{1,0:T(8,128)(2,1)S(1)} %get-tuple-element.91), channel_id=1, source_target_pairs={{0,12},{2,14},{4,0},{6,2},{8,4},{10,6},{12,8},{14,10},{1,13},{3,15... | collective-permute-start | bytes 359432 | tf_op jit(solution)/shard_map/ppermute | solution.py:349
  46.6 0.3 collective-permute-start.15
  46.9 1.7 %collective-permute-done.18 = bf16[104,576]{1,0:T(8,128)(2,1)S(1)} collective-permute-done((bf16[104,576]{1,0:T(8,128)(2,1)S(1)}, bf16[104,576]{1,0:T(8,128)(2,1)S(1)}, u32[]{:S(2)}, u32[]{:S(2)}) %collective-permute-start.18) | collective-permute-done | bytes 119840 | tf_op jit(solution)/shard_map/ppermute | solution.py:344
  48.6 0.1 fusion.5
  48.7 0.6 collective-permute-start.19
  49.2 1.4 %collective-permute-done.14.refs_1_ = bf16[104,576]{1,0:T(8,128)(2,1)S(1)} collective-permute-done((bf16[104,576]{1,0:T(8,128)(2,1)S(1)}, bf16[104,576]{1,0:T(8,128)(2,1)S(1)}, u32[]{:S(2)}, u32[]{:S(2)}) %collective-permute-start.14) | collective-permute-done | bytes 119840 | tf_op jit(solution)/shard_map/ppermute | solution.py:349
  50.6 1.1 %combine.1 = (f32[160,576]{1,0:T(8,128)S(1)}, f32[2,160]{1,0:T(2,128)S(1)}, bf16[2,160,104]{2,1,0:T(8,128)(2,1)S(1)}, f32[2,160,128]{2,1,0:T(8,128)S(1)}) custom-call(s32[3]{0:T(128)S(1)} %pad_add_fusion.meta, s32[2,160]{1,0:T(2,128)S(1)} %bitcast.38, f32[2,160]{1,0:T(2,128)S(1)} %bitcast.40, bf16[104,576]{1,0:T(8,128)(2,1)S(1)} %fusion.8.refs_0_, ...), custom_call_target="tpu_custom_call" | custom-call | flops 1000 | bytes 1000 | tf_op jit(solution)/shard_map/combine/pallas_call | solution.py:305
  51.7 6.8 %collective-permute-done.15.refs_0_ = bf16[104,576]{1,0:T(8,128)(2,1)S(1)} collective-permute-done((bf16[104,576]{1,0:T(8,128)(2,1)S(1)}, bf16[104,576]{1,0:T(8,128)(2,1)S(1)}, u32[]{:S(2)}, u32[]{:S(2)}) %collective-permute-start.15) | collective-permute-done | bytes 119840 | tf_op jit(solution)/shard_map/ppermute | solution.py:349
  58.5 1.5 %combine_late.1 = (bf16[160,576]{1,0:T(8,128)(2,1)}, bf16[2,160]{1,0:T(2,128)(2,1)}) custom-call(s32[3]{0:T(128)S(1)} %pad_add_fusion.meta, s32[2,160]{1,0:T(2,128)S(1)} %bitcast.39, f32[160,576]{1,0:T(8,128)S(1)} %get-tuple-element.81.sum_in, f32[2,160]{1,0:T(2,128)S(1)} %get-tuple-element.82.product_in, ...), custom_call_target="tpu_custom_call" | custom-call | flops 1000 | bytes 1000 | tf_op jit(solution)/shard_map/combine_late/pallas_call | solution.py:319
  (11 shorter events, 0.1 us)
Async XLA Ops:
  0.6 8.4 %collective-permute-start.1 = (bf16[400,1152]{1,0:T(8,128)(2,1)}, bf16[400,1152]{1,0:T(8,128)(2,1)S(1)}, u32[]{:S(2)}, u32[]{:S(2)}) collective-permute-start(bf16[400,1152]{1,0:T(8,128)(2,1)} %bitcast.41), channel_id=1, source_target_pairs={{0,2},{2,0},{4,6},{6,4},{8,10},{10,8},{12,14},{14,12},{1,3},{3,1},... | collective-permute-start | bytes 2764808 | tf_op jit(solution)/shard_map/ppermute | solution.py:339
  3.3 5.7 %collective-permute-start = (bf16[104,1152]{1,0:T(8,128)(2,1)S(1)}, bf16[104,1152]{1,0:T(8,128)(2,1)S(1)}, u32[]{:S(2)}, u32[]{:S(2)}) collective-permute-start(bf16[104,1152]{1,0:T(8,128)(2,1)S(1)} %get-tuple-element.47.refs_0_), channel_id=1, source_target_pairs={{0,2},{2,0},{4,6},{6,4},{8,10},{10,8},{12,14},{14,12},{1,3},{3,1},... | collective-permute-start | bytes 718856 | tf_op jit(solution)/shard_map/ppermute | solution.py:339
  3.4 20.8 %collective-permute-start.5 = (bf16[104,1152]{1,0:T(8,128)(2,1)S(1)}, bf16[104,1152]{1,0:T(8,128)(2,1)S(1)}, u32[]{:S(2)}, u32[]{:S(2)}) collective-permute-start(bf16[104,1152]{1,0:T(8,128)(2,1)S(1)} %get-tuple-element.60), channel_id=1, source_target_pairs={{0,4},{2,6},{4,8},{6,10},{8,12},{10,14},{12,0},{14,2},{1,5},{3,7},... | collective-permute-start | bytes 718856 | tf_op jit(solution)/shard_map/ppermute | solution.py:349
  6.4 18.3 %collective-permute-start.4 = (bf16[104,1152]{1,0:T(8,128)(2,1)S(1)}, bf16[104,1152]{1,0:T(8,128)(2,1)S(1)}, u32[]{:S(2)}, u32[]{:S(2)}) collective-permute-start(bf16[104,1152]{1,0:T(8,128)(2,1)S(1)} %get-tuple-element.58), channel_id=1, source_target_pairs={{0,8},{2,10},{4,12},{6,14},{8,0},{10,2},{12,4},{14,6},{1,9},{3,11}... | collective-permute-start | bytes 718856 | tf_op jit(solution)/shard_map/ppermute | solution.py:349
  22.2 2.5 %collective-permute-start.2 = (bf16[104,576]{1,0:T(8,128)(2,1)S(1)}, bf16[104,576]{1,0:T(8,128)(2,1)S(1)}, u32[]{:S(2)}, u32[]{:S(2)}) collective-permute-start(bf16[104,576]{1,0:T(8,128)(2,1)S(1)} %get-tuple-element.56), channel_id=1, source_target_pairs={{0,2},{2,0},{4,6},{6,4},{8,10},{10,8},{12,14},{14,12},{1,3},{3,1},... | collective-permute-start | bytes 359432 | tf_op jit(solution)/shard_map/ppermute | solution.py:339
  22.3 2.5 %collective-permute-start.3 = (bf16[104,576]{1,0:T(8,128)(2,1)S(1)}, bf16[104,576]{1,0:T(8,128)(2,1)S(1)}, u32[]{:S(2)}, u32[]{:S(2)}) collective-permute-start(bf16[104,576]{1,0:T(8,128)(2,1)S(1)} %get-tuple-element.57), channel_id=1, source_target_pairs={{0,2},{2,0},{4,6},{6,4},{8,10},{10,8},{12,14},{14,12},{1,3},{3,1},... | collective-permute-start | bytes 359432 | tf_op jit(solution)/shard_map/ppermute | solution.py:339
  22.8 10.5 %collective-permute-start.11 = (bf16[104,1152]{1,0:T(8,128)(2,1)S(1)}, bf16[104,1152]{1,0:T(8,128)(2,1)S(1)}, u32[]{:S(2)}, u32[]{:S(2)}) collective-permute-start(bf16[104,1152]{1,0:T(8,128)(2,1)S(1)} %get-tuple-element.72), channel_id=1, source_target_pairs={{0,12},{2,14},{4,0},{6,2},{8,4},{10,6},{12,8},{14,10},{1,13},{3,15... | collective-permute-start | bytes 718856 | tf_op jit(solution)/shard_map/ppermute | solution.py:349
  24.2 2.2 %collective-permute-start.8 = (bf16[104,1152]{1,0:T(8,128)(2,1)S(1)}, bf16[104,1152]{1,0:T(8,128)(2,1)S(1)}, u32[]{:S(2)}, u32[]{:S(2)}) collective-permute-start(bf16[104,1152]{1,0:T(8,128)(2,1)S(1)} %collective-permute-done.5.refs_1_), channel_id=1, source_target_pairs={{0,2},{2,0},{4,6},{6,4},{8,10},{10,8},{12,14},{14,12},{1,3},{3,1},... | collective-permute-start | bytes 718856 | tf_op jit(solution)/shard_map/ppermute | solution.py:339
  24.8 1.6 %collective-permute-start.7 = (bf16[104,1152]{1,0:T(8,128)(2,1)S(1)}, bf16[104,1152]{1,0:T(8,128)(2,1)S(1)}, u32[]{:S(2)}, u32[]{:S(2)}) collective-permute-start(bf16[104,1152]{1,0:T(8,128)(2,1)S(1)} %collective-permute-done.4.refs_0_), channel_id=1, source_target_pairs={{0,2},{2,0},{4,6},{6,4},{8,10},{10,8},{12,14},{14,12},{1,3},{3,1},... | collective-permute-start | bytes 718856 | tf_op jit(solution)/shard_map/ppermute | solution.py:339
  24.8 8.5 %collective-permute-start.6 = (bf16[104,576]{1,0:T(8,128)(2,1)S(1)}, bf16[104,576]{1,0:T(8,128)(2,1)S(1)}, u32[]{:S(2)}, u32[]{:S(2)}) collective-permute-start(bf16[104,576]{1,0:T(8,128)(2,1)S(1)} %fusion.6), channel_id=1, source_target_pairs={{0,1},{1,0},{2,3},{3,2},{4,5},{5,4},{6,7},{7,6},{8,9},{9,8},{10,11... | collective-permute-start | bytes 359432 | tf_op jit(solution)/shard_map/ppermute | solution.py:344
  32.7 1.6 %collective-permute-start.10 = (bf16[208,576]{1,0:T(8,128)(2,1)S(1)}, bf16[208,576]{1,0:T(8,128)(2,1)S(1)}, u32[]{:S(2)}, u32[]{:S(2)}) collective-permute-start(bf16[208,576]{1,0:T(8,128)(2,1)S(1)} %get-tuple-element.69), channel_id=1, source_target_pairs={{0,2},{2,0},{4,6},{6,4},{8,10},{10,8},{12,14},{14,12},{1,3},{3,1},... | collective-permute-start | bytes 718856 | tf_op jit(solution)/shard_map/ppermute | solution.py:339
  33.0 1.7 %collective-permute-start.9 = (bf16[208,576]{1,0:T(8,128)(2,1)S(1)}, bf16[208,576]{1,0:T(8,128)(2,1)S(1)}, u32[]{:S(2)}, u32[]{:S(2)}) collective-permute-start(bf16[208,576]{1,0:T(8,128)(2,1)S(1)} %get-tuple-element.68), channel_id=1, source_target_pairs={{0,2},{2,0},{4,6},{6,4},{8,10},{10,8},{12,14},{14,12},{1,3},{3,1},... | collective-permute-start | bytes 718856 | tf_op jit(solution)/shard_map/ppermute | solution.py:339
  33.3 2.9 %collective-permute-start.13 = (bf16[104,1152]{1,0:T(8,128)(2,1)S(1)}, bf16[104,1152]{1,0:T(8,128)(2,1)S(1)}, u32[]{:S(2)}, u32[]{:S(2)}) collective-permute-start(bf16[104,1152]{1,0:T(8,128)(2,1)S(1)} %collective-permute-done.11.refs_0_), channel_id=1, source_target_pairs={{0,2},{2,0},{4,6},{6,4},{8,10},{10,8},{12,14},{14,12},{1,3},{3,1},... | collective-permute-start | bytes 718856 | tf_op jit(solution)/shard_map/ppermute | solution.py:339
  34.8 8.6 %collective-permute-start.12 = (bf16[208,576]{1,0:T(8,128)(2,1)S(1)}, bf16[208,576]{1,0:T(8,128)(2,1)S(1)}, u32[]{:S(2)}, u32[]{:S(2)}) collective-permute-start(bf16[208,576]{1,0:T(8,128)(2,1)S(1)} %fusion), channel_id=1, source_target_pairs={{0,1},{1,0},{2,3},{3,2},{4,5},{5,4},{6,7},{7,6},{8,9},{9,8},{10,11... | collective-permute-start | bytes 718856 | tf_op jit(solution)/shard_map/ppermute | solution.py:344
  40.1 10.5 %copy-start = (s32[160,2]{0,1:T(2,128)S(1)}, s32[160,2]{0,1:T(2,128)}, u32[]{:S(2)}) copy-start(s32[160,2]{0,1:T(2,128)} %param.8) | copy-start | bytes 3844
  40.2 10.5 %copy-start.1 = (f32[160,2]{0,1:T(2,128)S(1)}, f32[160,2]{0,1:T(2,128)}, u32[]{:S(2)}) copy-start(f32[160,2]{0,1:T(2,128)} %param.9) | copy-start | bytes 3844
  40.2 3.3 %collective-permute-start.16 = (bf16[104,576]{1,0:T(8,128)(2,1)S(1)}, bf16[104,576]{1,0:T(8,128)(2,1)S(1)}, u32[]{:S(2)}, u32[]{:S(2)}) collective-permute-start(bf16[104,576]{1,0:T(8,128)(2,1)S(1)} %get-tuple-element.78), channel_id=1, source_target_pairs={{0,2},{2,0},{4,6},{6,4},{8,10},{10,8},{12,14},{14,12},{1,3},{3,1},... | collective-permute-start | bytes 359432 | tf_op jit(solution)/shard_map/ppermute | solution.py:339
  40.2 3.3 %collective-permute-start.17 = (bf16[104,576]{1,0:T(8,128)(2,1)S(1)}, bf16[104,576]{1,0:T(8,128)(2,1)S(1)}, u32[]{:S(2)}, u32[]{:S(2)}) collective-permute-start(bf16[104,576]{1,0:T(8,128)(2,1)S(1)} %get-tuple-element.79), channel_id=1, source_target_pairs={{0,2},{2,0},{4,6},{6,4},{8,10},{10,8},{12,14},{14,12},{1,3},{3,1},... | collective-permute-start | bytes 359432 | tf_op jit(solution)/shard_map/ppermute | solution.py:339
  43.5 5.1 %collective-permute-start.18 = (bf16[104,576]{1,0:T(8,128)(2,1)S(1)}, bf16[104,576]{1,0:T(8,128)(2,1)S(1)}, u32[]{:S(2)}, u32[]{:S(2)}) collective-permute-start(bf16[104,576]{1,0:T(8,128)(2,1)S(1)} %fusion.3), channel_id=1, source_target_pairs={{0,1},{1,0},{2,3},{3,2},{4,5},{5,4},{6,7},{7,6},{8,9},{9,8},{10,11... | collective-permute-start | bytes 359432 | tf_op jit(solution)/shard_map/ppermute | solution.py:344
  44.9 5.7 %collective-permute-start.14 = (bf16[104,576]{1,0:T(8,128)(2,1)S(1)}, bf16[104,576]{1,0:T(8,128)(2,1)S(1)}, u32[]{:S(2)}, u32[]{:S(2)}) collective-permute-start(bf16[104,576]{1,0:T(8,128)(2,1)S(1)} %get-tuple-element.91), channel_id=1, source_target_pairs={{0,12},{2,14},{4,0},{6,2},{8,4},{10,6},{12,8},{14,10},{1,13},{3,15... | collective-permute-start | bytes 359432 | tf_op jit(solution)/shard_map/ppermute | solution.py:349
  46.6 11.8 %collective-permute-start.15 = (bf16[104,576]{1,0:T(8,128)(2,1)S(1)}, bf16[104,576]{1,0:T(8,128)(2,1)S(1)}, u32[]{:S(2)}, u32[]{:S(2)}) collective-permute-start(bf16[104,576]{1,0:T(8,128)(2,1)S(1)} %get-tuple-element.90), channel_id=1, source_target_pairs={{0,8},{2,10},{4,12},{6,14},{8,0},{10,2},{12,4},{14,6},{1,9},{3,11}... | collective-permute-start | bytes 359432 | tf_op jit(solution)/shard_map/ppermute | solution.py:349
  48.7 9.8 %collective-permute-start.19 = (bf16[104,576]{1,0:T(8,128)(2,1)S(1)}, bf16[104,576]{1,0:T(8,128)(2,1)S(1)}, u32[]{:S(2)}, u32[]{:S(2)}) collective-permute-start(bf16[104,576]{1,0:T(8,128)(2,1)S(1)} %fusion.5), channel_id=1, source_target_pairs={{0,4},{2,6},{4,8},{6,10},{8,12},{10,14},{12,0},{14,2},{1,5},{3,7},... | collective-permute-start | bytes 359432 | tf_op jit(solution)/shard_map/ppermute | solution.py:349

commit v4 on v3

--- a/solution.py
+++ b/solution.py
@@ -252,7 +252,7 @@
 
 def combine_kernel(peers, cap, early, late, meta, index_ref, gates_ref, *refs):
     blocks = refs[: len(early)]
-    sum_ref, product_ref, pick_ref, weight_ref = refs[len(early) :]
+    sum_ref, product_ref, pick_ref, weight_ref, chosen_ref = refs[len(early) :]
     rows, padded = sum_ref.shape[0], pick_ref.shape[2]
     rel, named = named_rows(index_ref, meta[0], peers)
     slots = slot_rows(named)
@@ -279,21 +279,21 @@
         else:
             pick_ref[n - len(early)] = pick
             weight_ref[n - len(early)] = jnp.broadcast_to(weight, weight_ref.shape[1:])
+            chosen_ref[n - len(early)] = chosen.astype(jnp.float32)
     sum_ref[...] = total
     product_ref[...] = products
 
 
-def combine_late_kernel(peers, cap, late, meta, index_ref, sum_in, product_in, pick_ref, weight_ref, *refs):
-    blocks, (grad_ref, gate_out) = refs[: len(late)], refs[len(late) :]
-    rel = ring(index_ref[...] - meta[0], peers)
+def combine_late_kernel(cap, sum_in, product_in, pick_ref, weight_ref, chosen_ref, *refs):
+    blocks, (grad_ref, gate_out) = refs[:-2], refs[-2:]
     total = sum_in[...]
     products = product_in[...]
-    for n, (d, block) in enumerate(zip(late, blocks)):
+    for n, block in enumerate(blocks):
         values, pick = block[...], pick_ref[n]
         padded = values.shape[0]
         total += weight_ref[n][:, 0:1] * dot(pick, values)
         found = dot(values[cap:padded, :padded], pick, NT)
-        products += jnp.where(rel == d, found[0:1, :], 0.0)
+        products += jnp.where(chosen_ref[n] > 0.5, found[0:1, :], 0.0)
     grad_ref[...] = total.astype(jnp.bfloat16)
     gate_out[...] = products.astype(jnp.bfloat16)
 
@@ -309,25 +309,26 @@
             jax.ShapeDtypeStruct((count, rows), jnp.float32),
             jax.ShapeDtypeStruct((len(late), rows, padded), jnp.bfloat16),
             jax.ShapeDtypeStruct((len(late), rows, LANES), jnp.float32),
+            jax.ShapeDtypeStruct((len(late), count, rows), jnp.float32),
         ],
         in_specs=[smem()] + [whole()] * (2 + len(early)),
-        out_specs=[whole()] * 4,
+        out_specs=[whole()] * 5,
         compiler_params=params(),
         cost_estimate=cost(),
         name="combine",
     )(meta, index_rows, gate_rows, *[returned[d] for d in early])
     return pl.pallas_call(
-        functools.partial(combine_late_kernel, peers, cap, late),
+        functools.partial(combine_late_kernel, cap),
         out_shape=[
             jax.ShapeDtypeStruct((rows, share), jnp.bfloat16),
             jax.ShapeDtypeStruct((count, rows), jnp.bfloat16),
         ],
-        in_specs=[smem()] + [whole()] * (5 + len(late)),
+        in_specs=[whole()] * (5 + len(late)),
         out_specs=[whole()] * 2,
         compiler_params=params(),
         cost_estimate=cost(),
         name="combine_late",
-    )(meta, index_rows, *partial, *[returned[d] for d in late])
+    )(*partial, *[returned[d] for d in late])
 
 
 def after(value, others):
@@ -399,7 +400,7 @@
         gives.append(give)
         ready = {}
         for d in groups[n + 1] if n + 1 < len(groups) else []:
-            ready[d] = after(arrived[d], give)
+            ready[d] = after(arrived[d], (give, list(ready.values())))
         done = list(ready.values())
         if n:
             finish(n - 1, give)

time: 60.1 us -> 59.4 us (0.988)
    ppermute x6, waiting for transfers between devices: 8.71 us -> 7.79 us  [shifted(): lax.ppermute(block, 'expert', [(i, (i + 2 * d) % count) for i in range(co...]
    ppermute x3, waiting for transfers between devices: 4.29 us -> 5.1 us  [hidden_ring(): lax.ppermute(block, 'hidden', [(i, (i + r) % count) for i in range(count)])]
  transfers between devices with their start and end apart: 20 -> 20, of which waited for: 7 -> 6; matrix products, arithmetic and copies ran while one was open for 1% -> 1% of each run, Pallas kernels for 44% -> 45%
where the time goes in v4:
time: 59.4 us; the launch traced here: 59.3 us
  Pallas kernels  27.5 us (46%)
  starting transfers between devices  16.3 us (27%)
  waiting for transfers between devices  14.2 us (24%)
  between operations  0.79 us (1%)
    pallas_call x3, Pallas kernels, backward(): pl.pallas_call(functools.partial(backward_kernel, [len(cot) for cot in co...  14.2 us
    pallas_call x1, Pallas kernels, forward(): pl.pallas_call(functools.partial(forward_kernel, peers, cap, padded, orde...  9.32 us
    ppermute x6, starting transfers between devices, shifted(): lax.ppermute(block, 'expert', [(i, (i + 2 * d) % count) for i in range(co...  9.22 us
    ppermute x6, waiting for transfers between devices, shifted(): lax.ppermute(block, 'expert', [(i, (i + 2 * d) % count) for i in range(co...  7.79 us
    ppermute x3, waiting for transfers between devices, hidden_ring(): lax.ppermute(block, 'hidden', [(i, (i + r) % count) for i in range(count)])  5.1 us
    ppermute x3, starting transfers between devices, hidden_ring(): lax.ppermute(block, 'hidden', [(i, (i + r) % count) for i in range(count)])  4.16 us
    ppermute x11, starting transfers between devices, swap_pair(): return lax.ppermute(block, 'expert', [(i, i ^ 1) for i in range(count)])  2.94 us
    pallas_call x1, Pallas kernels, route(): pl.pallas_call(functools.partial(route_kernel, peers, padded, spread), ou...  2.02 us
  transfers between devices with their start and end apart: 20, of which 6 were waited for; matrix products, arithmetic and copies ran while one was open for 1% of the time, Pallas kernels for 45%

profile of v4, /device:TPU:0, one launch (start us, length us, event | category | flops | bytes accessed | tf_op | source)
XLA Modules:
  0.0 59.3 jit_solution(13993031598464971781)
XLA Ops:
  0.6 0.5 collective-permute-start.1
  1.1 0.1 pad_add_fusion.meta
  1.2 2.0 %route.1 = (bf16[104,1152]{1,0:T(8,128)(2,1)S(1)}, bf16[104,1152]{1,0:T(8,128)(2,1)S(1)}, bf16[104,1152]{1,0:T(8,128)(2,1)S(1)}, bf16[104,1152]{1,0:T(8,128)(2,1)S(1)}) custom-call(s32[3]{0:T(128)S(1)} %pad_add_fusion.meta, s32[2,160]{1,0:T(2,128)} %bitcast.37, bf16[160,1152]{1,0:T(8,128)(2,1)} %grad_hbm.1), custom_call_target="tpu_custom_call" | custom-call | flops 1000 | bytes 1000 | tf_op jit(solution)/shard_map/route/pallas_call | solution.py:90
  3.3 0.1 collective-permute-start
  3.4 4.0 %collective-permute-start.4 = (bf16[104,1152]{1,0:T(8,128)(2,1)S(1)}, bf16[104,1152]{1,0:T(8,128)(2,1)S(1)}, u32[]{:S(2)}, u32[]{:S(2)}) collective-permute-start(bf16[104,1152]{1,0:T(8,128)(2,1)S(1)} %get-tuple-element.59), channel_id=1, source_target_pairs={{0,8},{2,10},{4,12},{6,14},{8,0},{10,2},{12,4},{14,6},{1,9},{3,11}... | collective-permute-start | bytes 718856 | tf_op jit(solution)/shard_map/ppermute | solution.py:350
  7.4 1.6 %collective-permute-start.5 = (bf16[104,1152]{1,0:T(8,128)(2,1)S(1)}, bf16[104,1152]{1,0:T(8,128)(2,1)S(1)}, u32[]{:S(2)}, u32[]{:S(2)}) collective-permute-start(bf16[104,1152]{1,0:T(8,128)(2,1)S(1)} %get-tuple-element.61), channel_id=1, source_target_pairs={{0,4},{2,6},{4,8},{6,10},{8,12},{10,14},{12,0},{14,2},{1,5},{3,7},... | collective-permute-start | bytes 718856 | tf_op jit(solution)/shard_map/ppermute | solution.py:350
  9.0 9.3 %forward.1 = (bf16[896,1152]{1,0:T(8,128)(2,1)S(1)}, bf16[896,1152]{1,0:T(8,128)(2,1)S(1)}, bf16[896,1152]{1,0:T(8,128)(2,1)S(1)}, bf16[1152,1152]{1,0:T(8,128)(...) custom-call(s32[3]{0:T(128)S(1)} %pad_add_fusion.meta, bf16[1,400,1152]{2,1,0:T(8,128)(2,1)} %own_hbm.1, ...), custom_call_target="tpu_custom_call" | custom-call | flops 1000 | bytes 1000 | tf_op jit(solution)/shard_map/forward/pallas_call | solution.py:163
  18.3 3.9 %backward.3 = (f32[2,104,576]{2,1,0:T(8,128)S(1)}, bf16[104,576]{1,0:T(8,128)(2,1)S(1)}, bf16[104,576]{1,0:T(8,128)(2,1)S(1)}) custom-call(s32[3]{0:T(128)S(1)} %pad_add_fusion.meta, bf16[104,1152]{1,0:T(8,128)(2,1)S(1)} %get-tuple-element.48.refs_0_, bf16[104,1152]{1,0:T(8,128)(2,1)S(1)} %collective-permute-done.refs_1_, ...), custom_call_target="tpu_custom_call" | custom-call | flops 1000 | bytes 1000 | tf_op jit(solution)/shard_map/backward/pallas_call | solution.py:234
  22.2 0.1 collective-permute-start.2
  22.3 0.5 collective-permute-start.3
  22.8 2.2 %collective-permute-start.11 = (bf16[104,1152]{1,0:T(8,128)(2,1)S(1)}, bf16[104,1152]{1,0:T(8,128)(2,1)S(1)}, u32[]{:S(2)}, u32[]{:S(2)}) collective-permute-start(bf16[104,1152]{1,0:T(8,128)(2,1)S(1)} %get-tuple-element.73), channel_id=1, source_target_pairs={{0,12},{2,14},{4,0},{6,2},{8,4},{10,6},{12,8},{14,10},{1,13},{3,15... | collective-permute-start | bytes 718856 | tf_op jit(solution)/shard_map/ppermute | solution.py:350
  25.1 0.0 collective-permute-done.4.refs_0_
  25.1 0.0 collective-permute-start.7
  25.1 0.0 collective-permute-done.5.refs_1_
  25.1 0.5 collective-permute-start.8
  25.6 0.0 collective-permute-done.2
  25.6 0.0 collective-permute-done.3
  25.6 1.6 %collective-permute-start.6 = (bf16[104,576]{1,0:T(8,128)(2,1)S(1)}, bf16[104,576]{1,0:T(8,128)(2,1)S(1)}, u32[]{:S(2)}, u32[]{:S(2)}) collective-permute-start(bf16[104,576]{1,0:T(8,128)(2,1)S(1)} %fusion.6), channel_id=1, source_target_pairs={{0,1},{1,0},{2,3},{3,2},{4,5},{5,4},{6,7},{7,6},{8,9},{9,8},{10,11... | collective-permute-start | bytes 359432 | tf_op jit(solution)/shard_map/ppermute | solution.py:345
  27.2 0.0 collective-permute-done.8.refs_3_
  27.2 0.0 collective-permute-done.7.refs_2_
  27.2 6.4 %backward.4 = (f32[2,208,576]{2,1,0:T(8,128)S(1)}, bf16[208,576]{1,0:T(8,128)(2,1)S(1)}, bf16[208,576]{1,0:T(8,128)(2,1)S(1)}) custom-call(s32[3]{0:T(128)S(1)} %pad_add_fusion.meta, bf16[104,1152]{1,0:T(8,128)(2,1)S(1)} %collective-permute-done.4.refs_0_, bf16[104,1152]{1,0:T(8,128)(2,1)S(1)} %collective-permute-done.5.refs_1_, ...), custom_call_target="tpu_custom_call" | custom-call | flops 1000 | bytes 1000 | tf_op jit(solution)/shard_map/backward/pallas_call | solution.py:234
  33.6 0.1 collective-permute-start.10
  33.6 0.5 collective-permute-start.9
  34.1 0.1 collective-permute-start.13
  34.2 0.1 fusion.8.refs_0_
  34.3 0.9 %collective-permute-done.10 = bf16[208,576]{1,0:T(8,128)(2,1)S(1)} collective-permute-done((bf16[208,576]{1,0:T(8,128)(2,1)S(1)}, bf16[208,576]{1,0:T(8,128)(2,1)S(1)}, u32[]{:S(2)}, u32[]{:S(2)}) %collective-permute-start.10) | collective-permute-done | bytes 239648 | tf_op jit(solution)/shard_map/ppermute | solution.py:340
  35.2 0.4 collective-permute-done.9
  35.5 0.1 fusion
  35.6 1.3 %collective-permute-start.12 = (bf16[208,576]{1,0:T(8,128)(2,1)S(1)}, bf16[208,576]{1,0:T(8,128)(2,1)S(1)}, u32[]{:S(2)}, u32[]{:S(2)}) collective-permute-start(bf16[208,576]{1,0:T(8,128)(2,1)S(1)} %fusion), channel_id=1, source_target_pairs={{0,1},{1,0},{2,3},{3,2},{4,5},{5,4},{6,7},{7,6},{8,9},{9,8},{10,11... | collective-permute-start | bytes 718856 | tf_op jit(solution)/shard_map/ppermute | solution.py:345
  36.9 0.0 collective-permute-done.13.refs_1_
  36.9 3.9 %backward.5 = (f32[2,104,576]{2,1,0:T(8,128)S(1)}, bf16[104,576]{1,0:T(8,128)(2,1)S(1)}, bf16[104,576]{1,0:T(8,128)(2,1)S(1)}) custom-call(s32[3]{0:T(128)S(1)} %pad_add_fusion.meta, bf16[104,1152]{1,0:T(8,128)(2,1)S(1)} %collective-permute-done.11.refs_0_, bf16[104,1152]{1,0:T(8,128)(2,1)S(1)} %collective-permute-done.13.refs_1_, ...), custom_call_target="tpu_custom_call" | custom-call | flops 1000 | bytes 1000 | tf_op jit(solution)/shard_map/backward/pallas_call | solution.py:234
  40.8 0.0 copy-start
  40.8 0.0 copy-start.1
  40.8 0.1 collective-permute-start.16
  40.9 0.5 collective-permute-start.17
  41.4 2.7 %collective-permute-done.12 = bf16[208,576]{1,0:T(8,128)(2,1)S(1)} collective-permute-done((bf16[208,576]{1,0:T(8,128)(2,1)S(1)}, bf16[208,576]{1,0:T(8,128)(2,1)S(1)}, u32[]{:S(2)}, u32[]{:S(2)}) %collective-permute-start.12) | collective-permute-done | bytes 239648 | tf_op jit(solution)/shard_map/ppermute | solution.py:345
  44.1 0.1 fusion.2
  44.2 0.0 collective-permute-done.16
  44.3 1.3 %collective-permute-start.18 = (bf16[104,576]{1,0:T(8,128)(2,1)S(1)}, bf16[104,576]{1,0:T(8,128)(2,1)S(1)}, u32[]{:S(2)}, u32[]{:S(2)}) collective-permute-start(bf16[104,576]{1,0:T(8,128)(2,1)S(1)} %fusion.3), channel_id=1, source_target_pairs={{0,1},{1,0},{2,3},{3,2},{4,5},{5,4},{6,7},{7,6},{8,9},{9,8},{10,11... | collective-permute-start | bytes 359432 | tf_op jit(solution)/shard_map/ppermute | solution.py:345
  45.6 0.1 collective-permute-start.14
  45.7 1.2 %collective-permute-start.15 = (bf16[104,576]{1,0:T(8,128)(2,1)S(1)}, bf16[104,576]{1,0:T(8,128)(2,1)S(1)}, u32[]{:S(2)}, u32[]{:S(2)}) collective-permute-start(bf16[104,576]{1,0:T(8,128)(2,1)S(1)} %get-tuple-element.92), channel_id=1, source_target_pairs={{0,8},{2,10},{4,12},{6,14},{8,0},{10,2},{12,4},{14,6},{1,9},{3,11}... | collective-permute-start | bytes 359432 | tf_op jit(solution)/shard_map/ppermute | solution.py:350
  46.9 2.4 %collective-permute-done.18 = bf16[104,576]{1,0:T(8,128)(2,1)S(1)} collective-permute-done((bf16[104,576]{1,0:T(8,128)(2,1)S(1)}, bf16[104,576]{1,0:T(8,128)(2,1)S(1)}, u32[]{:S(2)}, u32[]{:S(2)}) %collective-permute-start.18) | collective-permute-done | bytes 119840 | tf_op jit(solution)/shard_map/ppermute | solution.py:345
  49.3 0.1 fusion.5
  49.4 0.1 collective-permute-start.19
  49.5 1.8 %collective-permute-done.14.refs_1_ = bf16[104,576]{1,0:T(8,128)(2,1)S(1)} collective-permute-done((bf16[104,576]{1,0:T(8,128)(2,1)S(1)}, bf16[104,576]{1,0:T(8,128)(2,1)S(1)}, u32[]{:S(2)}, u32[]{:S(2)}) %collective-permute-start.14) | collective-permute-done | bytes 119840 | tf_op jit(solution)/shard_map/ppermute | solution.py:350
  51.2 1.1 %combine.1 = (f32[160,576]{1,0:T(8,128)S(1)}, f32[2,160]{1,0:T(2,128)S(1)}, bf16[2,160,104]{2,1,0:T(8,128)(2,1)S(1)}, f32[2,160,128]{2,1,0:T(8,128)S(1)}, f32[2,2,160]{2,1,0:T(2,128)S(1)}) custom-call(s32[3]{0:T(128)S(1)} %pad_add_fusion.meta, s32[2,160]{1,0:T(2,128)S(1)} %bitcast.38, f32[2,160]{1,0:T(2,128)S(1)} %bitcast.39, ...), custom_call_target="tpu_custom_call" | custom-call | flops 1000 | bytes 1000 | tf_op jit(solution)/shard_map/combine/pallas_call | solution.py:305
  52.3 6.0 %collective-permute-done.15.refs_0_ = bf16[104,576]{1,0:T(8,128)(2,1)S(1)} collective-permute-done((bf16[104,576]{1,0:T(8,128)(2,1)S(1)}, bf16[104,576]{1,0:T(8,128)(2,1)S(1)}, u32[]{:S(2)}, u32[]{:S(2)}) %collective-permute-start.15) | collective-permute-done | bytes 119840 | tf_op jit(solution)/shard_map/ppermute | solution.py:350
  58.3 1.0 %combine_late.1 = (bf16[160,576]{1,0:T(8,128)(2,1)}, bf16[2,160]{1,0:T(2,128)(2,1)}) custom-call(f32[160,576]{1,0:T(8,128)S(1)} %get-tuple-element.82.sum_in, f32[2,160]{1,0:T(2,128)S(1)} %get-tuple-element.83.product_in, bf16[2,160,104]{2,1,0:T(8,128)(2,1)S(1)} %get-tuple-element.84.pick_ref, f32[2,160,128]{2,1,0:T(8,128)S(1)} %get-tuple-element.85.weight_ref, ...), custom_call_target="tpu_custom_call" | custom-call | flops 1000 | bytes 1000 | tf_op jit(solution)/shard_map/combine_late/pallas_call | solution.py:320
  (11 shorter events, 0.1 us)
Async XLA Ops:
  0.6 8.4 %collective-permute-start.1 = (bf16[400,1152]{1,0:T(8,128)(2,1)}, bf16[400,1152]{1,0:T(8,128)(2,1)S(1)}, u32[]{:S(2)}, u32[]{:S(2)}) collective-permute-start(bf16[400,1152]{1,0:T(8,128)(2,1)} %bitcast.40), channel_id=1, source_target_pairs={{0,2},{2,0},{4,6},{6,4},{8,10},{10,8},{12,14},{14,12},{1,3},{3,1},... | collective-permute-start | bytes 2764808 | tf_op jit(solution)/shard_map/ppermute | solution.py:340
  3.3 5.7 %collective-permute-start = (bf16[104,1152]{1,0:T(8,128)(2,1)S(1)}, bf16[104,1152]{1,0:T(8,128)(2,1)S(1)}, u32[]{:S(2)}, u32[]{:S(2)}) collective-permute-start(bf16[104,1152]{1,0:T(8,128)(2,1)S(1)} %get-tuple-element.48.refs_0_), channel_id=1, source_target_pairs={{0,2},{2,0},{4,6},{6,4},{8,10},{10,8},{12,14},{14,12},{1,3},{3,1},... | collective-permute-start | bytes 718856 | tf_op jit(solution)/shard_map/ppermute | solution.py:340
  3.4 21.7 %collective-permute-start.4 = (bf16[104,1152]{1,0:T(8,128)(2,1)S(1)}, bf16[104,1152]{1,0:T(8,128)(2,1)S(1)}, u32[]{:S(2)}, u32[]{:S(2)}) collective-permute-start(bf16[104,1152]{1,0:T(8,128)(2,1)S(1)} %get-tuple-element.59), channel_id=1, source_target_pairs={{0,8},{2,10},{4,12},{6,14},{8,0},{10,2},{12,4},{14,6},{1,9},{3,11}... | collective-permute-start | bytes 718856 | tf_op jit(solution)/shard_map/ppermute | solution.py:350
  7.4 17.7 %collective-permute-start.5 = (bf16[104,1152]{1,0:T(8,128)(2,1)S(1)}, bf16[104,1152]{1,0:T(8,128)(2,1)S(1)}, u32[]{:S(2)}, u32[]{:S(2)}) collective-permute-start(bf16[104,1152]{1,0:T(8,128)(2,1)S(1)} %get-tuple-element.61), channel_id=1, source_target_pairs={{0,4},{2,6},{4,8},{6,10},{8,12},{10,14},{12,0},{14,2},{1,5},{3,7},... | collective-permute-start | bytes 718856 | tf_op jit(solution)/shard_map/ppermute | solution.py:350
  22.2 3.3 %collective-permute-start.2 = (bf16[104,576]{1,0:T(8,128)(2,1)S(1)}, bf16[104,576]{1,0:T(8,128)(2,1)S(1)}, u32[]{:S(2)}, u32[]{:S(2)}) collective-permute-start(bf16[104,576]{1,0:T(8,128)(2,1)S(1)} %get-tuple-element.57), channel_id=1, source_target_pairs={{0,2},{2,0},{4,6},{6,4},{8,10},{10,8},{12,14},{14,12},{1,3},{3,1},... | collective-permute-start | bytes 359432 | tf_op jit(solution)/shard_map/ppermute | solution.py:340
  22.3 3.3 %collective-permute-start.3 = (bf16[104,576]{1,0:T(8,128)(2,1)S(1)}, bf16[104,576]{1,0:T(8,128)(2,1)S(1)}, u32[]{:S(2)}, u32[]{:S(2)}) collective-permute-start(bf16[104,576]{1,0:T(8,128)(2,1)S(1)} %get-tuple-element.58), channel_id=1, source_target_pairs={{0,2},{2,0},{4,6},{6,4},{8,10},{10,8},{12,14},{14,12},{1,3},{3,1},... | collective-permute-start | bytes 359432 | tf_op jit(solution)/shard_map/ppermute | solution.py:340
  22.8 11.3 %collective-permute-start.11 = (bf16[104,1152]{1,0:T(8,128)(2,1)S(1)}, bf16[104,1152]{1,0:T(8,128)(2,1)S(1)}, u32[]{:S(2)}, u32[]{:S(2)}) collective-permute-start(bf16[104,1152]{1,0:T(8,128)(2,1)S(1)} %get-tuple-element.73), channel_id=1, source_target_pairs={{0,12},{2,14},{4,0},{6,2},{8,4},{10,6},{12,8},{14,10},{1,13},{3,15... | collective-permute-start | bytes 718856 | tf_op jit(solution)/shard_map/ppermute | solution.py:350
  25.1 2.1 %collective-permute-start.7 = (bf16[104,1152]{1,0:T(8,128)(2,1)S(1)}, bf16[104,1152]{1,0:T(8,128)(2,1)S(1)}, u32[]{:S(2)}, u32[]{:S(2)}) collective-permute-start(bf16[104,1152]{1,0:T(8,128)(2,1)S(1)} %collective-permute-done.4.refs_0_), channel_id=1, source_target_pairs={{0,2},{2,0},{4,6},{6,4},{8,10},{10,8},{12,14},{14,12},{1,3},{3,1},... | collective-permute-start | bytes 718856 | tf_op jit(solution)/shard_map/ppermute | solution.py:340
  25.1 2.1 %collective-permute-start.8 = (bf16[104,1152]{1,0:T(8,128)(2,1)S(1)}, bf16[104,1152]{1,0:T(8,128)(2,1)S(1)}, u32[]{:S(2)}, u32[]{:S(2)}) collective-permute-start(bf16[104,1152]{1,0:T(8,128)(2,1)S(1)} %collective-permute-done.5.refs_1_), channel_id=1, source_target_pairs={{0,2},{2,0},{4,6},{6,4},{8,10},{10,8},{12,14},{14,12},{1,3},{3,1},... | collective-permute-start | bytes 718856 | tf_op jit(solution)/shard_map/ppermute | solution.py:340
  25.6 8.5 %collective-permute-start.6 = (bf16[104,576]{1,0:T(8,128)(2,1)S(1)}, bf16[104,576]{1,0:T(8,128)(2,1)S(1)}, u32[]{:S(2)}, u32[]{:S(2)}) collective-permute-start(bf16[104,576]{1,0:T(8,128)(2,1)S(1)} %fusion.6), channel_id=1, source_target_pairs={{0,1},{1,0},{2,3},{3,2},{4,5},{5,4},{6,7},{7,6},{8,9},{9,8},{10,11... | collective-permute-start | bytes 359432 | tf_op jit(solution)/shard_map/ppermute | solution.py:345
  33.6 1.6 %collective-permute-start.10 = (bf16[208,576]{1,0:T(8,128)(2,1)S(1)}, bf16[208,576]{1,0:T(8,128)(2,1)S(1)}, u32[]{:S(2)}, u32[]{:S(2)}) collective-permute-start(bf16[208,576]{1,0:T(8,128)(2,1)S(1)} %get-tuple-element.70), channel_id=1, source_target_pairs={{0,2},{2,0},{4,6},{6,4},{8,10},{10,8},{12,14},{14,12},{1,3},{3,1},... | collective-permute-start | bytes 718856 | tf_op jit(solution)/shard_map/ppermute | solution.py:340
  33.6 1.9 %collective-permute-start.9 = (bf16[208,576]{1,0:T(8,128)(2,1)S(1)}, bf16[208,576]{1,0:T(8,128)(2,1)S(1)}, u32[]{:S(2)}, u32[]{:S(2)}) collective-permute-start(bf16[208,576]{1,0:T(8,128)(2,1)S(1)} %get-tuple-element.69), channel_id=1, source_target_pairs={{0,2},{2,0},{4,6},{6,4},{8,10},{10,8},{12,14},{14,12},{1,3},{3,1},... | collective-permute-start | bytes 718856 | tf_op jit(solution)/shard_map/ppermute | solution.py:340
  34.1 2.8 %collective-permute-start.13 = (bf16[104,1152]{1,0:T(8,128)(2,1)S(1)}, bf16[104,1152]{1,0:T(8,128)(2,1)S(1)}, u32[]{:S(2)}, u32[]{:S(2)}) collective-permute-start(bf16[104,1152]{1,0:T(8,128)(2,1)S(1)} %collective-permute-done.11.refs_0_), channel_id=1, source_target_pairs={{0,2},{2,0},{4,6},{6,4},{8,10},{10,8},{12,14},{14,12},{1,3},{3,1},... | collective-permute-start | bytes 718856 | tf_op jit(solution)/shard_map/ppermute | solution.py:340
  35.6 8.5 %collective-permute-start.12 = (bf16[208,576]{1,0:T(8,128)(2,1)S(1)}, bf16[208,576]{1,0:T(8,128)(2,1)S(1)}, u32[]{:S(2)}, u32[]{:S(2)}) collective-permute-start(bf16[208,576]{1,0:T(8,128)(2,1)S(1)} %fusion), channel_id=1, source_target_pairs={{0,1},{1,0},{2,3},{3,2},{4,5},{5,4},{6,7},{7,6},{8,9},{9,8},{10,11... | collective-permute-start | bytes 718856 | tf_op jit(solution)/shard_map/ppermute | solution.py:345
  40.8 10.4 %copy-start = (s32[160,2]{0,1:T(2,128)S(1)}, s32[160,2]{0,1:T(2,128)}, u32[]{:S(2)}) copy-start(s32[160,2]{0,1:T(2,128)} %param.8) | copy-start | bytes 3844
  40.8 10.4 %copy-start.1 = (f32[160,2]{0,1:T(2,128)S(1)}, f32[160,2]{0,1:T(2,128)}, u32[]{:S(2)}) copy-start(f32[160,2]{0,1:T(2,128)} %param.9) | copy-start | bytes 3844
  40.8 3.4 %collective-permute-start.16 = (bf16[104,576]{1,0:T(8,128)(2,1)S(1)}, bf16[104,576]{1,0:T(8,128)(2,1)S(1)}, u32[]{:S(2)}, u32[]{:S(2)}) collective-permute-start(bf16[104,576]{1,0:T(8,128)(2,1)S(1)} %get-tuple-element.79), channel_id=1, source_target_pairs={{0,2},{2,0},{4,6},{6,4},{8,10},{10,8},{12,14},{14,12},{1,3},{3,1},... | collective-permute-start | bytes 359432 | tf_op jit(solution)/shard_map/ppermute | solution.py:340
  40.9 3.3 %collective-permute-start.17 = (bf16[104,576]{1,0:T(8,128)(2,1)S(1)}, bf16[104,576]{1,0:T(8,128)(2,1)S(1)}, u32[]{:S(2)}, u32[]{:S(2)}) collective-permute-start(bf16[104,576]{1,0:T(8,128)(2,1)S(1)} %get-tuple-element.80), channel_id=1, source_target_pairs={{0,2},{2,0},{4,6},{6,4},{8,10},{10,8},{12,14},{14,12},{1,3},{3,1},... | collective-permute-start | bytes 359432 | tf_op jit(solution)/shard_map/ppermute | solution.py:340
  44.3 5.1 %collective-permute-start.18 = (bf16[104,576]{1,0:T(8,128)(2,1)S(1)}, bf16[104,576]{1,0:T(8,128)(2,1)S(1)}, u32[]{:S(2)}, u32[]{:S(2)}) collective-permute-start(bf16[104,576]{1,0:T(8,128)(2,1)S(1)} %fusion.3), channel_id=1, source_target_pairs={{0,1},{1,0},{2,3},{3,2},{4,5},{5,4},{6,7},{7,6},{8,9},{9,8},{10,11... | collective-permute-start | bytes 359432 | tf_op jit(solution)/shard_map/ppermute | solution.py:345
  45.6 5.6 %collective-permute-start.14 = (bf16[104,576]{1,0:T(8,128)(2,1)S(1)}, bf16[104,576]{1,0:T(8,128)(2,1)S(1)}, u32[]{:S(2)}, u32[]{:S(2)}) collective-permute-start(bf16[104,576]{1,0:T(8,128)(2,1)S(1)} %get-tuple-element.93), channel_id=1, source_target_pairs={{0,12},{2,14},{4,0},{6,2},{8,4},{10,6},{12,8},{14,10},{1,13},{3,15... | collective-permute-start | bytes 359432 | tf_op jit(solution)/shard_map/ppermute | solution.py:350
  45.7 12.6 %collective-permute-start.15 = (bf16[104,576]{1,0:T(8,128)(2,1)S(1)}, bf16[104,576]{1,0:T(8,128)(2,1)S(1)}, u32[]{:S(2)}, u32[]{:S(2)}) collective-permute-start(bf16[104,576]{1,0:T(8,128)(2,1)S(1)} %get-tuple-element.92), channel_id=1, source_target_pairs={{0,8},{2,10},{4,12},{6,14},{8,0},{10,2},{12,4},{14,6},{1,9},{3,11}... | collective-permute-start | bytes 359432 | tf_op jit(solution)/shard_map/ppermute | solution.py:350
  49.4 8.9 %collective-permute-start.19 = (bf16[104,576]{1,0:T(8,128)(2,1)S(1)}, bf16[104,576]{1,0:T(8,128)(2,1)S(1)}, u32[]{:S(2)}, u32[]{:S(2)}) collective-permute-start(bf16[104,576]{1,0:T(8,128)(2,1)S(1)} %fusion.5), channel_id=1, source_target_pairs={{0,4},{2,6},{4,8},{6,10},{8,12},{10,14},{12,0},{14,2},{1,5},{3,7},... | collective-permute-start | bytes 359432 | tf_op jit(solution)/shard_map/ppermute | solution.py:350

commit v5 on v4

--- a/solution.py
+++ b/solution.py
@@ -146,7 +146,7 @@
             copy.wait()
         gate = dot(rows, gate_ref[:, unit])
         up = dot(rows, up_ref[:, unit])
-        sig = jax.nn.sigmoid(gate)
+        sig = 0.5 * jnp.tanh(0.5 * gate) + 0.5
         act = gate * sig
         act_ref[:, unit] = act.astype(jnp.bfloat16)
         slope_ref[:, unit] = (up * (sig + act * (1.0 - sig))).astype(jnp.bfloat16)

time: 59.4 us -> 59.6 us (level)
  no operation moved by 1% of the time
where the time goes in v5:
time: 59.6 us; the launch traced here: 59.4 us
  Pallas kernels  27.7 us (46%)
  starting transfers between devices  16.3 us (27%)
  waiting for transfers between devices  14.2 us (24%)
  between operations  0.79 us (1%)
    pallas_call x3, Pallas kernels, backward(): pl.pallas_call(functools.partial(backward_kernel, [len(cot) for cot in co...  14.2 us
    pallas_call x1, Pallas kernels, forward(): pl.pallas_call(functools.partial(forward_kernel, peers, cap, padded, orde...  9.5 us
    ppermute x6, starting transfers between devices, shifted(): lax.ppermute(block, 'expert', [(i, (i + 2 * d) % count) for i in range(co...  9.2 us
    ppermute x6, waiting for transfers between devices, shifted(): lax.ppermute(block, 'expert', [(i, (i + 2 * d) % count) for i in range(co...  7.79 us
    ppermute x3, waiting for transfers between devices, hidden_ring(): lax.ppermute(block, 'hidden', [(i, (i + r) % count) for i in range(count)])  5.11 us
    ppermute x3, starting transfers between devices, hidden_ring(): lax.ppermute(block, 'hidden', [(i, (i + r) % count) for i in range(count)])  4.16 us
    ppermute x11, starting transfers between devices, swap_pair(): return lax.ppermute(block, 'expert', [(i, i ^ 1) for i in range(count)])  2.94 us
    pallas_call x1, Pallas kernels, route(): pl.pallas_call(functools.partial(route_kernel, peers, padded, spread), ou...  2.02 us
  transfers between devices with their start and end apart: 20, of which 6 were waited for; matrix products, arithmetic and copies ran while one was open for 1% of the time, Pallas kernels for 45%

profile of v5, /device:TPU:0, one launch (start us, length us, event | category | flops | bytes accessed | tf_op | source)
XLA Modules:
  0.0 59.4 jit_solution(17028510954848115919)
XLA Ops:
  0.6 0.5 collective-permute-start.1
  1.1 0.1 pad_add_fusion.meta
  1.2 2.0 %route.1 = (bf16[104,1152]{1,0:T(8,128)(2,1)S(1)}, bf16[104,1152]{1,0:T(8,128)(2,1)S(1)}, bf16[104,1152]{1,0:T(8,128)(2,1)S(1)}, bf16[104,1152]{1,0:T(8,128)(2,1)S(1)}) custom-call(s32[3]{0:T(128)S(1)} %pad_add_fusion.meta, s32[2,160]{1,0:T(2,128)} %bitcast.37, bf16[160,1152]{1,0:T(8,128)(2,1)} %grad_hbm.1), custom_call_target="tpu_custom_call" | custom-call | flops 1000 | bytes 1000 | tf_op jit(solution)/shard_map/route/pallas_call | solution.py:90
  3.3 0.1 collective-permute-start
  3.4 4.0 %collective-permute-start.4 = (bf16[104,1152]{1,0:T(8,128)(2,1)S(1)}, bf16[104,1152]{1,0:T(8,128)(2,1)S(1)}, u32[]{:S(2)}, u32[]{:S(2)}) collective-permute-start(bf16[104,1152]{1,0:T(8,128)(2,1)S(1)} %get-tuple-element.59), channel_id=1, source_target_pairs={{0,8},{2,10},{4,12},{6,14},{8,0},{10,2},{12,4},{14,6},{1,9},{3,11}... | collective-permute-start | bytes 718856 | tf_op jit(solution)/shard_map/ppermute | solution.py:350
  7.4 1.6 %collective-permute-start.5 = (bf16[104,1152]{1,0:T(8,128)(2,1)S(1)}, bf16[104,1152]{1,0:T(8,128)(2,1)S(1)}, u32[]{:S(2)}, u32[]{:S(2)}) collective-permute-start(bf16[104,1152]{1,0:T(8,128)(2,1)S(1)} %get-tuple-element.61), channel_id=1, source_target_pairs={{0,4},{2,6},{4,8},{6,10},{8,12},{10,14},{12,0},{14,2},{1,5},{3,7},... | collective-permute-start | bytes 718856 | tf_op jit(solution)/shard_map/ppermute | solution.py:350
  9.0 0.0 collective-permute-done.refs_1_
  9.0 0.0 collective-permute-done.1.other_ref
  9.0 9.5 %forward.1 = (bf16[896,1152]{1,0:T(8,128)(2,1)S(1)}, bf16[896,1152]{1,0:T(8,128)(2,1)S(1)}, bf16[896,1152]{1,0:T(8,128)(2,1)S(1)}, bf16[1152,1152]{1,0:T(8,128)(...) custom-call(s32[3]{0:T(128)S(1)} %pad_add_fusion.meta, bf16[1,400,1152]{2,1,0:T(8,128)(2,1)} %own_hbm.1, ...), custom_call_target="tpu_custom_call" | custom-call | flops 1000 | bytes 1000 | tf_op jit(solution)/shard_map/forward/pallas_call | solution.py:163
  18.5 3.9 %backward.3 = (f32[2,104,576]{2,1,0:T(8,128)S(1)}, bf16[104,576]{1,0:T(8,128)(2,1)S(1)}, bf16[104,576]{1,0:T(8,128)(2,1)S(1)}) custom-call(s32[3]{0:T(128)S(1)} %pad_add_fusion.meta, bf16[104,1152]{1,0:T(8,128)(2,1)S(1)} %get-tuple-element.48.refs_0_, bf16[104,1152]{1,0:T(8,128)(2,1)S(1)} %collective-permute-done.refs_1_, ...), custom_call_target="tpu_custom_call" | custom-call | flops 1000 | bytes 1000 | tf_op jit(solution)/shard_map/backward/pallas_call | solution.py:234
  22.4 0.1 collective-permute-start.2
  22.5 0.5 collective-permute-start.3
  23.0 2.2 %collective-permute-start.11 = (bf16[104,1152]{1,0:T(8,128)(2,1)S(1)}, bf16[104,1152]{1,0:T(8,128)(2,1)S(1)}, u32[]{:S(2)}, u32[]{:S(2)}) collective-permute-start(bf16[104,1152]{1,0:T(8,128)(2,1)S(1)} %get-tuple-element.73), channel_id=1, source_target_pairs={{0,12},{2,14},{4,0},{6,2},{8,4},{10,6},{12,8},{14,10},{1,13},{3,15... | collective-permute-start | bytes 718856 | tf_op jit(solution)/shard_map/ppermute | solution.py:350
  25.2 0.0 collective-permute-done.4.refs_0_
  25.2 0.0 collective-permute-start.7
  25.2 0.0 collective-permute-done.5.refs_1_
  25.3 0.5 collective-permute-start.8
  25.8 0.0 collective-permute-done.2
  25.8 1.6 %collective-permute-start.6 = (bf16[104,576]{1,0:T(8,128)(2,1)S(1)}, bf16[104,576]{1,0:T(8,128)(2,1)S(1)}, u32[]{:S(2)}, u32[]{:S(2)}) collective-permute-start(bf16[104,576]{1,0:T(8,128)(2,1)S(1)} %fusion.6), channel_id=1, source_target_pairs={{0,1},{1,0},{2,3},{3,2},{4,5},{5,4},{6,7},{7,6},{8,9},{9,8},{10,11... | collective-permute-start | bytes 359432 | tf_op jit(solution)/shard_map/ppermute | solution.py:345
  27.4 6.4 %backward.4 = (f32[2,208,576]{2,1,0:T(8,128)S(1)}, bf16[208,576]{1,0:T(8,128)(2,1)S(1)}, bf16[208,576]{1,0:T(8,128)(2,1)S(1)}) custom-call(s32[3]{0:T(128)S(1)} %pad_add_fusion.meta, bf16[104,1152]{1,0:T(8,128)(2,1)S(1)} %collective-permute-done.4.refs_0_, bf16[104,1152]{1,0:T(8,128)(2,1)S(1)} %collective-permute-done.5.refs_1_, ...), custom_call_target="tpu_custom_call" | custom-call | flops 1000 | bytes 1000 | tf_op jit(solution)/shard_map/backward/pallas_call | solution.py:234
  33.7 0.1 collective-permute-start.10
  33.8 0.5 collective-permute-start.9
  34.3 0.0 collective-permute-done.11.refs_0_
  34.3 0.0 collective-permute-done.6
  34.3 0.1 collective-permute-start.13
  34.4 0.1 fusion.8.refs_0_
  34.5 0.9 %collective-permute-done.10 = bf16[208,576]{1,0:T(8,128)(2,1)S(1)} collective-permute-done((bf16[208,576]{1,0:T(8,128)(2,1)S(1)}, bf16[208,576]{1,0:T(8,128)(2,1)S(1)}, u32[]{:S(2)}, u32[]{:S(2)}) %collective-permute-start.10) | collective-permute-done | bytes 239648 | tf_op jit(solution)/shard_map/ppermute | solution.py:340
  35.3 0.4 collective-permute-done.9
  35.7 0.1 fusion
  35.8 1.3 %collective-permute-start.12 = (bf16[208,576]{1,0:T(8,128)(2,1)S(1)}, bf16[208,576]{1,0:T(8,128)(2,1)S(1)}, u32[]{:S(2)}, u32[]{:S(2)}) collective-permute-start(bf16[208,576]{1,0:T(8,128)(2,1)S(1)} %fusion), channel_id=1, source_target_pairs={{0,1},{1,0},{2,3},{3,2},{4,5},{5,4},{6,7},{7,6},{8,9},{9,8},{10,11... | collective-permute-start | bytes 718856 | tf_op jit(solution)/shard_map/ppermute | solution.py:345
  37.1 3.9 %backward.5 = (f32[2,104,576]{2,1,0:T(8,128)S(1)}, bf16[104,576]{1,0:T(8,128)(2,1)S(1)}, bf16[104,576]{1,0:T(8,128)(2,1)S(1)}) custom-call(s32[3]{0:T(128)S(1)} %pad_add_fusion.meta, bf16[104,1152]{1,0:T(8,128)(2,1)S(1)} %collective-permute-done.11.refs_0_, bf16[104,1152]{1,0:T(8,128)(2,1)S(1)} %collective-permute-done.13.refs_1_, ...), custom_call_target="tpu_custom_call" | custom-call | flops 1000 | bytes 1000 | tf_op jit(solution)/shard_map/backward/pallas_call | solution.py:234
  41.0 0.0 copy-start
  41.0 0.0 copy-start.1
  41.0 0.1 collective-permute-start.16
  41.1 0.5 collective-permute-start.17
  41.6 2.7 %collective-permute-done.12 = bf16[208,576]{1,0:T(8,128)(2,1)S(1)} collective-permute-done((bf16[208,576]{1,0:T(8,128)(2,1)S(1)}, bf16[208,576]{1,0:T(8,128)(2,1)S(1)}, u32[]{:S(2)}, u32[]{:S(2)}) %collective-permute-start.12) | collective-permute-done | bytes 239648 | tf_op jit(solution)/shard_map/ppermute | solution.py:345
  44.3 0.1 fusion.2
  44.4 0.0 collective-permute-done.17
  44.5 1.3 %collective-permute-start.18 = (bf16[104,576]{1,0:T(8,128)(2,1)S(1)}, bf16[104,576]{1,0:T(8,128)(2,1)S(1)}, u32[]{:S(2)}, u32[]{:S(2)}) collective-permute-start(bf16[104,576]{1,0:T(8,128)(2,1)S(1)} %fusion.3), channel_id=1, source_target_pairs={{0,1},{1,0},{2,3},{3,2},{4,5},{5,4},{6,7},{7,6},{8,9},{9,8},{10,11... | collective-permute-start | bytes 359432 | tf_op jit(solution)/shard_map/ppermute | solution.py:345
  45.8 0.1 collective-permute-start.14
  45.9 1.2 %collective-permute-start.15 = (bf16[104,576]{1,0:T(8,128)(2,1)S(1)}, bf16[104,576]{1,0:T(8,128)(2,1)S(1)}, u32[]{:S(2)}, u32[]{:S(2)}) collective-permute-start(bf16[104,576]{1,0:T(8,128)(2,1)S(1)} %get-tuple-element.92), channel_id=1, source_target_pairs={{0,8},{2,10},{4,12},{6,14},{8,0},{10,2},{12,4},{14,6},{1,9},{3,11}... | collective-permute-start | bytes 359432 | tf_op jit(solution)/shard_map/ppermute | solution.py:350
  47.1 2.4 %collective-permute-done.18 = bf16[104,576]{1,0:T(8,128)(2,1)S(1)} collective-permute-done((bf16[104,576]{1,0:T(8,128)(2,1)S(1)}, bf16[104,576]{1,0:T(8,128)(2,1)S(1)}, u32[]{:S(2)}, u32[]{:S(2)}) %collective-permute-start.18) | collective-permute-done | bytes 119840 | tf_op jit(solution)/shard_map/ppermute | solution.py:345
  49.5 0.1 fusion.5
  49.6 0.1 collective-permute-start.19
  49.6 1.8 %collective-permute-done.14.refs_1_ = bf16[104,576]{1,0:T(8,128)(2,1)S(1)} collective-permute-done((bf16[104,576]{1,0:T(8,128)(2,1)S(1)}, bf16[104,576]{1,0:T(8,128)(2,1)S(1)}, u32[]{:S(2)}, u32[]{:S(2)}) %collective-permute-start.14) | collective-permute-done | bytes 119840 | tf_op jit(solution)/shard_map/ppermute | solution.py:350
  51.5 1.1 %combine.1 = (f32[160,576]{1,0:T(8,128)S(1)}, f32[2,160]{1,0:T(2,128)S(1)}, bf16[2,160,104]{2,1,0:T(8,128)(2,1)S(1)}, f32[2,160,128]{2,1,0:T(8,128)S(1)}, f32[2,2,160]{2,1,0:T(2,128)S(1)}) custom-call(s32[3]{0:T(128)S(1)} %pad_add_fusion.meta, s32[2,160]{1,0:T(2,128)S(1)} %bitcast.38, f32[2,160]{1,0:T(2,128)S(1)} %bitcast.39, ...), custom_call_target="tpu_custom_call" | custom-call | flops 1000 | bytes 1000 | tf_op jit(solution)/shard_map/combine/pallas_call | solution.py:305
  52.5 6.0 %collective-permute-done.15.refs_0_ = bf16[104,576]{1,0:T(8,128)(2,1)S(1)} collective-permute-done((bf16[104,576]{1,0:T(8,128)(2,1)S(1)}, bf16[104,576]{1,0:T(8,128)(2,1)S(1)}, u32[]{:S(2)}, u32[]{:S(2)}) %collective-permute-start.15) | collective-permute-done | bytes 119840 | tf_op jit(solution)/shard_map/ppermute | solution.py:350
  58.5 1.0 %combine_late.1 = (bf16[160,576]{1,0:T(8,128)(2,1)}, bf16[2,160]{1,0:T(2,128)(2,1)}) custom-call(f32[160,576]{1,0:T(8,128)S(1)} %get-tuple-element.82.sum_in, f32[2,160]{1,0:T(2,128)S(1)} %get-tuple-element.83.product_in, bf16[2,160,104]{2,1,0:T(8,128)(2,1)S(1)} %get-tuple-element.84.pick_ref, f32[2,160,128]{2,1,0:T(8,128)S(1)} %get-tuple-element.85.weight_ref, ...), custom_call_target="tpu_custom_call" | custom-call | flops 1000 | bytes 1000 | tf_op jit(solution)/shard_map/combine_late/pallas_call | solution.py:320
  (11 shorter events, 0.1 us)
Async XLA Ops:
  0.6 8.4 %collective-permute-start.1 = (bf16[400,1152]{1,0:T(8,128)(2,1)}, bf16[400,1152]{1,0:T(8,128)(2,1)S(1)}, u32[]{:S(2)}, u32[]{:S(2)}) collective-permute-start(bf16[400,1152]{1,0:T(8,128)(2,1)} %bitcast.40), channel_id=1, source_target_pairs={{0,2},{2,0},{4,6},{6,4},{8,10},{10,8},{12,14},{14,12},{1,3},{3,1},... | collective-permute-start | bytes 2764808 | tf_op jit(solution)/shard_map/ppermute | solution.py:340
  3.3 5.7 %collective-permute-start = (bf16[104,1152]{1,0:T(8,128)(2,1)S(1)}, bf16[104,1152]{1,0:T(8,128)(2,1)S(1)}, u32[]{:S(2)}, u32[]{:S(2)}) collective-permute-start(bf16[104,1152]{1,0:T(8,128)(2,1)S(1)} %get-tuple-element.48.refs_0_), channel_id=1, source_target_pairs={{0,2},{2,0},{4,6},{6,4},{8,10},{10,8},{12,14},{14,12},{1,3},{3,1},... | collective-permute-start | bytes 718856 | tf_op jit(solution)/shard_map/ppermute | solution.py:340
  3.4 21.9 %collective-permute-start.4 = (bf16[104,1152]{1,0:T(8,128)(2,1)S(1)}, bf16[104,1152]{1,0:T(8,128)(2,1)S(1)}, u32[]{:S(2)}, u32[]{:S(2)}) collective-permute-start(bf16[104,1152]{1,0:T(8,128)(2,1)S(1)} %get-tuple-element.59), channel_id=1, source_target_pairs={{0,8},{2,10},{4,12},{6,14},{8,0},{10,2},{12,4},{14,6},{1,9},{3,11}... | collective-permute-start | bytes 718856 | tf_op jit(solution)/shard_map/ppermute | solution.py:350
  7.4 17.8 %collective-permute-start.5 = (bf16[104,1152]{1,0:T(8,128)(2,1)S(1)}, bf16[104,1152]{1,0:T(8,128)(2,1)S(1)}, u32[]{:S(2)}, u32[]{:S(2)}) collective-permute-start(bf16[104,1152]{1,0:T(8,128)(2,1)S(1)} %get-tuple-element.61), channel_id=1, source_target_pairs={{0,4},{2,6},{4,8},{6,10},{8,12},{10,14},{12,0},{14,2},{1,5},{3,7},... | collective-permute-start | bytes 718856 | tf_op jit(solution)/shard_map/ppermute | solution.py:350
  22.4 3.3 %collective-permute-start.2 = (bf16[104,576]{1,0:T(8,128)(2,1)S(1)}, bf16[104,576]{1,0:T(8,128)(2,1)S(1)}, u32[]{:S(2)}, u32[]{:S(2)}) collective-permute-start(bf16[104,576]{1,0:T(8,128)(2,1)S(1)} %get-tuple-element.57), channel_id=1, source_target_pairs={{0,2},{2,0},{4,6},{6,4},{8,10},{10,8},{12,14},{14,12},{1,3},{3,1},... | collective-permute-start | bytes 359432 | tf_op jit(solution)/shard_map/ppermute | solution.py:340
  22.5 3.3 %collective-permute-start.3 = (bf16[104,576]{1,0:T(8,128)(2,1)S(1)}, bf16[104,576]{1,0:T(8,128)(2,1)S(1)}, u32[]{:S(2)}, u32[]{:S(2)}) collective-permute-start(bf16[104,576]{1,0:T(8,128)(2,1)S(1)} %get-tuple-element.58), channel_id=1, source_target_pairs={{0,2},{2,0},{4,6},{6,4},{8,10},{10,8},{12,14},{14,12},{1,3},{3,1},... | collective-permute-start | bytes 359432 | tf_op jit(solution)/shard_map/ppermute | solution.py:340
  23.0 11.3 %collective-permute-start.11 = (bf16[104,1152]{1,0:T(8,128)(2,1)S(1)}, bf16[104,1152]{1,0:T(8,128)(2,1)S(1)}, u32[]{:S(2)}, u32[]{:S(2)}) collective-permute-start(bf16[104,1152]{1,0:T(8,128)(2,1)S(1)} %get-tuple-element.73), channel_id=1, source_target_pairs={{0,12},{2,14},{4,0},{6,2},{8,4},{10,6},{12,8},{14,10},{1,13},{3,15... | collective-permute-start | bytes 718856 | tf_op jit(solution)/shard_map/ppermute | solution.py:350
  25.2 2.1 %collective-permute-start.7 = (bf16[104,1152]{1,0:T(8,128)(2,1)S(1)}, bf16[104,1152]{1,0:T(8,128)(2,1)S(1)}, u32[]{:S(2)}, u32[]{:S(2)}) collective-permute-start(bf16[104,1152]{1,0:T(8,128)(2,1)S(1)} %collective-permute-done.4.refs_0_), channel_id=1, source_target_pairs={{0,2},{2,0},{4,6},{6,4},{8,10},{10,8},{12,14},{14,12},{1,3},{3,1},... | collective-permute-start | bytes 718856 | tf_op jit(solution)/shard_map/ppermute | solution.py:340
  25.3 2.1 %collective-permute-start.8 = (bf16[104,1152]{1,0:T(8,128)(2,1)S(1)}, bf16[104,1152]{1,0:T(8,128)(2,1)S(1)}, u32[]{:S(2)}, u32[]{:S(2)}) collective-permute-start(bf16[104,1152]{1,0:T(8,128)(2,1)S(1)} %collective-permute-done.5.refs_1_), channel_id=1, source_target_pairs={{0,2},{2,0},{4,6},{6,4},{8,10},{10,8},{12,14},{14,12},{1,3},{3,1},... | collective-permute-start | bytes 718856 | tf_op jit(solution)/shard_map/ppermute | solution.py:340
  25.8 8.5 %collective-permute-start.6 = (bf16[104,576]{1,0:T(8,128)(2,1)S(1)}, bf16[104,576]{1,0:T(8,128)(2,1)S(1)}, u32[]{:S(2)}, u32[]{:S(2)}) collective-permute-start(bf16[104,576]{1,0:T(8,128)(2,1)S(1)} %fusion.6), channel_id=1, source_target_pairs={{0,1},{1,0},{2,3},{3,2},{4,5},{5,4},{6,7},{7,6},{8,9},{9,8},{10,11... | collective-permute-start | bytes 359432 | tf_op jit(solution)/shard_map/ppermute | solution.py:345
  33.7 1.6 %collective-permute-start.10 = (bf16[208,576]{1,0:T(8,128)(2,1)S(1)}, bf16[208,576]{1,0:T(8,128)(2,1)S(1)}, u32[]{:S(2)}, u32[]{:S(2)}) collective-permute-start(bf16[208,576]{1,0:T(8,128)(2,1)S(1)} %get-tuple-element.70), channel_id=1, source_target_pairs={{0,2},{2,0},{4,6},{6,4},{8,10},{10,8},{12,14},{14,12},{1,3},{3,1},... | collective-permute-start | bytes 718856 | tf_op jit(solution)/shard_map/ppermute | solution.py:340
  33.8 1.9 %collective-permute-start.9 = (bf16[208,576]{1,0:T(8,128)(2,1)S(1)}, bf16[208,576]{1,0:T(8,128)(2,1)S(1)}, u32[]{:S(2)}, u32[]{:S(2)}) collective-permute-start(bf16[208,576]{1,0:T(8,128)(2,1)S(1)} %get-tuple-element.69), channel_id=1, source_target_pairs={{0,2},{2,0},{4,6},{6,4},{8,10},{10,8},{12,14},{14,12},{1,3},{3,1},... | collective-permute-start | bytes 718856 | tf_op jit(solution)/shard_map/ppermute | solution.py:340
  34.3 2.8 %collective-permute-start.13 = (bf16[104,1152]{1,0:T(8,128)(2,1)S(1)}, bf16[104,1152]{1,0:T(8,128)(2,1)S(1)}, u32[]{:S(2)}, u32[]{:S(2)}) collective-permute-start(bf16[104,1152]{1,0:T(8,128)(2,1)S(1)} %collective-permute-done.11.refs_0_), channel_id=1, source_target_pairs={{0,2},{2,0},{4,6},{6,4},{8,10},{10,8},{12,14},{14,12},{1,3},{3,1},... | collective-permute-start | bytes 718856 | tf_op jit(solution)/shard_map/ppermute | solution.py:340
  35.8 8.5 %collective-permute-start.12 = (bf16[208,576]{1,0:T(8,128)(2,1)S(1)}, bf16[208,576]{1,0:T(8,128)(2,1)S(1)}, u32[]{:S(2)}, u32[]{:S(2)}) collective-permute-start(bf16[208,576]{1,0:T(8,128)(2,1)S(1)} %fusion), channel_id=1, source_target_pairs={{0,1},{1,0},{2,3},{3,2},{4,5},{5,4},{6,7},{7,6},{8,9},{9,8},{10,11... | collective-permute-start | bytes 718856 | tf_op jit(solution)/shard_map/ppermute | solution.py:345
  41.0 10.5 %copy-start = (s32[160,2]{0,1:T(2,128)S(1)}, s32[160,2]{0,1:T(2,128)}, u32[]{:S(2)}) copy-start(s32[160,2]{0,1:T(2,128)} %param.8) | copy-start | bytes 3844
  41.0 10.4 %copy-start.1 = (f32[160,2]{0,1:T(2,128)S(1)}, f32[160,2]{0,1:T(2,128)}, u32[]{:S(2)}) copy-start(f32[160,2]{0,1:T(2,128)} %param.9) | copy-start | bytes 3844
  41.0 3.4 %collective-permute-start.16 = (bf16[104,576]{1,0:T(8,128)(2,1)S(1)}, bf16[104,576]{1,0:T(8,128)(2,1)S(1)}, u32[]{:S(2)}, u32[]{:S(2)}) collective-permute-start(bf16[104,576]{1,0:T(8,128)(2,1)S(1)} %get-tuple-element.79), channel_id=1, source_target_pairs={{0,2},{2,0},{4,6},{6,4},{8,10},{10,8},{12,14},{14,12},{1,3},{3,1},... | collective-permute-start | bytes 359432 | tf_op jit(solution)/shard_map/ppermute | solution.py:340
  41.1 3.3 %collective-permute-start.17 = (bf16[104,576]{1,0:T(8,128)(2,1)S(1)}, bf16[104,576]{1,0:T(8,128)(2,1)S(1)}, u32[]{:S(2)}, u32[]{:S(2)}) collective-permute-start(bf16[104,576]{1,0:T(8,128)(2,1)S(1)} %get-tuple-element.80), channel_id=1, source_target_pairs={{0,2},{2,0},{4,6},{6,4},{8,10},{10,8},{12,14},{14,12},{1,3},{3,1},... | collective-permute-start | bytes 359432 | tf_op jit(solution)/shard_map/ppermute | solution.py:340
  44.5 5.1 %collective-permute-start.18 = (bf16[104,576]{1,0:T(8,128)(2,1)S(1)}, bf16[104,576]{1,0:T(8,128)(2,1)S(1)}, u32[]{:S(2)}, u32[]{:S(2)}) collective-permute-start(bf16[104,576]{1,0:T(8,128)(2,1)S(1)} %fusion.3), channel_id=1, source_target_pairs={{0,1},{1,0},{2,3},{3,2},{4,5},{5,4},{6,7},{7,6},{8,9},{9,8},{10,11... | collective-permute-start | bytes 359432 | tf_op jit(solution)/shard_map/ppermute | solution.py:345
  45.8 5.6 %collective-permute-start.14 = (bf16[104,576]{1,0:T(8,128)(2,1)S(1)}, bf16[104,576]{1,0:T(8,128)(2,1)S(1)}, u32[]{:S(2)}, u32[]{:S(2)}) collective-permute-start(bf16[104,576]{1,0:T(8,128)(2,1)S(1)} %get-tuple-element.93), channel_id=1, source_target_pairs={{0,12},{2,14},{4,0},{6,2},{8,4},{10,6},{12,8},{14,10},{1,13},{3,15... | collective-permute-start | bytes 359432 | tf_op jit(solution)/shard_map/ppermute | solution.py:350
  45.9 12.6 %collective-permute-start.15 = (bf16[104,576]{1,0:T(8,128)(2,1)S(1)}, bf16[104,576]{1,0:T(8,128)(2,1)S(1)}, u32[]{:S(2)}, u32[]{:S(2)}) collective-permute-start(bf16[104,576]{1,0:T(8,128)(2,1)S(1)} %get-tuple-element.92), channel_id=1, source_target_pairs={{0,8},{2,10},{4,12},{6,14},{8,0},{10,2},{12,4},{14,6},{1,9},{3,11}... | collective-permute-start | bytes 359432 | tf_op jit(solution)/shard_map/ppermute | solution.py:350
  49.6 8.9 %collective-permute-start.19 = (bf16[104,576]{1,0:T(8,128)(2,1)S(1)}, bf16[104,576]{1,0:T(8,128)(2,1)S(1)}, u32[]{:S(2)}, u32[]{:S(2)}) collective-permute-start(bf16[104,576]{1,0:T(8,128)(2,1)S(1)} %fusion.5), channel_id=1, source_target_pairs={{0,4},{2,6},{4,8},{6,10},{8,12},{10,14},{12,0},{14,2},{1,5},{3,7},... | collective-permute-start | bytes 359432 | tf_op jit(solution)/shard_map/ppermute | solution.py:350
